TPU v7x, 32 devices: a whole 2x2x4 slice. The times are simulated.
32 devices in a mesh: dp: 2 (over y), seq: 16 (over z, x, core).
Axes of the slice: x: 2, y: 2, z: 4, core: 2. Of those that a mesh axis runs over, the one named last changes fastest.
Arguments:
- normed: bfloat16 [2, 3072, 2560], P('dp', 'seq'), may hold values from -6 to 6
- values: bfloat16 [2, 3072, 2560], P('dp', 'seq'), may hold values from -6 to 6
- cotangent: bfloat16 [2, 3072, 2560], P('dp', 'seq'), may hold values from -0.59765625 to 0.59765625
- w_bc: bfloat16 [2560, 256], replicated, may hold values from -0.009765625 to 0.009765625
- rate_index: int32 [2, 40, 3072], P('dp', None, 'seq'), may hold values from 0 to 15, as said below
- starts: int32 [2, 3072], P('dp', 'seq'), may hold values 0 or 1
Outputs:
- grad_values: bfloat16 [2, 3072, 2560], P('dp', 'seq')
- grad_wbc: float32 [2560, 256], P(('dp', 'seq'))
Inputs may be any that keep to these rules, and one draw needn't show every extreme that they name: `rate_index`: indices into the table of 16 decays.
All inputs are finite; a program needn't handle non-finite values. No bound on the sum of `starts` on one device may be relied on, other than what follows from the above.
Results may differ from a plain program's by a relative error of at most 0.0057.
Values sent between devices are 32-bit elements; how exact they have to be, the bound alone decides.
No kernel may reach another device: no remote copies, remote signals or barrier semaphores. Data moves between devices by JAX's collectives and lax.ppermute only.
A program may use at most 64 MiB of HBM per device.

v0:
```python
import jax
import jax.numpy as jnp
from jax import lax
from jax.sharding import PartitionSpec as P

RATES = 16


highest = lax.Precision.HIGHEST


def partner(value, axis, apart):
    mask = 2**apart
    pairs = [(source, source ^ mask) for source in range(lax.axis_size(axis))]
    return lax.ppermute(value, axis, pairs)


def rate_logs():
    ranks = jnp.arange(RATES).astype(jnp.float32)
    return -0.0001 * jnp.power(jnp.float32(500.0), ranks / (RATES - 1))


def decay_parts(logrates, flags):
    length = flags.shape[0]
    sums = jnp.cumsum(logrates, axis=1)
    segment = jnp.cumsum(flags)
    order = jnp.arange(length)
    inside = (segment[:, None] == segment[None, :]) & (order[:, None] >= order[None, :])
    spread = sums[:, :, None] - sums[:, None, :]
    lower_mat = jnp.where(inside[None], jnp.exp(jnp.where(inside[None], spread, 0.0)), 0.0)
    cumulative = jnp.where((segment == 0)[None, :], jnp.exp(sums), 0.0)
    end_weight = lower_mat[:, length - 1, :]
    return (lower_mat, cumulative, end_weight)


def join_pairs(earlier, later):
    return (earlier[0] * later[0], later[0][:, None, None] * earlier[1] + later[1])


def pick_pair(flag, first, second):
    return (jnp.where(flag, first[0], second[0]), jnp.where(flag, first[1], second[1]))


def send_states(pair, bit):
    return partner((pair[0], pair[1]), "seq", bit)


def send_grads(pair, bit):
    return partner((pair[0], pair[1]), "seq", bit)


def combine_chain(own, identity, sender, from_higher):
    position = lax.axis_index("seq")
    levels = lax.axis_size("seq").bit_length() - 1
    prefix = identity
    total = own
    for bit in range(levels):
        other = sender(total, bit)
        high_half = position // (1 << bit) % 2 == 1
        takes_other = jnp.logical_not(high_half) if from_higher else high_half
        prefix = pick_pair(takes_other, join_pairs(other, prefix), prefix)
        total = pick_pair(takes_other, join_pairs(other, total), join_pairs(total, other))
    return prefix


def local(normed, values, cotangent, w_bc, rate_index, starts):
    hidden = normed[0]
    length = hidden.shape[0]
    heads = rate_index.shape[1]
    width = values.shape[2]
    head_dim = width // heads
    state = w_bc.shape[1] // 2
    proj = jnp.dot(hidden, w_bc, preferred_element_type=jnp.float32).astype(jnp.bfloat16)
    bmat = proj[:, :state].astype(jnp.float32)
    cmat = proj[:, state:].astype(jnp.float32)
    levels_table = rate_logs()
    matches = rate_index[0][:, :, None] == jnp.arange(RATES)[None, None, :]
    logrates = jnp.sum(jnp.where(matches, levels_table[None, None, :], 0.0), axis=2)
    lower_mat, cumulative, end_weight = decay_parts(logrates, starts[0])
    vals = values[0].astype(jnp.float32).reshape(length, heads, head_dim)
    cots = cotangent[0].astype(jnp.float32).reshape(length, heads, head_dim)
    decay_total = cumulative[:, -1]
    ends = jnp.einsum("hk,kn,khp->hnp", end_weight, bmat, vals, precision=highest)
    feeds = jnp.einsum("hk,kn,khp->hnp", cumulative, cmat, cots, precision=highest)
    identity = (jnp.ones((heads,), jnp.float32), jnp.zeros((heads, state, head_dim), jnp.float32))
    before = combine_chain((decay_total, ends), identity, send_states, False)[1]
    after = combine_chain((decay_total, feeds), identity, send_grads, True)[1]
    scores = jnp.dot(cmat, bmat.T, precision=highest)
    mixed = lower_mat * scores[None]
    grad_vals = jnp.einsum("hts,thp->shp", mixed, cots, precision=highest)
    grad_vals = grad_vals + end_weight.T[:, :, None] * jnp.einsum(
        "sn,hnp->shp", bmat, after, precision=highest
    )
    paired = lower_mat * jnp.einsum("thp,shp->hts", cots, vals, precision=highest)
    grad_b = jnp.einsum("hts,tn->sn", paired, cmat, precision=highest)
    grad_b = grad_b + jnp.einsum("hs,shp,hnp->sn", end_weight, vals, after, precision=highest)
    grad_c = jnp.einsum("hts,sn->tn", paired, bmat, precision=highest)
    grad_c = grad_c + jnp.einsum("ht,thp,hnp->tn", cumulative, cots, before, precision=highest)
    grad_values = grad_vals.reshape(length, width).astype(jnp.bfloat16)[None]
    grad_bc = jnp.concatenate([grad_b, grad_c], axis=1).astype(jnp.bfloat16)
    scale = 1.0 / (lax.axis_size("dp") * lax.axis_size("seq") * length)
    product = lax.dot_general(
        hidden, grad_bc, (((0,), (0,)), ((), ())), preferred_element_type=jnp.float32
    )
    grad_wbc = lax.psum_scatter(product * scale, ("dp", "seq"), scatter_dimension=0, tiled=True)
    return (grad_values, grad_wbc)


def solution(mesh):
    placed = (
        P("dp", "seq", None),
        P("dp", "seq", None),
        P("dp", "seq", None),
        P(),
        P("dp", None, "seq"),
        P("dp", "seq"),
    )
    return jax.shard_map(
        local,
        mesh=mesh,
        in_specs=placed,
        out_specs=(P("dp", "seq", None), P(("dp", "seq"), None)),
        check_vma=False,
    )
```

profile of v0, /device:TPU:0, one launch (start us, length us, event | category | flops | bytes accessed | tf_op | source)
XLA Modules:
  0.0 434.0 jit_solution(10135395526798417003)
XLA Ops:
  15.7 2.5 fusion.14
  18.7 2.4 copy.37
  21.0 3.9 fusion.13
  25.7 2.2 collective-permute-done
  28.4 4.5 %add_select_fusion.9 = (f32[40,128,64]{1,2,0:T(8,128)}, f32[40,128,64]{1,2,0:T(8,128)}) fusion(f32[40,128,64]{1,2,0:T(8,128)} %collective-permute-done.7, f32[40,128,64]{1,2,0:T(8,128)} %fusion.14, f32[40]{0:T(128)S(1)} %collective-permute-done, f32[40]{0:T(128)S(1)} %slice_reduce_fusion.1, pred[]{:T(512)S(6)} %eq.75, ...), kind=kLoop, calls=%fused_computation.33 | loop fusion | flops 3276800 | bytes 7864642 | tf_op jit(solution)/shard_map/jit(_where)/select_n | solution.py:41
  32.9 2.7 collective-permute-start.4
  35.6 2.0 collective-permute-start.1
  37.6 55.7 %collective-permute-done.1 = f32[40]{0:T(128)S(1)} collective-permute-done((f32[40]{0:T(128)S(1)}, f32[40]{0:T(128)S(1)}, u32[]{:S(2)}, u32[]{:S(2)}) %collective-permute-start.1) | collective-permute-done | bytes 192 | tf_op jit(solution)/shard_map/ppermute | solution.py:15
  93.3 4.5 %add_select_fusion.8 = (f32[40,128,64]{1,2,0:T(8,128)}, f32[40,128,64]{1,2,0:T(8,128)}) fusion(f32[40,128,64]{1,2,0:T(8,128)} %collective-permute-done.8, f32[40,128,64]{1,2,0:T(8,128)} %get-tuple-element.27, f32[40]{0:T(128)S(1)} %collective-permute-done.1, f32[40]{0:T(128)S(1)} %mul.195, pred[]{:T(512)S(6)} %eq.74, ...), kind=kLoop, calls=%fused_computation.32 | loop fusion | flops 3276800 | bytes 7864642 | tf_op jit(solution)/shard_map/jit(_where)/select_n | solution.py:41
  97.8 1.8 collective-permute-start.5
  99.8 1.8 collective-permute-start.2
  101.7 55.0 %collective-permute-done.2 = f32[40]{0:T(128)S(1)} collective-permute-done((f32[40]{0:T(128)S(1)}, f32[40]{0:T(128)S(1)}, u32[]{:S(2)}, u32[]{:S(2)}) %collective-permute-start.2) | collective-permute-done | bytes 192 | tf_op jit(solution)/shard_map/ppermute | solution.py:15
  156.7 4.6 %add_select_fusion.7 = (f32[40,128,64]{1,2,0:T(8,128)}, f32[40,128,64]{1,2,0:T(8,128)}) fusion(f32[40,128,64]{1,2,0:T(8,128)} %collective-permute-done.9, f32[40,128,64]{1,2,0:T(8,128)} %get-tuple-element.25, f32[40]{0:T(128)S(1)} %collective-permute-done.2, f32[40]{0:T(128)S(1)} %mul.196, pred[]{:T(512)S(6)} %eq.71, ...), kind=kLoop, calls=%fused_computation.31 | loop fusion | flops 3276800 | bytes 7864642 | tf_op jit(solution)/shard_map/jit(_where)/select_n | solution.py:41
  161.3 2.6 collective-permute-start.6
  163.9 4.5 %multiply_reduce_fusion = f32[192,192]{1,0:T(8,128)S(1)} fusion(f32[40,192]{1,0:T(8,128)S(1)} %get-tuple-element.19, pred[192,192]{1,0:T(8,128)(4,1)S(1)} %fusion.39, bf16[192,40,64]{0,2,1:T(8,128)(2,1)} %bitcast.76, bf16[192,40,64]{0,2,1:T(8,128)(2,1)S(1)} %bitcast.73), kind=kOutput, calls=%fused_computation | convolution fusion | flops 196079616 | bytes 2181120 | tf_op jit(solution)/shard_map/thp,shp->hts/dot_general | solution.py:94
  169.4 79.8 %collective-permute-done.6 = f32[40,128,64]{1,2,0:T(8,128)} collective-permute-done((f32[40,128,64]{1,2,0:T(8,128)}, f32[40,128,64]{1,2,0:T(8,128)}, u32[]{:S(2)}, u32[]{:S(2)}) %collective-permute-start.6) | collective-permute-done | bytes 1310752 | tf_op jit(solution)/shard_map/ppermute | solution.py:15
  249.2 3.1 add_select_fusion.3
  252.4 4.3 fusion.28
  256.7 19.6 %collective-permute-done.10 = f32[40,128,64]{1,2,0:T(8,128)S(1)} collective-permute-done((f32[40,128,64]{1,2,0:T(8,128)S(1)}, f32[40,128,64]{1,2,0:T(8,128)S(1)}, u32[]{:S(2)}, u32[]{:S(2)}) %collective-permute-start.10) | collective-permute-done | bytes 1310752 | tf_op jit(solution)/shard_map/ppermute | solution.py:15
  276.3 6.6 %fusion.27 = bf16[192,128]{1,0:T(8,128)(2,1)S(1)} fusion(f32[192,128]{1,0:T(8,128)S(1)} %fusion.51, f32[40,128,64]{1,2,0:T(8,128)} %collective-permute-done.7, f32[40,128,64]{1,2,0:T(8,128)} %collective-permute-done.8, f32[40,128,64]{1,2,0:T(8,128)} %collective-permute-done.9, f32[40,128,64]{1,2,0:T(8,128)S(1)} %collective-permute-done.10, ...), kind=kOutput, calls=%fused_computation.46 | convolution fusion | flops 759283712 | bytes 6404580 | tf_op jit(solution)/shard_map/ht,thp,hnp->tn/dot_general | solution.py:98
  282.9 2.1 fusion.2
  284.9 3.2 copy.41
  289.5 5.2 %fusion = f32[40,192,64]{1,2,0:T(8,128)S(1)} fusion(bf16[192,40,64]{0,2,1:T(8,128)(2,1)S(1)} %bitcast.78, f32[192,192]{1,0:T(8,128)S(1)} %fusion.48, f32[40,192]{1,0:T(8,128)S(1)} %get-tuple-element.19, pred[192,192]{1,0:T(8,128)(4,1)S(1)} %fusion.39), kind=kOutput, calls=%fused_computation.1 | convolution fusion | flops 1138360320 | bytes 3164160 | tf_op jit(solution)/shard_map/hts,thp->shp/dot_general | solution.py:90
  297.9 129.2 %reduce-scatter.4.cloned.1.call-done = f32[80,256]{1,0:T(8,128)} async-done(((f32[2560,256]{1,0:T(8,128)}), f32[80,256]{1,0:T(8,128)}) %reduce-scatter.4.cloned.1.call-update) | async-done | bytes 81936
  (60 shorter events, 15.8 us)
Async XLA Ops:
  7.2 6.9 %copy-start = (bf16[2560,256]{1,0:T(8,128)(2,1)S(1)}, bf16[2560,256]{1,0:T(8,128)(2,1)}, u32[]{:S(2)}) copy-start(bf16[2560,256]{1,0:T(8,128)(2,1)} %param.9) | copy-start | bytes 3932164
  7.2 420.0 %reduce-scatter.4.cloned.1.call-start = ((), (), s32[]{:S(2)}) async-start(), calls=%async_computation.1 | async-start | bytes 2703360
  18.2 9.8 %collective-permute-start.7 = (f32[40,128,64]{1,2,0:T(8,128)}, f32[40,128,64]{1,2,0:T(8,128)}, u32[]{:S(2)}, u32[]{:S(2)}) collective-permute-start(f32[40,128,64]{1,2,0:T(8,128)} %fusion.14), channel_id=1, source_target_pairs={{0,1},{1,0},{2,3},{3,2},{4,5},{5,4},{6,7},{7,6},{8,9},{9,8},{10,11... | collective-permute-start | bytes 3932168 | tf_op jit(solution)/shard_map/ppermute | solution.py:15
  25.0 3.4 collective-permute-start.3
  25.2 2.8 collective-permute-start
  32.9 60.3 %collective-permute-start.4 = (f32[40,128,64]{1,2,0:T(8,128)}, f32[40,128,64]{1,2,0:T(8,128)}, u32[]{:S(2)}, u32[]{:S(2)}) collective-permute-start(f32[40,128,64]{1,2,0:T(8,128)} %get-tuple-element.28), channel_id=1, source_target_pairs={{0,2},{1,3},{2,0},{3,1},{4,6},{5,7},{6,4},{7,5},{8,10},{9,11},{10,... | collective-permute-start | bytes 3932168 | tf_op jit(solution)/shard_map/ppermute | solution.py:15
  35.6 57.7 %collective-permute-start.8 = (f32[40,128,64]{1,2,0:T(8,128)}, f32[40,128,64]{1,2,0:T(8,128)}, u32[]{:S(2)}, u32[]{:S(2)}) collective-permute-start(f32[40,128,64]{1,2,0:T(8,128)} %get-tuple-element.27), channel_id=1, source_target_pairs={{0,2},{1,3},{2,0},{3,1},{4,6},{5,7},{6,4},{7,5},{8,10},{9,11},{10,... | collective-permute-start | bytes 3932168 | tf_op jit(solution)/shard_map/ppermute | solution.py:15
  35.6 57.7 %collective-permute-start.1 = (f32[40]{0:T(128)S(1)}, f32[40]{0:T(128)S(1)}, u32[]{:S(2)}, u32[]{:S(2)}) collective-permute-start(f32[40]{0:T(128)S(1)} %mul.195), channel_id=1, source_target_pairs={{0,2},{1,3},{2,0},{3,1},{4,6},{5,7},{6,4},{7,5},{8,10},{9,11},{10,... | collective-permute-start | bytes 488 | tf_op jit(solution)/shard_map/ppermute | solution.py:15
  97.8 58.9 %collective-permute-start.5 = (f32[40,128,64]{1,2,0:T(8,128)}, f32[40,128,64]{1,2,0:T(8,128)}, u32[]{:S(2)}, u32[]{:S(2)}) collective-permute-start(f32[40,128,64]{1,2,0:T(8,128)} %get-tuple-element.26), channel_id=1, source_target_pairs={{0,4},{1,5},{2,6},{3,7},{4,0},{5,1},{6,2},{7,3},{8,12},{9,13},{10,... | collective-permute-start | bytes 3932168 | tf_op jit(solution)/shard_map/ppermute | solution.py:15
  99.6 57.1 %collective-permute-start.9 = (f32[40,128,64]{1,2,0:T(8,128)}, f32[40,128,64]{1,2,0:T(8,128)}, u32[]{:S(2)}, u32[]{:S(2)}) collective-permute-start(f32[40,128,64]{1,2,0:T(8,128)} %get-tuple-element.25), channel_id=1, source_target_pairs={{0,4},{1,5},{2,6},{3,7},{4,0},{5,1},{6,2},{7,3},{8,12},{9,13},{10,... | collective-permute-start | bytes 3932168 | tf_op jit(solution)/shard_map/ppermute | solution.py:15
  99.8 56.9 %collective-permute-start.2 = (f32[40]{0:T(128)S(1)}, f32[40]{0:T(128)S(1)}, u32[]{:S(2)}, u32[]{:S(2)}) collective-permute-start(f32[40]{0:T(128)S(1)} %mul.196), channel_id=1, source_target_pairs={{0,4},{1,5},{2,6},{3,7},{4,0},{5,1},{6,2},{7,3},{8,12},{9,13},{10,... | collective-permute-start | bytes 488 | tf_op jit(solution)/shard_map/ppermute | solution.py:15
  161.3 87.9 %collective-permute-start.6 = (f32[40,128,64]{1,2,0:T(8,128)}, f32[40,128,64]{1,2,0:T(8,128)}, u32[]{:S(2)}, u32[]{:S(2)}) collective-permute-start(f32[40,128,64]{1,2,0:T(8,128)} %get-tuple-element.24), channel_id=1, source_target_pairs={{0,8},{1,9},{2,10},{3,11},{4,12},{5,13},{6,14},{7,15},{8,0},{9,1},... | collective-permute-start | bytes 3932168 | tf_op jit(solution)/shard_map/ppermute | solution.py:15
  163.9 4.5 %copy-start.6 = (f32[40,128,64]{1,2,0:T(8,128)S(1)}, f32[40,128,64]{1,2,0:T(8,128)}, u32[]{:S(2)}) copy-start(f32[40,128,64]{1,2,0:T(8,128)} %get-tuple-element.23) | copy-start | bytes 3932164
  168.4 107.9 %collective-permute-start.10 = (f32[40,128,64]{1,2,0:T(8,128)S(1)}, f32[40,128,64]{1,2,0:T(8,128)S(1)}, u32[]{:S(2)}, u32[]{:S(2)}) collective-permute-start(f32[40,128,64]{1,2,0:T(8,128)S(1)} %copy-done.6), channel_id=1, source_target_pairs={{0,8},{1,9},{2,10},{3,11},{4,12},{5,13},{6,14},{7,15},{8,0},{9,1},... | collective-permute-start | bytes 3932168 | tf_op jit(solution)/shard_map/ppermute | solution.py:15
  252.3 4.4 %copy-start.3 = (f32[40,128,64]{1,2,0:T(8,128)}, f32[40,128,64]{1,2,0:T(8,128)S(1)}, u32[]{:S(2)}) copy-start(f32[40,128,64]{1,2,0:T(8,128)S(1)} %add_select_fusion.3) | copy-start | bytes 3932164
  252.4 23.9 %copy-start.1 = (bf16[1,192,2560]{1,2,0:T(8,128)(2,1)S(1)}, bf16[1,192,2560]{1,2,0:T(8,128)(2,1)}, u32[]{:S(2)}) copy-start(bf16[1,192,2560]{1,2,0:T(8,128)(2,1)} %copy.37) | copy-start | bytes 2949124
  276.3 6.6 %copy-start.5 = (bf16[1,192,2560]{2,1,0:T(8,128)(2,1)S(1)}, bf16[1,192,2560]{2,1,0:T(8,128)(2,1)}, u32[]{:S(2)}) copy-start(bf16[1,192,2560]{2,1,0:T(8,128)(2,1)} %param.6) | copy-start | bytes 2949124
  288.1 1.3 copy-start.2
  289.5 5.2 %copy-start.4 = (f32[40,128,64]{1,2,0:T(8,128)S(1)}, f32[40,128,64]{1,2,0:T(8,128)}, u32[]{:S(2)}) copy-start(f32[40,128,64]{1,2,0:T(8,128)} %copy-done.3) | copy-start | bytes 3932164
Sparse Core Ops, SparseCore 0:
  288.3 138.8 reduce-scatter.3
where the time goes:
time: 434 us
  waiting for transfers between devices  342 us (79%)
  matrix products  32.7 us (8%)
  other arithmetic  21.6 us (5%)
  between operations  14.2 us (3%)
  starting transfers between devices  12.6 us (3%)
  local copies, waits for them, and re-layouts  11 us (3%)
    ppermute x11, waiting for transfers between devices, partner(): return lax.ppermute(value, axis, pairs)  213 us
    unnamed x2, waiting for transfers between devices  129 us
    select_n x4, other arithmetic, pick_pair(): jnp.where(flag, first[1], second[1])  16.8 us
    ppermute x11, starting transfers between devices, partner(): return lax.ppermute(value, axis, pairs)  12.6 us
    unnamed x19, local copies, waits for them, and re-layouts  9.62 us
  transfers between devices with their start and end apart: 12, of which 7 were waited for; matrix products, arithmetic and copies ran while one was open for 6% of the time, Pallas kernels for 0%

commit v1 on v0

v1 whole, which is shorter than its diff:
```python
import math

import jax
import jax.numpy as jnp
from jax import lax
from jax.experimental import pallas as pl
from jax.experimental.pallas import tpu as pltpu
from jax.sharding import PartitionSpec as P

RATES = 16
CHUNKS = 2
LANES = 128
MIB = 1024 * 1024

f32 = jnp.float32
bf16 = jnp.bfloat16
highest = lax.Precision.HIGHEST


def log_rate(index):
    return -0.0001 * jnp.exp(index.astype(f32) * (math.log(500.0) / (RATES - 1)))


def dot(lhs, rhs, over=(1, 0), precision=None):
    dims = (((over[0],), (over[1],)), ((), ()))
    return lax.dot_general(lhs, rhs, dims, precision=precision, preferred_element_type=f32)


def padded(rows):
    return -(-rows // 8) * 8


def spread(small, heads, width):
    lane = lax.broadcasted_iota(jnp.int32, (heads, width), 1) // (width // heads)
    row = lax.broadcasted_iota(jnp.int32, (heads, width), 0)
    pattern = jnp.where(lane == row, 1.0, 0.0).astype(bf16)
    high = small.astype(bf16)
    low = (small - high.astype(f32)).astype(bf16)
    return dot(high, pattern) + dot(low, pattern)


def orders(length):
    return (lax.broadcasted_iota(jnp.int32, (length, length), 0), lax.broadcasted_iota(jnp.int32, (length, length), 1))


def decay_sums(logs):
    order, other = orders(logs.shape[1])
    lower = jnp.where(other <= order, 1.0, 0.0).astype(f32)
    return dot(lower, logs, (1, 1), highest)


def segments(flags):
    order, other = orders(flags.shape[1])
    column = jnp.sum(jnp.where(other <= order, flags, 0.0), axis=1, keepdims=True)
    return column, jnp.sum(flags, axis=1, keepdims=True)


def pieces_of(array, count):
    rows = array.shape[0] // count
    return [slice(i * rows, (i + 1) * rows) for i in range(count)]


def first_body(
    place, normed_far, w_far, vals_far, cots_far, rate_far, starts_far, message, keep_f, keep_g, decays, u_out, v_out, bc_out,
    groups, normed, w_bc, vals, cots, rate, starts, small, first, second, third, fourth,
):
    heads = rate.shape[0]
    width = vals.shape[1]
    state = w_bc.shape[1] // 2
    early = [pltpu.make_async_copy(rate_far.at[0], rate, small.at[0]), pltpu.make_async_copy(starts_far, starts, small.at[1])]
    waves = []
    for source, target, sems in (
        (normed_far.at[0], normed, first), (w_far, w_bc, second), (cots_far.at[0], cots, third), (vals_far.at[0], vals, fourth),
    ):
        waves.append([
            pltpu.make_async_copy(source.at[rows], target.at[rows], sems.at[i])
            for i, rows in enumerate(pieces_of(target, sems.shape[0]))
        ])
    for copies in [early] + waves:
        for copy in copies:
            copy.start()
    for copy in early:
        copy.wait()
    logs = log_rate(rate[...])
    flags = starts[...].astype(f32)
    sums = decay_sums(logs)
    segment, last_segment = segments(flags)
    total = jnp.where(last_segment == 0.0, jnp.exp(jnp.sum(logs, axis=1, keepdims=True)), 0.0)
    total = jnp.broadcast_to(total, (heads, LANES))
    eighth = heads // 8
    for group in range(8):
        groups[group, :eighth, :] = total[group * eighth:(group + 1) * eighth]
    up = jnp.where(segment == 0.0, jnp.exp(sums), 0.0)
    down = jnp.where(segment == last_segment, jnp.exp(sums[-1:, :] - sums), 0.0)
    up_wide = spread(up, heads, width)
    down_wide = spread(down, heads, width)
    for copy in waves[0] + waves[1]:
        copy.wait()
    bc = dot(normed[...], w_bc[...]).astype(bf16)
    bc_out[...] = bc
    for copy in waves[2]:
        copy.wait()
    u_out[...] = (up_wide * cots[...].astype(f32)).astype(bf16)
    for copy in waves[3]:
        copy.wait()
    v_out[...] = (down_wide * vals[...].astype(f32)).astype(bf16)
    bmat, cmat = bc[:, :state], bc[:, state:]
    slot = groups.shape[1]
    half, part = width // 2, width // 8
    quad = quad_of(place)
    for near_set in (1, 0):
        which = lax.rem(place[0] + near_set, 2)
        columns = pl.ds(pl.multiple_of(which * half, half), half)
        forward = dot(v_out[:, columns], bmat, (0, 0))
        backward = dot(u_out[:, columns], cmat, (0, 0))
        for group in range(4):
            flip = jnp.bitwise_xor(quad, group)
            rows = slice(group * part, (group + 1) * part)
            to = pl.ds(pl.multiple_of(flip * part, part), part)
            behind = pl.ds(pl.multiple_of(half + flip * part, part), part)
            factors = groups[which * 4 + group]
            if near_set == 0:
                keep_f[to, :] = forward[rows]
                keep_g[to, :] = backward[rows]
                decays[pl.ds(pl.multiple_of(flip * slot, slot), slot), :] = factors
            else:
                message[to, :] = forward[rows]
                message[behind, :] = backward[rows]
                message[pl.ds(pl.multiple_of(2 * half + flip * slot, slot), slot), :] = factors


def local_body(place, vals, cots, rate, starts, bc_ref, grad_out, scale_out, dbc_out):
    heads, length = rate.shape
    width = vals.shape[1]
    state = bc_ref.shape[1] // 2
    flags = starts[...].astype(f32)
    sums = decay_sums(log_rate(rate[...]))
    segment, last_segment = segments(flags)
    order, other = orders(length)
    later = jnp.where(other <= order, flags, 0.0)
    reach = dot(later.astype(bf16), jnp.where(order > other, 1.0, 0.0).astype(bf16))
    inside = jnp.logical_and(order >= other, reach == 0.0)
    scale = spread(jnp.exp(sums[-1:, :] - sums), heads, width)
    lifted = (spread(jnp.exp(sums - sums[-1:, :]), heads, width) * cots[...].astype(f32)).astype(bf16)
    weighted = (scale * vals[...].astype(f32)).astype(bf16)
    bmat, cmat = bc_ref[:, :state], bc_ref[:, state:]
    paired = jnp.where(inside, dot(lifted, weighted, (1, 1)), 0.0).astype(bf16)
    scores = jnp.where(inside, dot(cmat, bmat, (1, 1)), 0.0).astype(bf16)
    grad_out[...] = scale * dot(scores, lifted, (0, 0))
    scale_out[...] = jnp.where(segment == last_segment, scale, 0.0)
    dbc_out[:, :state] = dot(paired, cmat, (0, 0))
    dbc_out[:, state:] = dot(paired, bmat)


def pick(flag, first, second):
    return jnp.where(flag, first, second)


def quad_of(place):
    return lax.rem(place[2], 2) * 2 + place[1]


def chip_body(start, size, head, place, keep_f, keep_g, decays, recv, *outs):
    rows = size * head
    base = keep_f.shape[0]
    slot = decays.shape[0] // 4
    second = place[0] == 1
    for flip, out in enumerate(outs):
        for k in range(size):
            at = flip * (base // 4) + (start + k) * head
            spot = flip * slot + start + k
            mine = decays[spot:spot + 1, :]
            theirs = recv[2 * base + spot:2 * base + spot + 1, :]
            kf, rf = keep_f[at:at + head, :], recv[at:at + head, :]
            kg, rg = keep_g[at:at + head, :], recv[base + at:base + at + head, :]
            to = slice(k * head, (k + 1) * head)
            out[to, :] = pick(second, 1.0, theirs) * kf + pick(second, mine, 1.0) * rf
            to = slice(rows + k * head, rows + (k + 1) * head)
            out[to, :] = pick(second, theirs, 1.0) * kg + pick(second, 1.0, mine) * rg
            out[2 * rows + k:2 * rows + k + 1, :] = mine * theirs


def parts(ref, size, head, k):
    rows = size * head
    return ref[k * head:(k + 1) * head, :], ref[rows + k * head:rows + (k + 1) * head, :], ref[2 * rows + k:2 * rows + k + 1, :]


def joined(mine, theirs, second):
    forward = pick(second, 1.0, theirs[2]) * mine[0] + pick(second, mine[2], 1.0) * theirs[0]
    backward = pick(second, theirs[2], 1.0) * mine[1] + pick(second, 1.0, mine[2]) * theirs[1]
    return forward, backward, mine[2] * theirs[2]


def entering(mine, theirs, second, before, behind):
    my_before = pick(second, theirs[2], 1.0) * before + pick(second, 1.0, 0.0) * theirs[0]
    their_before = pick(second, 1.0, mine[2]) * before + pick(second, 0.0, 1.0) * mine[0]
    my_behind = pick(second, 1.0, theirs[2]) * behind + pick(second, 0.0, 1.0) * theirs[1]
    their_behind = pick(second, mine[2], 1.0) * behind + pick(second, 1.0, 0.0) * mine[1]
    return (my_before, my_behind), (their_before, their_behind)


def level_bit(place, bit):
    return lax.rem(place[2] // (1 << bit), 2) == 1


def store_total(out, total, size, head, k, upper):
    rows = size * head
    if upper is None:
        out[k * head:(k + 1) * head, :] = total[0]
        out[rows + k * head:rows + (k + 1) * head, :] = total[1]
        out[2 * rows + k:2 * rows + k + 1, :] = total[2]
    else:
        out[k * head:(k + 1) * head, :] = pick(upper, total[1], total[0])


def quad_body(size, head, last, place, own, one, two, three, out):
    second, later = place[1] == 1, level_bit(place, 0)
    upper = None if last is None else level_bit(place, last)
    for k in range(size):
        here, beside, along, across = (parts(ref, size, head, k) for ref in (own, one, two, three))
        total = joined(joined(here, beside, second), joined(along, across, second), later)
        store_total(out, total, size, head, k, upper)


def join_body(size, head, bit, last, place, total, recv, out):
    upper = None if last is None else level_bit(place, last)
    for k in range(size):
        mine, theirs = parts(total, size, head, k), parts(recv, size, head, k)
        store_total(out, joined(mine, theirs, level_bit(place, bit)), size, head, k, upper)


def enter_body(chunks, head, bits, place, *refs):
    outs = refs[-4:]
    second, later, total = place[1] == 1, level_bit(place, 0), outs[0].shape[0] // 2
    each = 4 + bits - 1
    for number, (start, size) in enumerate(chunks):
        own, one, two, three, *levels, final = refs[number * each:(number + 1) * each]
        for k in range(size):
            before, behind, left, right = 0.0, 0.0, 1.0, 1.0
            for bit, recv in enumerate(levels):
                high = level_bit(place, bit + 1)
                forward, backward, decay = parts(recv, size, head, k)
                before = before + pick(high, left, 0.0) * forward
                behind = behind + pick(high, 0.0, right) * backward
                left = pick(high, left * decay, left)
                right = pick(high, right, right * decay)
            high = level_bit(place, bits - 1)
            last = final[k * head:(k + 1) * head, :]
            before = before + pick(high, left, 0.0) * last
            behind = behind + pick(high, 0.0, right) * last
            here, beside, along, across = (parts(ref, size, head, k) for ref in (own, one, two, three))
            row, other = entering(joined(here, beside, second), joined(along, across, second), later, before, behind)
            states = entering(here, beside, second, *row) + entering(along, across, second, *other)
            at = (start + k) * head
            for out, (state_before, state_behind) in zip(outs, states):
                out[at:at + head, :] = state_before
                out[total + at:total + at + head, :] = state_behind


def core_body(start, size, head, place, *refs):
    states, keep_f, keep_g, decays, recv, send, own = refs[:4], *refs[4:]
    rows = size * head
    base = keep_f.shape[0]
    slot = decays.shape[0] // 4
    second = place[0] == 1
    for flip, ref in enumerate(states):
        for k in range(size):
            at = flip * (base // 4) + (start + k) * head
            spot = flip * slot + start + k
            here = decays[spot:spot + 1, :]
            there = recv[2 * base + spot:2 * base + spot + 1, :]
            state = ref[k * head:(k + 1) * head, :]
            to = slice(flip * rows + k * head, flip * rows + (k + 1) * head)
            send[to, :] = pick(second, 1.0, here) * state + pick(second, 0.0, 1.0) * keep_f[at:at + head, :]
            own[to, :] = (pick(second, there, 1.0) * state + pick(second, 1.0, 0.0) * recv[at:at + head, :]).astype(bf16)
            state = ref[rows + k * head:rows + (k + 1) * head, :]
            to = slice((4 + flip) * rows + k * head, (4 + flip) * rows + (k + 1) * head)
            send[to, :] = pick(second, here, 1.0) * state + pick(second, 1.0, 0.0) * keep_g[at:at + head, :]
            own[to, :] = (pick(second, 1.0, there) * state + pick(second, 0.0, 1.0) * recv[base + at:base + at + head, :]).astype(bf16)


def cross_body(chunks, head, place, u_ref, v_ref, local_ref, *refs):
    count = len(chunks)
    mine, theirs = refs[:count], refs[count:2 * count]
    out, after, before = refs[2 * count:]
    group = after.shape[0] // 8
    state = after.shape[1]
    quad = quad_of(place)
    for near_set, pieces in ((0, mine), (1, theirs)):
        for (start, size), piece in zip(chunks, pieces):
            rows = size * head
            for flip in range(4):
                which = lax.rem(place[0] + near_set, 2) * 4 + jnp.bitwise_xor(quad, flip)
                to = pl.ds(pl.multiple_of(which * group + start * head, head), rows)
                before[to, :] = piece[flip * rows:(flip + 1) * rows, :].astype(bf16)
                after[to, :] = piece[(4 + flip) * rows:(5 + flip) * rows, :].astype(bf16)
    out[:, :state] = (local_ref[:, :state] + dot(v_ref[...], after[...])).astype(bf16).astype(f32)
    out[:, state:] = (local_ref[:, state:] + dot(u_ref[...], before[...])).astype(bf16).astype(f32)


def values_body(place, grad_ref, scale_ref, bc_ref, after, grad_out, done):
    done[...] = jnp.zeros_like(done)
    bmat = bc_ref[:, : after.shape[1]]
    grad_out[...] = (grad_ref[...] + scale_ref[...] * dot(bmat, after[...], (1, 1))).astype(bf16)


def block_row(quarter, position, levels, rows):
    quad, rest = position // (levels // 2), position % (levels // 2)
    level = 0
    for bit in range(levels.bit_length() - 2):
        level = level * 2 + rest % 2
        rest //= 2
    index = (quarter // 2) * (4 * levels) + (level * 2 + quad // 2) * 4 + quad % 2 * 2 + lax.rem(quarter, 2)
    return pl.multiple_of(index * rows, rows)


def turn_body(levels, rows, place, normed, own, beside, beyond, turned):
    turned[...] = normed[...].T.astype(f32)
    count = 2 * levels
    quarter = place[3] * 2 + place[0]
    half = count // 2 * rows
    for flip in range(4):
        out, base = ((own, 0), (beside, 0), (beyond, 0), (beyond, 3 * half))[flip]
        for position in range(count):
            start = block_row(jnp.bitwise_xor(quarter, flip), position, levels, rows)
            block = turned[pl.ds(start, rows), :]
            at = position * rows
            if flip == 0:
                out[at:at + rows, :] = block.astype(bf16)
            else:
                out[base + at:base + at + rows, :] = block[:, :LANES]
                tail = base + 2 * half + at % half
                lanes = slice(0, LANES // 2) if position < count // 2 else slice(LANES // 2, LANES)
                out[tail:tail + rows, lanes] = block[:, LANES:]


def stack_body(place, beside, beyond, out):
    rows = beside.shape[0]
    out[:rows, :] = beside[...]
    out[rows:, :] = beyond[rows:, :]


def unpack_body(place, own, beside, beyond, out):
    length = own.shape[1]
    total = own.shape[0]
    half = total // 2
    wide = 3 * half
    out[:, :length] = own[...]
    for index, (ref, base) in enumerate(((beside, 0), (beyond, 0), (beside, wide)), 1):
        left = index * length
        out[:, left:left + LANES] = ref[base:base + total, :].astype(bf16)
        out[:half, left + LANES:left + length] = ref[base + total:base + wide, :LANES // 2].astype(bf16)
        out[half:, left + LANES:left + length] = ref[base + total:base + wide, LANES // 2:].astype(bf16)


def weight_body(place, turned, own, one, two, three, *refs):
    outs, product = refs[:4], refs[4]
    length = own.shape[0]
    total = None
    for index, ref in enumerate((own, one, two, three)):
        term = dot(turned[:, index * length:(index + 1) * length], ref[...].astype(bf16))
        total = term if total is None else total + term
    product[...] = total
    rows = outs[0].shape[0]
    for flip, out in enumerate(outs):
        block = jnp.bitwise_xor(quad_of(place), flip)
        out[...] = product[pl.ds(pl.multiple_of(block * rows, rows), rows), :]


def halve_body(bit, place, *refs):
    terms, send, keep = refs[:-2], refs[-2], refs[-1]
    rows = keep.shape[0]
    here = lax.rem(place[2] // (1 << bit), 2)
    for which, out in ((1 - here, send), (here, keep)):
        at = pl.ds(pl.multiple_of(which * rows, rows), rows)
        total = terms[0][at, :]
        for term in terms[1:]:
            total = total + term[at, :]
        out[...] = total


def local(normed, values, cotangent, w_bc, rate_index, starts):
    hidden, vals, cots = normed[0], values[0], cotangent[0]
    rate = rate_index[0]
    length, width = vals.shape
    depth = hidden.shape[1]
    heads = rate.shape[0]
    head = width // heads
    state = w_bc.shape[1] // 2
    shards = lax.axis_size("seq")
    packs = lax.axis_size("dp")
    levels = shards // 4
    bits = levels.bit_length() - 1
    eighth = heads // 8
    slot = padded(eighth)
    base = width // 2

    def shape(rows, columns, dtype=f32):
        return jax.ShapeDtypeStruct((rows, columns), dtype)

    token = []

    def kernel(body, outs, *args, scratch=(), vmem=4, far=False, behind=()):
        count = len(args)
        after = list(token) + list(behind)
        single = not isinstance(outs, tuple)

        def run(*refs):
            spot = lax.axis_index("seq")
            place = (spot & 1, (spot >> 1) & 1, spot >> 2, lax.axis_index("dp") & 1)
            body(place, *refs[:count], *refs[count + len(after):])

        here = pl.BlockSpec(memory_space=pltpu.VMEM)
        there = pl.BlockSpec(memory_space=pltpu.HBM) if far else here
        if far:
            args = [pltpu.with_memory_space_constraint(array, pltpu.HBM) for array in args]
        result = pl.pallas_call(
            run,
            in_specs=[there] * count + [pl.BlockSpec(memory_space=pl.ANY)] * len(after),
            out_specs=here if single else (here,) * len(outs),
            out_shape=outs,
            scratch_shapes=list(scratch),
            compiler_params=pltpu.CompilerParams(vmem_limit_bytes=vmem * MIB),
            cost_estimate=pl.CostEstimate(flops=1000, bytes_accessed=1000, transcendentals=0),
        )(*args, *after)
        token[:] = [result if single else min(result, key=lambda array: array.size)]
        return result

    def bind(body, *constants):
        return lambda *refs: body(*constants, *refs)

    def swap(array, mask):
        return lax.ppermute(array, "seq", [(s, s ^ mask) for s in range(shards)])

    def swap_pack(array):
        return lax.ppermute(array, "dp", [(d, d ^ 1) for d in range(packs)])

    def swap_both(array):
        return lax.ppermute(array, ("dp", "seq"), [(d * shards + s, (d ^ 1) * shards + (s ^ 1)) for d in range(packs) for s in range(shards)])

    message, keep_f, keep_g, decays, u, v, bc = kernel(
        first_body,
        (
            shape(2 * base + 4 * slot, state), shape(base, state), shape(base, state), shape(4 * slot, state),
            shape(length, width, bf16), shape(length, width, bf16), shape(length, 2 * state, bf16),
        ),
        normed, w_bc, values, cotangent, rate_index, starts,
        scratch=[
            pltpu.VMEM((8, slot, LANES), f32), pltpu.VMEM(hidden.shape, bf16), pltpu.VMEM(w_bc.shape, bf16),
            pltpu.VMEM(vals.shape, bf16), pltpu.VMEM(cots.shape, bf16), pltpu.VMEM(rate.shape, jnp.int32),
            pltpu.VMEM(starts.shape, jnp.int32),
        ] + [pltpu.SemaphoreType.DMA((count,)) for count in (2, 4, 4, 4, 4)],
        vmem=24, far=True,
    )
    recv = swap(message, 1)

    direct = packs == 2 and depth % (packs * shards * 16) == 0 and length == 3 * LANES // 2
    rows = depth // (packs * shards)
    part = depth // 4
    wide = part + part // 2
    pack_turned = None
    if direct:
        own_turned, core_turned, message = kernel(
            bind(turn_body, levels, rows), (shape(part, length, bf16), shape(wide, LANES), shape(2 * wide, LANES)),
            hidden, scratch=[pltpu.VMEM((depth, length), f32)], vmem=16,
        )
        pack_turned = swap_pack(message)

    bounds = [-(-eighth * i // CHUNKS) for i in range(CHUNKS + 1)]
    chunks = [(a, b - a) for a, b in zip(bounds, bounds[1:])]

    def parcel(size):
        return shape(2 * size * head + padded(size), state)

    def to_quad(arrays):
        return [swap(array, flip * 2) for flip, array in enumerate(arrays, 1)]

    quads = []
    for start, size in chunks:
        waits = quads[-1][1:2] if quads else ()
        own, *sends = kernel(bind(chip_body, start, size, head), (parcel(size),) * 4, keep_f, keep_g, decays, recv, behind=waits)
        quads.append([own] + to_quad(sends))

    totals, arrived = [], [[] for unused in chunks]
    for number, ((start, size), group) in enumerate(zip(chunks, quads)):
        last = 1 if bits == 2 else None
        out = parcel(size) if last is None else shape(size * head, state)
        totals.append(kernel(bind(quad_body, size, head, last), out, *group))
        arrived[number].append(swap(totals[number], 8))
    for bit in range(1, bits - 1):
        last = bit + 1 if bit == bits - 2 else None
        for number, (start, size) in enumerate(chunks):
            out = parcel(size) if last is None else shape(size * head, state)
            totals[number] = kernel(bind(join_body, size, head, bit, last), out, totals[number], arrived[number][-1])
            arrived[number].append(swap(totals[number], 8 << bit))
    grad_local, scale, dbc_local = kernel(
        local_body, (shape(length, width), shape(length, width), shape(length, 2 * state)),
        vals, cots, rate, starts, bc, vmem=24,
    )
    if direct:
        beside = swap(kernel(stack_body, shape(2 * wide, LANES), core_turned, pack_turned, vmem=8), 1)
    pieces = [array for group, steps in zip(quads, arrived) for array in group + steps]
    enter, *sends = kernel(
        bind(enter_body, chunks, head, bits), (shape(2 * eighth * head, state),) * 4, *pieces,
    )
    send, final = kernel(
        bind(core_body, 0, eighth, head), (shape(base * 2, state), shape(base * 2, state, bf16)),
        enter, *to_quad(sends), keep_f, keep_g, decays, recv, behind=[beside] if direct else [],
    )
    core_recv = swap(send, 1)
    dbc, after = kernel(
        bind(cross_body, ((0, eighth),), head), (shape(length, 2 * state), shape(width, state, bf16)),
        u, v, dbc_local, final, core_recv, scratch=[pltpu.VMEM((width, state), bf16)], vmem=16,
    )
    portion = 1.0 / (packs * shards * length)
    if direct:
        from_pack = swap_pack(dbc)
        from_core = swap(dbc, 1)
        from_both = swap(from_pack, 1)
    grad_values, unused_done = kernel(
        values_body, (shape(length, width, bf16), shape(8, LANES)), grad_local, scale, bc, after, vmem=16,
    )
    if not direct:
        product = lax.dot_general(hidden, dbc.astype(bf16), (((0,), (0,)), ((), ())), preferred_element_type=f32)
        return (grad_values[None], lax.psum_scatter(product * portion, ("dp", "seq"), scatter_dimension=0, tiled=True))
    turned = kernel(unpack_body, shape(part, 4 * length, bf16), own_turned, beside, pack_turned, vmem=8)
    keep, *sends = kernel(
        weight_body, (shape(part // 4, 2 * state),) * 4, turned, dbc, from_core, from_pack, from_both,
        scratch=[pltpu.VMEM((part, 2 * state), f32)], vmem=16,
    )
    terms = [keep] + to_quad(sends)
    size = part // 4
    for bit in range(1, bits):
        size //= 2
        send, keep = kernel(bind(halve_body, bit), (shape(size, 2 * state), shape(size, 2 * state)), *terms)
        terms = [keep, swap(send, 4 << bit)]
    grad_wbc = (terms[0] + terms[1]) * portion
    return (grad_values[None], grad_wbc)


def solution(mesh):
    placed = (
        P("dp", "seq", None),
        P("dp", "seq", None),
        P("dp", "seq", None),
        P(),
        P("dp", None, "seq"),
        P("dp", "seq"),
    )
    return jax.shard_map(
        local,
        mesh=mesh,
        in_specs=placed,
        out_specs=(P("dp", "seq", None), P(("dp", "seq"), None)),
        check_vma=False,
    )
```

time: 434 us -> 94.3 us (0.22)
  waiting for transfers between devices: 342 us -> 54.5 us
  matrix products: 32.7 us -> 0 us
  other arithmetic: 21.6 us -> 0.65 us
  between operations: 14.2 us -> 0.82 us
  Pallas kernels: 0 us -> 12.8 us
  starting transfers between devices: 12.6 us -> 25.4 us
  local copies, waits for them, and re-layouts: 11 us -> 0.03 us
    ppermute x11 -> x22, waiting for transfers between devices: 213 us -> 54.5 us  [the longest x20 48.2 us: swap(): return lax.ppermute(array, 'seq', [(s, s ^ mask) for s in range(shards)])]
    unnamed x2 -> x0, waiting for transfers between devices: 129 us -> none
    dot_general x11 -> x0, matrix products: 31.5 us -> none  [the longest x1 6.58 us: local(): jnp.einsum('ht,thp,hnp->tn', cumulative, cots, before, precision=highest)]
    select_n x7 -> x0, other arithmetic: 18.6 us -> none  [the longest x4 16.8 us: pick_pair(): jnp.where(flag, first[1], second[1])]
    ppermute x11 -> x22, starting transfers between devices: 12.6 us -> 25.4 us  [the longest x20 21.4 us: swap(): return lax.ppermute(array, 'seq', [(s, s ^ mask) for s in range(shards)])]
    pallas_call x0 -> x15, Pallas kernels: none -> 12.8 us  [kernel(): pl.pallas_call(run, in_specs=[there] * count + [pl.BlockSpec(memory_space...]
    unnamed x19 -> x10, local copies, waits for them, and re-layouts: 9.62 us -> 0.03 us
  transfers between devices with their start and end apart: 12 -> 22, of which waited for: 7 -> 17; matrix products, arithmetic and copies ran while one was open for 6% -> 0% of each run, Pallas kernels for 0% -> 6%
where the time goes in v1:
time: 94.3 us; the launch traced here: 94.2 us
  waiting for transfers between devices  54.5 us (58%)
  starting transfers between devices  25.4 us (27%)
  Pallas kernels  12.8 us (14%)
    ppermute x20, waiting for transfers between devices, swap(): return lax.ppermute(array, 'seq', [(s, s ^ mask) for s in range(shards)])  48.2 us
    ppermute x20, starting transfers between devices, swap(): return lax.ppermute(array, 'seq', [(s, s ^ mask) for s in range(shards)])  21.4 us
    pallas_call x15, Pallas kernels, kernel(): pl.pallas_call(run, in_specs=[there] * count + [pl.BlockSpec(memory_space...  12.8 us
    ppermute x2, waiting for transfers between devices, swap_pack(): return lax.ppermute(array, 'dp', [(d, d ^ 1) for d in range(packs)])  6.31 us
    ppermute x2, starting transfers between devices, swap_pack(): return lax.ppermute(array, 'dp', [(d, d ^ 1) for d in range(packs)])  4.1 us
  transfers between devices with their start and end apart: 22, of which 17 were waited for; matrix products, arithmetic and copies ran while one was open for 0% of the time, Pallas kernels for 6%

profile of v1, /device:TPU:0, one launch (start us, length us, event | category | flops | bytes accessed | tf_op | source)
XLA Modules:
  0.0 94.2 jit_solution(6995733526477068145)
XLA Ops:
  0.6 5.6 %shard_map.77 = (f32[2592,128]{1,0:T(8,128)S(1)}, f32[1280,128]{1,0:T(8,128)S(1)}, f32[1280,128]{1,0:T(8,128)S(1)}, f32[32,128]{1,0:T(8,128)S(1)}, bf16[192,2560...) custom-call(bf16[1,192,2560]{2,1,0:T(8,128)(2,1)} %refs_0_.1, ...), custom_call_target="tpu_custom_call" | custom-call | flops 1000 | bytes 1000 | tf_op jit(solution)/shard_map/pallas_call | solution.py:417
  7.4 2.6 %collective-permute-start.9 = (f32[1920,128]{1,0:T(8,128)S(1)}, f32[1920,128]{1,0:T(8,128)S(1)}, u32[]{:S(2)}, u32[]{:S(2)}) collective-permute-start(f32[1920,128]{1,0:T(8,128)S(1)} %get-tuple-element.59), channel_id=1, source_target_pairs={{0,16},{16,0},{1,17},{17,1},{2,18},{18,2},{3,19},{19,3},{4,20},{20... | collective-permute-start | bytes 2949128 | tf_op jit(solution)/shard_map/ppermute | solution.py:436
  10.1 2.3 %collective-permute-start.1 = (f32[392,128]{1,0:T(8,128)S(1)}, f32[392,128]{1,0:T(8,128)S(1)}, u32[]{:S(2)}, u32[]{:S(2)}) collective-permute-start(f32[392,128]{1,0:T(8,128)S(1)} %get-tuple-element.46), channel_id=1, source_target_pairs={{0,2},{1,3},{2,0},{3,1},{4,6},{5,7},{6,4},{7,5},{8,10},{9,11},{10,... | collective-permute-start | bytes 602120 | tf_op jit(solution)/shard_map/ppermute | solution.py:433
  12.5 1.6 %collective-permute-start.5 = (f32[392,128]{1,0:T(8,128)S(1)}, f32[392,128]{1,0:T(8,128)S(1)}, u32[]{:S(2)}, u32[]{:S(2)}) collective-permute-start(f32[392,128]{1,0:T(8,128)S(1)} %get-tuple-element.51), channel_id=1, source_target_pairs={{0,4},{1,5},{2,6},{3,7},{4,0},{5,1},{6,2},{7,3},{8,12},{9,13},{10,... | collective-permute-start | bytes 602120 | tf_op jit(solution)/shard_map/ppermute | solution.py:433
  14.0 3.7 %collective-permute-done.1.refs_5_.refs_1_ = f32[392,128]{1,0:T(8,128)S(1)} collective-permute-done((f32[392,128]{1,0:T(8,128)S(1)}, f32[392,128]{1,0:T(8,128)S(1)}, u32[]{:S(2)}, u32[]{:S(2)}) %collective-permute-start.1) | collective-permute-done | bytes 200736 | tf_op jit(solution)/shard_map/ppermute | solution.py:433
  17.9 1.8 %collective-permute-start.2 = (f32[264,128]{1,0:T(8,128)S(1)}, f32[264,128]{1,0:T(8,128)S(1)}, u32[]{:S(2)}, u32[]{:S(2)}) collective-permute-start(f32[264,128]{1,0:T(8,128)S(1)} %get-tuple-element.48), channel_id=1, source_target_pairs={{0,2},{1,3},{2,0},{3,1},{4,6},{5,7},{6,4},{7,5},{8,10},{9,11},{10,... | collective-permute-start | bytes 405512 | tf_op jit(solution)/shard_map/ppermute | solution.py:433
  19.7 1.6 %collective-permute-start.3 = (f32[264,128]{1,0:T(8,128)S(1)}, f32[264,128]{1,0:T(8,128)S(1)}, u32[]{:S(2)}, u32[]{:S(2)}) collective-permute-start(f32[264,128]{1,0:T(8,128)S(1)} %get-tuple-element.49), channel_id=1, source_target_pairs={{0,4},{1,5},{2,6},{3,7},{4,0},{5,1},{6,2},{7,3},{8,12},{9,13},{10,... | collective-permute-start | bytes 405512 | tf_op jit(solution)/shard_map/ppermute | solution.py:433
  21.9 2.3 %collective-permute-done.6.refs_3_ = f32[392,128]{1,0:T(8,128)S(1)} collective-permute-done((f32[392,128]{1,0:T(8,128)S(1)}, f32[392,128]{1,0:T(8,128)S(1)}, u32[]{:S(2)}, u32[]{:S(2)}) %collective-permute-start.6) | collective-permute-done | bytes 200736 | tf_op jit(solution)/shard_map/ppermute | solution.py:433
  24.2 2.7 %collective-permute-done.2.refs_1_.refs_6_ = f32[264,128]{1,0:T(8,128)S(1)} collective-permute-done((f32[264,128]{1,0:T(8,128)S(1)}, f32[264,128]{1,0:T(8,128)S(1)}, u32[]{:S(2)}, u32[]{:S(2)}) %collective-permute-start.2) | collective-permute-done | bytes 135200 | tf_op jit(solution)/shard_map/ppermute | solution.py:433
  27.6 1.6 %collective-permute-done.4.refs_3_.refs_8_ = f32[264,128]{1,0:T(8,128)S(1)} collective-permute-done((f32[264,128]{1,0:T(8,128)S(1)}, f32[264,128]{1,0:T(8,128)S(1)}, u32[]{:S(2)}, u32[]{:S(2)}) %collective-permute-start.4) | collective-permute-done | bytes 135200 | tf_op jit(solution)/shard_map/ppermute | solution.py:433
  29.3 2.4 %shard_map.83 = (f32[192,2560]{1,0:T(8,128)S(1)}, f32[192,2560]{1,0:T(8,128)S(1)}, f32[192,256]{1,0:T(8,128)S(1)}) custom-call(bf16[192,2560]{1,0:T(8,128)(2,1)S(1)} %bitcast.6, bf16[192,2560]{1,0:T(8,128)(2,1)S(1)} %bitcast.7, s32[40,192]{1,0:T(8,128)S(1)} %bitcast.8, s32[1,192]{1,0:T(1,128)S(1)} %copy-done.4, ...), custom_call_target="tpu_custom_call" | custom-call | flops 1000 | bytes 1000 | tf_op jit(solution)/shard_map/pallas_call | solution.py:417
  32.6 2.9 %collective-permute-start.7 = (f32[192,128]{1,0:T(8,128)S(1)}, f32[192,128]{1,0:T(8,128)S(1)}, u32[]{:S(2)}, u32[]{:S(2)}) collective-permute-start(f32[192,128]{1,0:T(8,128)S(1)} %shard_map.81.refs_4_), channel_id=1, source_target_pairs={{0,8},{1,9},{2,10},{3,11},{4,12},{5,13},{6,14},{7,15},{8,0},{9,1},... | collective-permute-start | bytes 294920 | tf_op jit(solution)/shard_map/ppermute | solution.py:433
  35.6 7.1 %collective-permute-done.7.refs_4_ = f32[192,128]{1,0:T(8,128)S(1)} collective-permute-done((f32[192,128]{1,0:T(8,128)S(1)}, f32[192,128]{1,0:T(8,128)S(1)}, u32[]{:S(2)}, u32[]{:S(2)}) %collective-permute-start.7) | collective-permute-done | bytes 98336 | tf_op jit(solution)/shard_map/ppermute | solution.py:433
  44.1 1.6 %collective-permute-start.10 = (f32[640,128]{1,0:T(8,128)S(1)}, f32[640,128]{1,0:T(8,128)S(1)}, u32[]{:S(2)}, u32[]{:S(2)}) collective-permute-start(f32[640,128]{1,0:T(8,128)S(1)} %get-tuple-element.61), channel_id=1, source_target_pairs={{0,2},{1,3},{2,0},{3,1},{4,6},{5,7},{6,4},{7,5},{8,10},{9,11},{10,... | collective-permute-start | bytes 983048 | tf_op jit(solution)/shard_map/ppermute | solution.py:433
  47.6 6.2 %collective-permute-done.10.refs_1_ = f32[640,128]{1,0:T(8,128)S(1)} collective-permute-done((f32[640,128]{1,0:T(8,128)S(1)}, f32[640,128]{1,0:T(8,128)S(1)}, u32[]{:S(2)}, u32[]{:S(2)}) %collective-permute-start.10) | collective-permute-done | bytes 327712 | tf_op jit(solution)/shard_map/ppermute | solution.py:433
  53.9 2.5 %collective-permute-done.11.refs_2_ = f32[640,128]{1,0:T(8,128)S(1)} collective-permute-done((f32[640,128]{1,0:T(8,128)S(1)}, f32[640,128]{1,0:T(8,128)S(1)}, u32[]{:S(2)}, u32[]{:S(2)}) %collective-permute-start.11) | collective-permute-done | bytes 327712 | tf_op jit(solution)/shard_map/ppermute | solution.py:433
  56.3 5.4 %collective-permute-done.12.refs_3_ = f32[640,128]{1,0:T(8,128)S(1)} collective-permute-done((f32[640,128]{1,0:T(8,128)S(1)}, f32[640,128]{1,0:T(8,128)S(1)}, u32[]{:S(2)}, u32[]{:S(2)}) %collective-permute-start.12) | collective-permute-done | bytes 327712 | tf_op jit(solution)/shard_map/ppermute | solution.py:433
  62.2 3.0 %collective-permute-done.14.refs_4_ = f32[2560,128]{1,0:T(8,128)S(1)} collective-permute-done((f32[2560,128]{1,0:T(8,128)S(1)}, f32[2560,128]{1,0:T(8,128)S(1)}, u32[]{:S(2)}, u32[]{:S(2)}) %collective-permute-start.14) | collective-permute-done | bytes 1310752 | tf_op jit(solution)/shard_map/ppermute | solution.py:433
  67.5 5.5 %collective-permute-done.16.refs_3_ = f32[192,256]{1,0:T(8,128)S(1)} collective-permute-done((f32[192,256]{1,0:T(8,128)S(1)}, f32[192,256]{1,0:T(8,128)S(1)}, u32[]{:S(2)}, u32[]{:S(2)}) %collective-permute-start.16) | collective-permute-done | bytes 196640 | tf_op jit(solution)/shard_map/ppermute | solution.py:436
  78.9 3.1 %collective-permute-done.18.refs_1_ = f32[160,256]{1,0:T(8,128)S(1)} collective-permute-done((f32[160,256]{1,0:T(8,128)S(1)}, f32[160,256]{1,0:T(8,128)S(1)}, u32[]{:S(2)}, u32[]{:S(2)}) %collective-permute-start.18) | collective-permute-done | bytes 163872 | tf_op jit(solution)/shard_map/ppermute | solution.py:433
  82.0 1.8 %collective-permute-done.19.refs_2_ = f32[160,256]{1,0:T(8,128)S(1)} collective-permute-done((f32[160,256]{1,0:T(8,128)S(1)}, f32[160,256]{1,0:T(8,128)S(1)}, u32[]{:S(2)}, u32[]{:S(2)}) %collective-permute-start.19) | collective-permute-done | bytes 163872 | tf_op jit(solution)/shard_map/ppermute | solution.py:433
  83.9 2.9 %collective-permute-done.20.refs_3_ = f32[160,256]{1,0:T(8,128)S(1)} collective-permute-done((f32[160,256]{1,0:T(8,128)S(1)}, f32[160,256]{1,0:T(8,128)S(1)}, u32[]{:S(2)}, u32[]{:S(2)}) %collective-permute-start.20) | collective-permute-done | bytes 163872 | tf_op jit(solution)/shard_map/ppermute | solution.py:433
  86.8 2.7 %collective-permute-start.21 = (f32[80,256]{1,0:T(8,128)S(1)}, f32[80,256]{1,0:T(8,128)S(1)}, u32[]{:S(2)}, u32[]{:S(2)}) collective-permute-start(f32[80,256]{1,0:T(8,128)S(1)} %get-tuple-element.75), channel_id=1, source_target_pairs={{0,8},{1,9},{2,10},{3,11},{4,12},{5,13},{6,14},{7,15},{8,0},{9,1},... | collective-permute-start | bytes 245768 | tf_op jit(solution)/shard_map/ppermute | solution.py:433
  89.4 4.1 %collective-permute-done.21 = f32[80,256]{1,0:T(8,128)S(1)} collective-permute-done((f32[80,256]{1,0:T(8,128)S(1)}, f32[80,256]{1,0:T(8,128)S(1)}, u32[]{:S(2)}, u32[]{:S(2)}) %collective-permute-start.21) | collective-permute-done | bytes 81952 | tf_op jit(solution)/shard_map/ppermute | solution.py:433
  (46 shorter events, 16.4 us)
Async XLA Ops:
  6.2 3.8 %collective-permute-start = (f32[2592,128]{1,0:T(8,128)S(1)}, f32[2592,128]{1,0:T(8,128)S(1)}, u32[]{:S(2)}, u32[]{:S(2)}) collective-permute-start(f32[2592,128]{1,0:T(8,128)S(1)} %get-tuple-element.43), channel_id=1, source_target_pairs={{0,1},{1,0},{2,3},{3,2},{4,5},{5,4},{6,7},{7,6},{8,9},{9,8},{10,11... | collective-permute-start | bytes 3981320 | tf_op jit(solution)/shard_map/ppermute | solution.py:433
  7.4 25.0 %collective-permute-start.9 = (f32[1920,128]{1,0:T(8,128)S(1)}, f32[1920,128]{1,0:T(8,128)S(1)}, u32[]{:S(2)}, u32[]{:S(2)}) collective-permute-start(f32[1920,128]{1,0:T(8,128)S(1)} %get-tuple-element.59), channel_id=1, source_target_pairs={{0,16},{16,0},{1,17},{17,1},{2,18},{18,2},{3,19},{19,3},{4,20},{20... | collective-permute-start | bytes 2949128 | tf_op jit(solution)/shard_map/ppermute | solution.py:436
  10.1 7.6 %collective-permute-start.1 = (f32[392,128]{1,0:T(8,128)S(1)}, f32[392,128]{1,0:T(8,128)S(1)}, u32[]{:S(2)}, u32[]{:S(2)}) collective-permute-start(f32[392,128]{1,0:T(8,128)S(1)} %get-tuple-element.46), channel_id=1, source_target_pairs={{0,2},{1,3},{2,0},{3,1},{4,6},{5,7},{6,4},{7,5},{8,10},{9,11},{10,... | collective-permute-start | bytes 602120 | tf_op jit(solution)/shard_map/ppermute | solution.py:433
  12.5 8.8 %collective-permute-start.5 = (f32[392,128]{1,0:T(8,128)S(1)}, f32[392,128]{1,0:T(8,128)S(1)}, u32[]{:S(2)}, u32[]{:S(2)}) collective-permute-start(f32[392,128]{1,0:T(8,128)S(1)} %get-tuple-element.51), channel_id=1, source_target_pairs={{0,4},{1,5},{2,6},{3,7},{4,0},{5,1},{6,2},{7,3},{8,12},{9,13},{10,... | collective-permute-start | bytes 602120 | tf_op jit(solution)/shard_map/ppermute | solution.py:433
  14.0 10.1 %collective-permute-start.6 = (f32[392,128]{1,0:T(8,128)S(1)}, f32[392,128]{1,0:T(8,128)S(1)}, u32[]{:S(2)}, u32[]{:S(2)}) collective-permute-start(f32[392,128]{1,0:T(8,128)S(1)} %get-tuple-element.52), channel_id=1, source_target_pairs={{0,6},{1,7},{2,4},{3,5},{4,2},{5,3},{6,0},{7,1},{8,14},{9,15},{10,... | collective-permute-start | bytes 602120 | tf_op jit(solution)/shard_map/ppermute | solution.py:433
  17.7 11.5 %copy-start.2 = (bf16[1,192,2560]{2,1,0:T(8,128)(2,1)S(1)}, bf16[1,192,2560]{2,1,0:T(8,128)(2,1)}, u32[]{:S(2)}) copy-start(bf16[1,192,2560]{2,1,0:T(8,128)(2,1)} %refs_3_.2) | copy-start | bytes 2949124
  17.8 11.4 %copy-start.1 = (bf16[1,192,2560]{2,1,0:T(8,128)(2,1)S(1)}, bf16[1,192,2560]{2,1,0:T(8,128)(2,1)}, u32[]{:S(2)}) copy-start(bf16[1,192,2560]{2,1,0:T(8,128)(2,1)} %refs_2_.1) | copy-start | bytes 2949124
  17.9 9.1 %collective-permute-start.2 = (f32[264,128]{1,0:T(8,128)S(1)}, f32[264,128]{1,0:T(8,128)S(1)}, u32[]{:S(2)}, u32[]{:S(2)}) collective-permute-start(f32[264,128]{1,0:T(8,128)S(1)} %get-tuple-element.48), channel_id=1, source_target_pairs={{0,2},{1,3},{2,0},{3,1},{4,6},{5,7},{6,4},{7,5},{8,10},{9,11},{10,... | collective-permute-start | bytes 405512 | tf_op jit(solution)/shard_map/ppermute | solution.py:433
  19.7 7.9 %collective-permute-start.3 = (f32[264,128]{1,0:T(8,128)S(1)}, f32[264,128]{1,0:T(8,128)S(1)}, u32[]{:S(2)}, u32[]{:S(2)}) collective-permute-start(f32[264,128]{1,0:T(8,128)S(1)} %get-tuple-element.49), channel_id=1, source_target_pairs={{0,4},{1,5},{2,6},{3,7},{4,0},{5,1},{6,2},{7,3},{8,12},{9,13},{10,... | collective-permute-start | bytes 405512 | tf_op jit(solution)/shard_map/ppermute | solution.py:433
  21.2 7.9 %collective-permute-start.4 = (f32[264,128]{1,0:T(8,128)S(1)}, f32[264,128]{1,0:T(8,128)S(1)}, u32[]{:S(2)}, u32[]{:S(2)}) collective-permute-start(f32[264,128]{1,0:T(8,128)S(1)} %get-tuple-element.50), channel_id=1, source_target_pairs={{0,6},{1,7},{2,4},{3,5},{4,2},{5,3},{6,0},{7,1},{8,14},{9,15},{10,... | collective-permute-start | bytes 405512 | tf_op jit(solution)/shard_map/ppermute | solution.py:433
  32.5 29.3 %collective-permute-start.13 = (f32[1920,128]{1,0:T(8,128)S(1)}, f32[1920,128]{1,0:T(8,128)S(1)}, u32[]{:S(2)}, u32[]{:S(2)}) collective-permute-start(f32[1920,128]{1,0:T(8,128)S(1)} %shard_map.84.refs_10_), channel_id=1, source_target_pairs={{0,1},{1,0},{2,3},{3,2},{4,5},{5,4},{6,7},{7,6},{8,9},{9,8},{10,11... | collective-permute-start | bytes 2949128 | tf_op jit(solution)/shard_map/ppermute | solution.py:433
  32.6 10.1 %collective-permute-start.7 = (f32[192,128]{1,0:T(8,128)S(1)}, f32[192,128]{1,0:T(8,128)S(1)}, u32[]{:S(2)}, u32[]{:S(2)}) collective-permute-start(f32[192,128]{1,0:T(8,128)S(1)} %shard_map.81.refs_4_), channel_id=1, source_target_pairs={{0,8},{1,9},{2,10},{3,11},{4,12},{5,13},{6,14},{7,15},{8,0},{9,1},... | collective-permute-start | bytes 294920 | tf_op jit(solution)/shard_map/ppermute | solution.py:433
  35.4 8.3 %collective-permute-start.8 = (f32[128,128]{1,0:T(8,128)S(1)}, f32[128,128]{1,0:T(8,128)S(1)}, u32[]{:S(2)}, u32[]{:S(2)}) collective-permute-start(f32[128,128]{1,0:T(8,128)S(1)} %shard_map.82.refs_5_), channel_id=1, source_target_pairs={{0,8},{1,9},{2,10},{3,11},{4,12},{5,13},{6,14},{7,15},{8,0},{9,1},... | collective-permute-start | bytes 196616 | tf_op jit(solution)/shard_map/ppermute | solution.py:433
  44.1 9.8 %collective-permute-start.10 = (f32[640,128]{1,0:T(8,128)S(1)}, f32[640,128]{1,0:T(8,128)S(1)}, u32[]{:S(2)}, u32[]{:S(2)}) collective-permute-start(f32[640,128]{1,0:T(8,128)S(1)} %get-tuple-element.61), channel_id=1, source_target_pairs={{0,2},{1,3},{2,0},{3,1},{4,6},{5,7},{6,4},{7,5},{8,10},{9,11},{10,... | collective-permute-start | bytes 983048 | tf_op jit(solution)/shard_map/ppermute | solution.py:433
  45.7 10.6 %collective-permute-start.11 = (f32[640,128]{1,0:T(8,128)S(1)}, f32[640,128]{1,0:T(8,128)S(1)}, u32[]{:S(2)}, u32[]{:S(2)}) collective-permute-start(f32[640,128]{1,0:T(8,128)S(1)} %get-tuple-element.62), channel_id=1, source_target_pairs={{0,4},{1,5},{2,6},{3,7},{4,0},{5,1},{6,2},{7,3},{8,12},{9,13},{10,... | collective-permute-start | bytes 983048 | tf_op jit(solution)/shard_map/ppermute | solution.py:433
  46.4 15.4 %collective-permute-start.12 = (f32[640,128]{1,0:T(8,128)S(1)}, f32[640,128]{1,0:T(8,128)S(1)}, u32[]{:S(2)}, u32[]{:S(2)}) collective-permute-start(f32[640,128]{1,0:T(8,128)S(1)} %get-tuple-element.63), channel_id=1, source_target_pairs={{0,6},{1,7},{2,4},{3,5},{4,2},{5,3},{6,0},{7,1},{8,14},{9,15},{10,... | collective-permute-start | bytes 983048 | tf_op jit(solution)/shard_map/ppermute | solution.py:433
  62.1 3.1 %collective-permute-start.14 = (f32[2560,128]{1,0:T(8,128)S(1)}, f32[2560,128]{1,0:T(8,128)S(1)}, u32[]{:S(2)}, u32[]{:S(2)}) collective-permute-start(f32[2560,128]{1,0:T(8,128)S(1)} %get-tuple-element.65.refs_5_), channel_id=1, source_target_pairs={{0,1},{1,0},{2,3},{3,2},{4,5},{5,4},{6,7},{7,6},{8,9},{9,8},{10,11... | collective-permute-start | bytes 3932168 | tf_op jit(solution)/shard_map/ppermute | solution.py:433
  66.0 7.0 %collective-permute-start.16 = (f32[192,256]{1,0:T(8,128)S(1)}, f32[192,256]{1,0:T(8,128)S(1)}, u32[]{:S(2)}, u32[]{:S(2)}) collective-permute-start(f32[192,256]{1,0:T(8,128)S(1)} %get-tuple-element.67.refs_4_.refs_1_), channel_id=1, source_target_pairs={{0,16},{16,0},{1,17},{17,1},{2,18},{18,2},{3,19},{19,3},{4,20},{20... | collective-permute-start | bytes 589832 | tf_op jit(solution)/shard_map/ppermute | solution.py:436
  67.5 7.3 %collective-permute-start.15 = (f32[192,256]{1,0:T(8,128)S(1)}, f32[192,256]{1,0:T(8,128)S(1)}, u32[]{:S(2)}, u32[]{:S(2)}) collective-permute-start(f32[192,256]{1,0:T(8,128)S(1)} %get-tuple-element.67.refs_4_.refs_1_), channel_id=1, source_target_pairs={{0,1},{1,0},{2,3},{3,2},{4,5},{5,4},{6,7},{7,6},{8,9},{9,8},{10,11... | collective-permute-start | bytes 589832 | tf_op jit(solution)/shard_map/ppermute | solution.py:433
  73.0 1.8 %collective-permute-start.17 = (f32[192,256]{1,0:T(8,128)S(1)}, f32[192,256]{1,0:T(8,128)S(1)}, u32[]{:S(2)}, u32[]{:S(2)}) collective-permute-start(f32[192,256]{1,0:T(8,128)S(1)} %collective-permute-done.16.refs_3_), channel_id=1, source_target_pairs={{0,1},{1,0},{2,3},{3,2},{4,5},{5,4},{6,7},{7,6},{8,9},{9,8},{10,11... | collective-permute-start | bytes 589832 | tf_op jit(solution)/shard_map/ppermute | solution.py:433
  75.4 6.7 %collective-permute-start.18 = (f32[160,256]{1,0:T(8,128)S(1)}, f32[160,256]{1,0:T(8,128)S(1)}, u32[]{:S(2)}, u32[]{:S(2)}) collective-permute-start(f32[160,256]{1,0:T(8,128)S(1)} %get-tuple-element.71), channel_id=1, source_target_pairs={{0,2},{1,3},{2,0},{3,1},{4,6},{5,7},{6,4},{7,5},{8,10},{9,11},{10,... | collective-permute-start | bytes 491528 | tf_op jit(solution)/shard_map/ppermute | solution.py:433
  76.8 7.0 %collective-permute-start.19 = (f32[160,256]{1,0:T(8,128)S(1)}, f32[160,256]{1,0:T(8,128)S(1)}, u32[]{:S(2)}, u32[]{:S(2)}) collective-permute-start(f32[160,256]{1,0:T(8,128)S(1)} %get-tuple-element.72), channel_id=1, source_target_pairs={{0,4},{1,5},{2,6},{3,7},{4,0},{5,1},{6,2},{7,3},{8,12},{9,13},{10,... | collective-permute-start | bytes 491528 | tf_op jit(solution)/shard_map/ppermute | solution.py:433
  77.9 8.8 %collective-permute-start.20 = (f32[160,256]{1,0:T(8,128)S(1)}, f32[160,256]{1,0:T(8,128)S(1)}, u32[]{:S(2)}, u32[]{:S(2)}) collective-permute-start(f32[160,256]{1,0:T(8,128)S(1)} %get-tuple-element.73), channel_id=1, source_target_pairs={{0,6},{1,7},{2,4},{3,5},{4,2},{5,3},{6,0},{7,1},{8,14},{9,15},{10,... | collective-permute-start | bytes 491528 | tf_op jit(solution)/shard_map/ppermute | solution.py:433
  86.8 6.7 %collective-permute-start.21 = (f32[80,256]{1,0:T(8,128)S(1)}, f32[80,256]{1,0:T(8,128)S(1)}, u32[]{:S(2)}, u32[]{:S(2)}) collective-permute-start(f32[80,256]{1,0:T(8,128)S(1)} %get-tuple-element.75), channel_id=1, source_target_pairs={{0,8},{1,9},{2,10},{3,11},{4,12},{5,13},{6,14},{7,15},{8,0},{9,1},... | collective-permute-start | bytes 245768 | tf_op jit(solution)/shard_map/ppermute | solution.py:433
  (3 other events, 28.9 us)

commit v2 on v1

--- a/solution.py
+++ b/solution.py
@@ -229,54 +229,54 @@
         store_total(out, joined(mine, theirs, level_bit(place, bit)), size, head, k, upper)
 
 
-def enter_body(chunks, head, bits, place, *refs):
-    outs = refs[-4:]
-    second, later, total = place[1] == 1, level_bit(place, 0), outs[0].shape[0] // 2
-    each = 4 + bits - 1
-    for number, (start, size) in enumerate(chunks):
-        own, one, two, three, *levels, final = refs[number * each:(number + 1) * each]
-        for k in range(size):
-            before, behind, left, right = 0.0, 0.0, 1.0, 1.0
-            for bit, recv in enumerate(levels):
-                high = level_bit(place, bit + 1)
-                forward, backward, decay = parts(recv, size, head, k)
-                before = before + pick(high, left, 0.0) * forward
-                behind = behind + pick(high, 0.0, right) * backward
-                left = pick(high, left * decay, left)
-                right = pick(high, right, right * decay)
-            high = level_bit(place, bits - 1)
-            last = final[k * head:(k + 1) * head, :]
-            before = before + pick(high, left, 0.0) * last
-            behind = behind + pick(high, 0.0, right) * last
-            here, beside, along, across = (parts(ref, size, head, k) for ref in (own, one, two, three))
-            row, other = entering(joined(here, beside, second), joined(along, across, second), later, before, behind)
-            states = entering(here, beside, second, *row) + entering(along, across, second, *other)
-            at = (start + k) * head
-            for out, (state_before, state_behind) in zip(outs, states):
-                out[at:at + head, :] = state_before
-                out[total + at:total + at + head, :] = state_behind
-
-
-def core_body(start, size, head, place, *refs):
-    states, keep_f, keep_g, decays, recv, send, own = refs[:4], *refs[4:]
+def enter_body(size, head, bits, place, own, one, two, three, *refs):
+    levels, final, outs = refs[:bits - 2], refs[bits - 2], refs[bits - 1:]
     rows = size * head
+    second, later = place[1] == 1, level_bit(place, 0)
+    for k in range(size):
+        before, behind, left, right = 0.0, 0.0, 1.0, 1.0
+        for bit, recv in enumerate(levels):
+            high = level_bit(place, bit + 1)
+            forward, backward, decay = parts(recv, size, head, k)
+            before = before + pick(high, left, 0.0) * forward
+            behind = behind + pick(high, 0.0, right) * backward
+            left = pick(high, left * decay, left)
+            right = pick(high, right, right * decay)
+        high = level_bit(place, bits - 1)
+        at, after = slice(k * head, (k + 1) * head), slice(rows + k * head, rows + (k + 1) * head)
+        last = final[at, :]
+        before = before + pick(high, left, 0.0) * last
+        behind = behind + pick(high, 0.0, right) * last
+        here, beside, along, across = (parts(ref, size, head, k) for ref in (own, one, two, three))
+        row, other = entering(joined(here, beside, second), joined(along, across, second), later, before, behind)
+        states = entering(here, beside, second, *row) + entering(along, across, second, *other)
+        for out, (state_before, state_behind) in zip(outs, states):
+            out[at, :] = state_before
+            out[after, :] = state_behind
+
+
+def core_body(chunks, head, place, *refs):
+    count = 4 * len(chunks)
+    keep_f, keep_g, decays, recv, send, own = refs[count:]
     base = keep_f.shape[0]
+    rows = base // 4
     slot = decays.shape[0] // 4
     second = place[0] == 1
-    for flip, ref in enumerate(states):
-        for k in range(size):
-            at = flip * (base // 4) + (start + k) * head
-            spot = flip * slot + start + k
-            here = decays[spot:spot + 1, :]
-            there = recv[2 * base + spot:2 * base + spot + 1, :]
-            state = ref[k * head:(k + 1) * head, :]
-            to = slice(flip * rows + k * head, flip * rows + (k + 1) * head)
-            send[to, :] = pick(second, 1.0, here) * state + pick(second, 0.0, 1.0) * keep_f[at:at + head, :]
-            own[to, :] = (pick(second, there, 1.0) * state + pick(second, 1.0, 0.0) * recv[at:at + head, :]).astype(bf16)
-            state = ref[rows + k * head:rows + (k + 1) * head, :]
-            to = slice((4 + flip) * rows + k * head, (4 + flip) * rows + (k + 1) * head)
-            send[to, :] = pick(second, here, 1.0) * state + pick(second, 1.0, 0.0) * keep_g[at:at + head, :]
-            own[to, :] = (pick(second, 1.0, there) * state + pick(second, 0.0, 1.0) * recv[base + at:base + at + head, :]).astype(bf16)
+    for number, (start, size) in enumerate(chunks):
+        for flip, ref in enumerate(refs[number * 4:number * 4 + 4]):
+            for k in range(size):
+                at = flip * rows + (start + k) * head
+                spot = flip * slot + start + k
+                here = decays[spot:spot + 1, :]
+                there = recv[2 * base + spot:2 * base + spot + 1, :]
+                state = ref[k * head:(k + 1) * head, :]
+                to, got = slice(at, at + head), recv[at:at + head, :]
+                send[to, :] = pick(second, 1.0, here) * state + pick(second, 0.0, 1.0) * keep_f[to, :]
+                own[to, :] = (pick(second, there, 1.0) * state + pick(second, 1.0, 0.0) * got).astype(bf16)
+                state = ref[(size + k) * head:(size + k + 1) * head, :]
+                to, got = slice(base + at, base + at + head), recv[base + at:base + at + head, :]
+                send[to, :] = pick(second, here, 1.0) * state + pick(second, 1.0, 0.0) * keep_g[at:at + head, :]
+                own[to, :] = (pick(second, 1.0, there) * state + pick(second, 0.0, 1.0) * got).astype(bf16)
 
 
 def cross_body(chunks, head, place, u_ref, v_ref, local_ref, *refs):
@@ -497,15 +497,15 @@
         local_body, (shape(length, width), shape(length, width), shape(length, 2 * state)),
         vals, cots, rate, starts, bc, vmem=24,
     )
-    if direct:
-        beside = swap(kernel(stack_body, shape(2 * wide, LANES), core_turned, pack_turned, vmem=8), 1)
-    pieces = [array for group, steps in zip(quads, arrived) for array in group + steps]
-    enter, *sends = kernel(
-        bind(enter_body, chunks, head, bits), (shape(2 * eighth * head, state),) * 4, *pieces,
-    )
+    states = []
+    for number, ((start, size), group, steps) in enumerate(zip(chunks, quads, arrived)):
+        waits = states[1:2] if states else ([pack_turned] if direct else [])
+        enter, *sends = kernel(
+            bind(enter_body, size, head, bits), (shape(2 * size * head, state),) * 4, *group, *steps, behind=waits,
+        )
+        states += [enter] + to_quad(sends)
     send, final = kernel(
-        bind(core_body, 0, eighth, head), (shape(base * 2, state), shape(base * 2, state, bf16)),
-        enter, *to_quad(sends), keep_f, keep_g, decays, recv, behind=[beside] if direct else [],
+        bind(core_body, chunks, head), (shape(2 * base, state), shape(2 * base, state, bf16)), *states, keep_f, keep_g, decays, recv,
     )
     core_recv = swap(send, 1)
     dbc, after = kernel(
@@ -517,6 +517,7 @@
         from_pack = swap_pack(dbc)
         from_core = swap(dbc, 1)
         from_both = swap(from_pack, 1)
+        beside = swap(kernel(stack_body, shape(2 * wide, LANES), core_turned, pack_turned, vmem=8), 1)
     grad_values, unused_done = kernel(
         values_body, (shape(length, width, bf16), shape(8, LANES)), grad_local, scale, bc, after, vmem=16,
     )

time: 94.3 us -> 86.3 us (0.915)
  waiting for transfers between devices: 54.5 us -> 41.3 us
  starting transfers between devices: 25.4 us -> 30.6 us
    ppermute x20 -> x23, waiting for transfers between devices: 48.2 us -> 35.7 us  [swap(): return lax.ppermute(array, 'seq', [(s, s ^ mask) for s in range(shards)])]
    ppermute x20 -> x23, starting transfers between devices: 21.4 us -> 26.5 us  [swap(): return lax.ppermute(array, 'seq', [(s, s ^ mask) for s in range(shards)])]
    pallas_call x15 -> x16, Pallas kernels: 12.8 us -> 12.8 us  [kernel(): pl.pallas_call(run, in_specs=[there] * count + [pl.BlockSpec(memory_space...]
  transfers between devices with their start and end apart: 22 -> 25, of which waited for: 17 -> 15; matrix products, arithmetic and copies ran while one was open for 0% -> 0% of each run, Pallas kernels for 6% -> 6%
where the time goes in v2:
time: 86.3 us; the launch traced here: 86.2 us
  waiting for transfers between devices  41.3 us (48%)
  starting transfers between devices  30.6 us (35%)
  Pallas kernels  12.8 us (15%)
    ppermute x23, waiting for transfers between devices, swap(): return lax.ppermute(array, 'seq', [(s, s ^ mask) for s in range(shards)])  35.7 us
    ppermute x23, starting transfers between devices, swap(): return lax.ppermute(array, 'seq', [(s, s ^ mask) for s in range(shards)])  26.5 us
    pallas_call x16, Pallas kernels, kernel(): pl.pallas_call(run, in_specs=[there] * count + [pl.BlockSpec(memory_space...  12.8 us
    ppermute x2, waiting for transfers between devices, swap_pack(): return lax.ppermute(array, 'dp', [(d, d ^ 1) for d in range(packs)])  5.58 us
    ppermute x2, starting transfers between devices, swap_pack(): return lax.ppermute(array, 'dp', [(d, d ^ 1) for d in range(packs)])  4.14 us
  transfers between devices with their start and end apart: 25, of which 15 were waited for; matrix products, arithmetic and copies ran while one was open for 0% of the time, Pallas kernels for 6%

profile of v2, /device:TPU:0, one launch (start us, length us, event | category | flops | bytes accessed | tf_op | source)
XLA Modules:
  0.0 86.2 jit_solution(18044950503145343125)
XLA Ops:
  0.6 5.6 %shard_map.77 = (f32[2592,128]{1,0:T(8,128)S(1)}, f32[1280,128]{1,0:T(8,128)S(1)}, f32[1280,128]{1,0:T(8,128)S(1)}, f32[32,128]{1,0:T(8,128)S(1)}, bf16[192,2560...) custom-call(bf16[1,192,2560]{2,1,0:T(8,128)(2,1)} %refs_0_.1, ...), custom_call_target="tpu_custom_call" | custom-call | flops 1000 | bytes 1000 | tf_op jit(solution)/shard_map/pallas_call | solution.py:417
  7.4 2.6 %collective-permute-start.8 = (f32[1920,128]{1,0:T(8,128)S(1)}, f32[1920,128]{1,0:T(8,128)S(1)}, u32[]{:S(2)}, u32[]{:S(2)}) collective-permute-start(f32[1920,128]{1,0:T(8,128)S(1)} %get-tuple-element.62), channel_id=1, source_target_pairs={{0,16},{16,0},{1,17},{17,1},{2,18},{18,2},{3,19},{19,3},{4,20},{20... | collective-permute-start | bytes 2949128 | tf_op jit(solution)/shard_map/ppermute | solution.py:436
  10.1 2.3 %collective-permute-start.1 = (f32[392,128]{1,0:T(8,128)S(1)}, f32[392,128]{1,0:T(8,128)S(1)}, u32[]{:S(2)}, u32[]{:S(2)}) collective-permute-start(f32[392,128]{1,0:T(8,128)S(1)} %get-tuple-element.50), channel_id=1, source_target_pairs={{0,2},{1,3},{2,0},{3,1},{4,6},{5,7},{6,4},{7,5},{8,10},{9,11},{10,... | collective-permute-start | bytes 602120 | tf_op jit(solution)/shard_map/ppermute | solution.py:433
  12.5 1.6 %collective-permute-start.5 = (f32[392,128]{1,0:T(8,128)S(1)}, f32[392,128]{1,0:T(8,128)S(1)}, u32[]{:S(2)}, u32[]{:S(2)}) collective-permute-start(f32[392,128]{1,0:T(8,128)S(1)} %get-tuple-element.55), channel_id=1, source_target_pairs={{0,4},{1,5},{2,6},{3,7},{4,0},{5,1},{6,2},{7,3},{8,12},{9,13},{10,... | collective-permute-start | bytes 602120 | tf_op jit(solution)/shard_map/ppermute | solution.py:433
  14.0 3.7 %collective-permute-done.1.refs_5_.refs_1_ = f32[392,128]{1,0:T(8,128)S(1)} collective-permute-done((f32[392,128]{1,0:T(8,128)S(1)}, f32[392,128]{1,0:T(8,128)S(1)}, u32[]{:S(2)}, u32[]{:S(2)}) %collective-permute-start.1) | collective-permute-done | bytes 200736 | tf_op jit(solution)/shard_map/ppermute | solution.py:433
  17.9 1.8 %collective-permute-start.2 = (f32[264,128]{1,0:T(8,128)S(1)}, f32[264,128]{1,0:T(8,128)S(1)}, u32[]{:S(2)}, u32[]{:S(2)}) collective-permute-start(f32[264,128]{1,0:T(8,128)S(1)} %get-tuple-element.52), channel_id=1, source_target_pairs={{0,2},{1,3},{2,0},{3,1},{4,6},{5,7},{6,4},{7,5},{8,10},{9,11},{10,... | collective-permute-start | bytes 405512 | tf_op jit(solution)/shard_map/ppermute | solution.py:433
  19.7 1.6 %collective-permute-start.3 = (f32[264,128]{1,0:T(8,128)S(1)}, f32[264,128]{1,0:T(8,128)S(1)}, u32[]{:S(2)}, u32[]{:S(2)}) collective-permute-start(f32[264,128]{1,0:T(8,128)S(1)} %get-tuple-element.53), channel_id=1, source_target_pairs={{0,4},{1,5},{2,6},{3,7},{4,0},{5,1},{6,2},{7,3},{8,12},{9,13},{10,... | collective-permute-start | bytes 405512 | tf_op jit(solution)/shard_map/ppermute | solution.py:433
  21.9 2.3 %collective-permute-done.6.refs_3_ = f32[392,128]{1,0:T(8,128)S(1)} collective-permute-done((f32[392,128]{1,0:T(8,128)S(1)}, f32[392,128]{1,0:T(8,128)S(1)}, u32[]{:S(2)}, u32[]{:S(2)}) %collective-permute-start.6) | collective-permute-done | bytes 200736 | tf_op jit(solution)/shard_map/ppermute | solution.py:433
  24.2 3.2 %collective-permute-start.7 = (f32[192,128]{1,0:T(8,128)S(1)}, f32[192,128]{1,0:T(8,128)S(1)}, u32[]{:S(2)}, u32[]{:S(2)}) collective-permute-start(f32[192,128]{1,0:T(8,128)S(1)} %shard_map.81.refs_4_), channel_id=1, source_target_pairs={{0,8},{1,9},{2,10},{3,11},{4,12},{5,13},{6,14},{7,15},{8,0},{9,1},... | collective-permute-start | bytes 294920 | tf_op jit(solution)/shard_map/ppermute | solution.py:433
  28.6 1.6 %collective-permute-done.4.refs_3_ = f32[264,128]{1,0:T(8,128)S(1)} collective-permute-done((f32[264,128]{1,0:T(8,128)S(1)}, f32[264,128]{1,0:T(8,128)S(1)}, u32[]{:S(2)}, u32[]{:S(2)}) %collective-permute-start.4) | collective-permute-done | bytes 135200 | tf_op jit(solution)/shard_map/ppermute | solution.py:433
  30.3 2.4 %shard_map.83 = (f32[192,2560]{1,0:T(8,128)S(1)}, f32[192,2560]{1,0:T(8,128)S(1)}, f32[192,256]{1,0:T(8,128)S(1)}) custom-call(bf16[192,2560]{1,0:T(8,128)(2,1)S(1)} %bitcast.6, bf16[192,2560]{1,0:T(8,128)(2,1)S(1)} %bitcast.7, s32[40,192]{1,0:T(8,128)S(1)} %bitcast.8, s32[1,192]{1,0:T(1,128)S(1)} %copy-done.4, ...), custom_call_target="tpu_custom_call" | custom-call | flops 1000 | bytes 1000 | tf_op jit(solution)/shard_map/pallas_call | solution.py:417
  32.9 2.8 %collective-permute-start.9 = (f32[384,128]{1,0:T(8,128)S(1)}, f32[384,128]{1,0:T(8,128)S(1)}, u32[]{:S(2)}, u32[]{:S(2)}) collective-permute-start(f32[384,128]{1,0:T(8,128)S(1)} %get-tuple-element.64), channel_id=1, source_target_pairs={{0,2},{1,3},{2,0},{3,1},{4,6},{5,7},{6,4},{7,5},{8,10},{9,11},{10,... | collective-permute-start | bytes 589832 | tf_op jit(solution)/shard_map/ppermute | solution.py:433
  37.2 2.2 %collective-permute-start.10 = (f32[384,128]{1,0:T(8,128)S(1)}, f32[384,128]{1,0:T(8,128)S(1)}, u32[]{:S(2)}, u32[]{:S(2)}) collective-permute-start(f32[384,128]{1,0:T(8,128)S(1)} %get-tuple-element.65), channel_id=1, source_target_pairs={{0,4},{1,5},{2,6},{3,7},{4,0},{5,1},{6,2},{7,3},{8,12},{9,13},{10,... | collective-permute-start | bytes 589832 | tf_op jit(solution)/shard_map/ppermute | solution.py:433
  39.4 1.9 %collective-permute-done.12.refs_4_ = f32[128,128]{1,0:T(8,128)S(1)} collective-permute-done((f32[128,128]{1,0:T(8,128)S(1)}, f32[128,128]{1,0:T(8,128)S(1)}, u32[]{:S(2)}, u32[]{:S(2)}) %collective-permute-start.12) | collective-permute-done | bytes 65568 | tf_op jit(solution)/shard_map/ppermute | solution.py:433
  43.1 1.9 %collective-permute-start.15 = (f32[256,128]{1,0:T(8,128)S(1)}, f32[256,128]{1,0:T(8,128)S(1)}, u32[]{:S(2)}, u32[]{:S(2)}) collective-permute-start(f32[256,128]{1,0:T(8,128)S(1)} %get-tuple-element.70), channel_id=1, source_target_pairs={{0,6},{1,7},{2,4},{3,5},{4,2},{5,3},{6,0},{7,1},{8,14},{9,15},{10,... | collective-permute-start | bytes 393224 | tf_op jit(solution)/shard_map/ppermute | solution.py:433
  45.4 3.9 %collective-permute-done.11.refs_3_ = f32[384,128]{1,0:T(8,128)S(1)} collective-permute-done((f32[384,128]{1,0:T(8,128)S(1)}, f32[384,128]{1,0:T(8,128)S(1)}, u32[]{:S(2)}, u32[]{:S(2)}) %collective-permute-start.11) | collective-permute-done | bytes 196640 | tf_op jit(solution)/shard_map/ppermute | solution.py:433
  49.3 3.0 %collective-permute-done.14.refs_6_ = f32[256,128]{1,0:T(8,128)S(1)} collective-permute-done((f32[256,128]{1,0:T(8,128)S(1)}, f32[256,128]{1,0:T(8,128)S(1)}, u32[]{:S(2)}, u32[]{:S(2)}) %collective-permute-start.14) | collective-permute-done | bytes 131104 | tf_op jit(solution)/shard_map/ppermute | solution.py:433
  53.9 3.0 %collective-permute-done.16.refs_4_ = f32[2560,128]{1,0:T(8,128)S(1)} collective-permute-done((f32[2560,128]{1,0:T(8,128)S(1)}, f32[2560,128]{1,0:T(8,128)S(1)}, u32[]{:S(2)}, u32[]{:S(2)}) %collective-permute-start.16) | collective-permute-done | bytes 1310752 | tf_op jit(solution)/shard_map/ppermute | solution.py:433
  59.5 5.6 %collective-permute-done.19.refs_3_ = f32[192,256]{1,0:T(8,128)S(1)} collective-permute-done((f32[192,256]{1,0:T(8,128)S(1)}, f32[192,256]{1,0:T(8,128)S(1)}, u32[]{:S(2)}, u32[]{:S(2)}) %collective-permute-start.19) | collective-permute-done | bytes 196640 | tf_op jit(solution)/shard_map/ppermute | solution.py:436
  67.5 1.7 %collective-permute-start.21 = (f32[160,256]{1,0:T(8,128)S(1)}, f32[160,256]{1,0:T(8,128)S(1)}, u32[]{:S(2)}, u32[]{:S(2)}) collective-permute-start(f32[160,256]{1,0:T(8,128)S(1)} %get-tuple-element.79), channel_id=1, source_target_pairs={{0,2},{1,3},{2,0},{3,1},{4,6},{5,7},{6,4},{7,5},{8,10},{9,11},{10,... | collective-permute-start | bytes 491528 | tf_op jit(solution)/shard_map/ppermute | solution.py:433
  71.0 3.1 %collective-permute-done.21.refs_1_ = f32[160,256]{1,0:T(8,128)S(1)} collective-permute-done((f32[160,256]{1,0:T(8,128)S(1)}, f32[160,256]{1,0:T(8,128)S(1)}, u32[]{:S(2)}, u32[]{:S(2)}) %collective-permute-start.21) | collective-permute-done | bytes 163872 | tf_op jit(solution)/shard_map/ppermute | solution.py:433
  74.1 2.1 %collective-permute-done.22.refs_2_ = f32[160,256]{1,0:T(8,128)S(1)} collective-permute-done((f32[160,256]{1,0:T(8,128)S(1)}, f32[160,256]{1,0:T(8,128)S(1)}, u32[]{:S(2)}, u32[]{:S(2)}) %collective-permute-start.22) | collective-permute-done | bytes 163872 | tf_op jit(solution)/shard_map/ppermute | solution.py:433
  76.3 2.6 %collective-permute-done.23.refs_3_ = f32[160,256]{1,0:T(8,128)S(1)} collective-permute-done((f32[160,256]{1,0:T(8,128)S(1)}, f32[160,256]{1,0:T(8,128)S(1)}, u32[]{:S(2)}, u32[]{:S(2)}) %collective-permute-start.23) | collective-permute-done | bytes 163872 | tf_op jit(solution)/shard_map/ppermute | solution.py:433
  79.8 5.7 %collective-permute-done.24 = f32[80,256]{1,0:T(8,128)S(1)} collective-permute-done((f32[80,256]{1,0:T(8,128)S(1)}, f32[80,256]{1,0:T(8,128)S(1)}, u32[]{:S(2)}, u32[]{:S(2)}) %collective-permute-start.24) | collective-permute-done | bytes 81952 | tf_op jit(solution)/shard_map/ppermute | solution.py:433
  (53 shorter events, 17.3 us)
Async XLA Ops:
  6.2 3.8 %collective-permute-start = (f32[2592,128]{1,0:T(8,128)S(1)}, f32[2592,128]{1,0:T(8,128)S(1)}, u32[]{:S(2)}, u32[]{:S(2)}) collective-permute-start(f32[2592,128]{1,0:T(8,128)S(1)} %get-tuple-element.47), channel_id=1, source_target_pairs={{0,1},{1,0},{2,3},{3,2},{4,5},{5,4},{6,7},{7,6},{8,9},{9,8},{10,11... | collective-permute-start | bytes 3981320 | tf_op jit(solution)/shard_map/ppermute | solution.py:433
  7.4 25.3 %collective-permute-start.8 = (f32[1920,128]{1,0:T(8,128)S(1)}, f32[1920,128]{1,0:T(8,128)S(1)}, u32[]{:S(2)}, u32[]{:S(2)}) collective-permute-start(f32[1920,128]{1,0:T(8,128)S(1)} %get-tuple-element.62), channel_id=1, source_target_pairs={{0,16},{16,0},{1,17},{17,1},{2,18},{18,2},{3,19},{19,3},{4,20},{20... | collective-permute-start | bytes 2949128 | tf_op jit(solution)/shard_map/ppermute | solution.py:436
  10.1 7.6 %collective-permute-start.1 = (f32[392,128]{1,0:T(8,128)S(1)}, f32[392,128]{1,0:T(8,128)S(1)}, u32[]{:S(2)}, u32[]{:S(2)}) collective-permute-start(f32[392,128]{1,0:T(8,128)S(1)} %get-tuple-element.50), channel_id=1, source_target_pairs={{0,2},{1,3},{2,0},{3,1},{4,6},{5,7},{6,4},{7,5},{8,10},{9,11},{10,... | collective-permute-start | bytes 602120 | tf_op jit(solution)/shard_map/ppermute | solution.py:433
  12.5 8.8 %collective-permute-start.5 = (f32[392,128]{1,0:T(8,128)S(1)}, f32[392,128]{1,0:T(8,128)S(1)}, u32[]{:S(2)}, u32[]{:S(2)}) collective-permute-start(f32[392,128]{1,0:T(8,128)S(1)} %get-tuple-element.55), channel_id=1, source_target_pairs={{0,4},{1,5},{2,6},{3,7},{4,0},{5,1},{6,2},{7,3},{8,12},{9,13},{10,... | collective-permute-start | bytes 602120 | tf_op jit(solution)/shard_map/ppermute | solution.py:433
  14.0 10.1 %collective-permute-start.6 = (f32[392,128]{1,0:T(8,128)S(1)}, f32[392,128]{1,0:T(8,128)S(1)}, u32[]{:S(2)}, u32[]{:S(2)}) collective-permute-start(f32[392,128]{1,0:T(8,128)S(1)} %get-tuple-element.56), channel_id=1, source_target_pairs={{0,6},{1,7},{2,4},{3,5},{4,2},{5,3},{6,0},{7,1},{8,14},{9,15},{10,... | collective-permute-start | bytes 602120 | tf_op jit(solution)/shard_map/ppermute | solution.py:433
  17.9 9.5 %collective-permute-start.2 = (f32[264,128]{1,0:T(8,128)S(1)}, f32[264,128]{1,0:T(8,128)S(1)}, u32[]{:S(2)}, u32[]{:S(2)}) collective-permute-start(f32[264,128]{1,0:T(8,128)S(1)} %get-tuple-element.52), channel_id=1, source_target_pairs={{0,2},{1,3},{2,0},{3,1},{4,6},{5,7},{6,4},{7,5},{8,10},{9,11},{10,... | collective-permute-start | bytes 405512 | tf_op jit(solution)/shard_map/ppermute | solution.py:433
  19.7 9.0 %collective-permute-start.3 = (f32[264,128]{1,0:T(8,128)S(1)}, f32[264,128]{1,0:T(8,128)S(1)}, u32[]{:S(2)}, u32[]{:S(2)}) collective-permute-start(f32[264,128]{1,0:T(8,128)S(1)} %get-tuple-element.53), channel_id=1, source_target_pairs={{0,4},{1,5},{2,6},{3,7},{4,0},{5,1},{6,2},{7,3},{8,12},{9,13},{10,... | collective-permute-start | bytes 405512 | tf_op jit(solution)/shard_map/ppermute | solution.py:433
  21.2 8.9 %collective-permute-start.4 = (f32[264,128]{1,0:T(8,128)S(1)}, f32[264,128]{1,0:T(8,128)S(1)}, u32[]{:S(2)}, u32[]{:S(2)}) collective-permute-start(f32[264,128]{1,0:T(8,128)S(1)} %get-tuple-element.54), channel_id=1, source_target_pairs={{0,6},{1,7},{2,4},{3,5},{4,2},{5,3},{6,0},{7,1},{8,14},{9,15},{10,... | collective-permute-start | bytes 405512 | tf_op jit(solution)/shard_map/ppermute | solution.py:433
  24.2 8.5 %collective-permute-start.7 = (f32[192,128]{1,0:T(8,128)S(1)}, f32[192,128]{1,0:T(8,128)S(1)}, u32[]{:S(2)}, u32[]{:S(2)}) collective-permute-start(f32[192,128]{1,0:T(8,128)S(1)} %shard_map.81.refs_4_), channel_id=1, source_target_pairs={{0,8},{1,9},{2,10},{3,11},{4,12},{5,13},{6,14},{7,15},{8,0},{9,1},... | collective-permute-start | bytes 294920 | tf_op jit(solution)/shard_map/ppermute | solution.py:433
  32.9 8.4 %collective-permute-start.9 = (f32[384,128]{1,0:T(8,128)S(1)}, f32[384,128]{1,0:T(8,128)S(1)}, u32[]{:S(2)}, u32[]{:S(2)}) collective-permute-start(f32[384,128]{1,0:T(8,128)S(1)} %get-tuple-element.64), channel_id=1, source_target_pairs={{0,2},{1,3},{2,0},{3,1},{4,6},{5,7},{6,4},{7,5},{8,10},{9,11},{10,... | collective-permute-start | bytes 589832 | tf_op jit(solution)/shard_map/ppermute | solution.py:433
  35.7 5.6 %collective-permute-start.12 = (f32[128,128]{1,0:T(8,128)S(1)}, f32[128,128]{1,0:T(8,128)S(1)}, u32[]{:S(2)}, u32[]{:S(2)}) collective-permute-start(f32[128,128]{1,0:T(8,128)S(1)} %shard_map.82.refs_5_), channel_id=1, source_target_pairs={{0,8},{1,9},{2,10},{3,11},{4,12},{5,13},{6,14},{7,15},{8,0},{9,1},... | collective-permute-start | bytes 196616 | tf_op jit(solution)/shard_map/ppermute | solution.py:433
  37.2 8.2 %collective-permute-start.10 = (f32[384,128]{1,0:T(8,128)S(1)}, f32[384,128]{1,0:T(8,128)S(1)}, u32[]{:S(2)}, u32[]{:S(2)}) collective-permute-start(f32[384,128]{1,0:T(8,128)S(1)} %get-tuple-element.65), channel_id=1, source_target_pairs={{0,4},{1,5},{2,6},{3,7},{4,0},{5,1},{6,2},{7,3},{8,12},{9,13},{10,... | collective-permute-start | bytes 589832 | tf_op jit(solution)/shard_map/ppermute | solution.py:433
  39.4 9.9 %collective-permute-start.11 = (f32[384,128]{1,0:T(8,128)S(1)}, f32[384,128]{1,0:T(8,128)S(1)}, u32[]{:S(2)}, u32[]{:S(2)}) collective-permute-start(f32[384,128]{1,0:T(8,128)S(1)} %get-tuple-element.66), channel_id=1, source_target_pairs={{0,6},{1,7},{2,4},{3,5},{4,2},{5,3},{6,0},{7,1},{8,14},{9,15},{10,... | collective-permute-start | bytes 589832 | tf_op jit(solution)/shard_map/ppermute | solution.py:433
  41.4 7.8 %collective-permute-start.13 = (f32[256,128]{1,0:T(8,128)S(1)}, f32[256,128]{1,0:T(8,128)S(1)}, u32[]{:S(2)}, u32[]{:S(2)}) collective-permute-start(f32[256,128]{1,0:T(8,128)S(1)} %get-tuple-element.68), channel_id=1, source_target_pairs={{0,2},{1,3},{2,0},{3,1},{4,6},{5,7},{6,4},{7,5},{8,10},{9,11},{10,... | collective-permute-start | bytes 393224 | tf_op jit(solution)/shard_map/ppermute | solution.py:433
  41.7 10.6 %collective-permute-start.14 = (f32[256,128]{1,0:T(8,128)S(1)}, f32[256,128]{1,0:T(8,128)S(1)}, u32[]{:S(2)}, u32[]{:S(2)}) collective-permute-start(f32[256,128]{1,0:T(8,128)S(1)} %get-tuple-element.69), channel_id=1, source_target_pairs={{0,4},{1,5},{2,6},{3,7},{4,0},{5,1},{6,2},{7,3},{8,12},{9,13},{10,... | collective-permute-start | bytes 393224 | tf_op jit(solution)/shard_map/ppermute | solution.py:433
  43.1 10.3 %collective-permute-start.15 = (f32[256,128]{1,0:T(8,128)S(1)}, f32[256,128]{1,0:T(8,128)S(1)}, u32[]{:S(2)}, u32[]{:S(2)}) collective-permute-start(f32[256,128]{1,0:T(8,128)S(1)} %get-tuple-element.70), channel_id=1, source_target_pairs={{0,6},{1,7},{2,4},{3,5},{4,2},{5,3},{6,0},{7,1},{8,14},{9,15},{10,... | collective-permute-start | bytes 393224 | tf_op jit(solution)/shard_map/ppermute | solution.py:433
  53.8 3.1 %collective-permute-start.16 = (f32[2560,128]{1,0:T(8,128)S(1)}, f32[2560,128]{1,0:T(8,128)S(1)}, u32[]{:S(2)}, u32[]{:S(2)}) collective-permute-start(f32[2560,128]{1,0:T(8,128)S(1)} %get-tuple-element.72.refs_5_), channel_id=1, source_target_pairs={{0,1},{1,0},{2,3},{3,2},{4,5},{5,4},{6,7},{7,6},{8,9},{9,8},{10,11... | collective-permute-start | bytes 3932168 | tf_op jit(solution)/shard_map/ppermute | solution.py:433
  57.7 8.8 %collective-permute-start.17 = (f32[1920,128]{1,0:T(8,128)S(1)}, f32[1920,128]{1,0:T(8,128)S(1)}, u32[]{:S(2)}, u32[]{:S(2)}) collective-permute-start(f32[1920,128]{1,0:T(8,128)S(1)} %shard_map.88.refs_4_), channel_id=1, source_target_pairs={{0,1},{1,0},{2,3},{3,2},{4,5},{5,4},{6,7},{7,6},{8,9},{9,8},{10,11... | collective-permute-start | bytes 2949128 | tf_op jit(solution)/shard_map/ppermute | solution.py:433
  57.9 7.2 %collective-permute-start.19 = (f32[192,256]{1,0:T(8,128)S(1)}, f32[192,256]{1,0:T(8,128)S(1)}, u32[]{:S(2)}, u32[]{:S(2)}) collective-permute-start(f32[192,256]{1,0:T(8,128)S(1)} %get-tuple-element.75.refs_2_.refs_1_), channel_id=1, source_target_pairs={{0,16},{16,0},{1,17},{17,1},{2,18},{18,2},{3,19},{19,3},{4,20},{20... | collective-permute-start | bytes 589832 | tf_op jit(solution)/shard_map/ppermute | solution.py:436
  59.4 7.4 %collective-permute-start.18 = (f32[192,256]{1,0:T(8,128)S(1)}, f32[192,256]{1,0:T(8,128)S(1)}, u32[]{:S(2)}, u32[]{:S(2)}) collective-permute-start(f32[192,256]{1,0:T(8,128)S(1)} %get-tuple-element.75.refs_2_.refs_1_), channel_id=1, source_target_pairs={{0,1},{1,0},{2,3},{3,2},{4,5},{5,4},{6,7},{7,6},{8,9},{9,8},{10,11... | collective-permute-start | bytes 589832 | tf_op jit(solution)/shard_map/ppermute | solution.py:433
  67.5 6.7 %collective-permute-start.21 = (f32[160,256]{1,0:T(8,128)S(1)}, f32[160,256]{1,0:T(8,128)S(1)}, u32[]{:S(2)}, u32[]{:S(2)}) collective-permute-start(f32[160,256]{1,0:T(8,128)S(1)} %get-tuple-element.79), channel_id=1, source_target_pairs={{0,2},{1,3},{2,0},{3,1},{4,6},{5,7},{6,4},{7,5},{8,10},{9,11},{10,... | collective-permute-start | bytes 491528 | tf_op jit(solution)/shard_map/ppermute | solution.py:433
  69.2 7.0 %collective-permute-start.22 = (f32[160,256]{1,0:T(8,128)S(1)}, f32[160,256]{1,0:T(8,128)S(1)}, u32[]{:S(2)}, u32[]{:S(2)}) collective-permute-start(f32[160,256]{1,0:T(8,128)S(1)} %get-tuple-element.80), channel_id=1, source_target_pairs={{0,4},{1,5},{2,6},{3,7},{4,0},{5,1},{6,2},{7,3},{8,12},{9,13},{10,... | collective-permute-start | bytes 491528 | tf_op jit(solution)/shard_map/ppermute | solution.py:433
  70.6 8.2 %collective-permute-start.23 = (f32[160,256]{1,0:T(8,128)S(1)}, f32[160,256]{1,0:T(8,128)S(1)}, u32[]{:S(2)}, u32[]{:S(2)}) collective-permute-start(f32[160,256]{1,0:T(8,128)S(1)} %get-tuple-element.81), channel_id=1, source_target_pairs={{0,6},{1,7},{2,4},{3,5},{4,2},{5,3},{6,0},{7,1},{8,14},{9,15},{10,... | collective-permute-start | bytes 491528 | tf_op jit(solution)/shard_map/ppermute | solution.py:433
  78.9 6.6 %collective-permute-start.24 = (f32[80,256]{1,0:T(8,128)S(1)}, f32[80,256]{1,0:T(8,128)S(1)}, u32[]{:S(2)}, u32[]{:S(2)}) collective-permute-start(f32[80,256]{1,0:T(8,128)S(1)} %get-tuple-element.83), channel_id=1, source_target_pairs={{0,8},{1,9},{2,10},{3,11},{4,12},{5,13},{6,14},{7,15},{8,0},{9,1},... | collective-permute-start | bytes 245768 | tf_op jit(solution)/shard_map/ppermute | solution.py:433
  (6 other events, 57.8 us)

commit v3 on v2

--- a/solution.py
+++ b/solution.py
@@ -34,9 +34,9 @@
     lane = lax.broadcasted_iota(jnp.int32, (heads, width), 1) // (width // heads)
     row = lax.broadcasted_iota(jnp.int32, (heads, width), 0)
     pattern = jnp.where(lane == row, 1.0, 0.0).astype(bf16)
-    high = small.astype(bf16)
-    low = (small - high.astype(f32)).astype(bf16)
-    return dot(high, pattern) + dot(low, pattern)
+    high = small.astype(bf16).astype(f32)
+    halves = jnp.concatenate([high, small - high], axis=1).astype(bf16)
+    return dot(halves, jnp.concatenate([pattern, pattern], axis=0))
 
 
 def orders(length):
@@ -61,7 +61,7 @@
 
 
 def first_body(
-    place, normed_far, w_far, vals_far, cots_far, rate_far, starts_far, message, keep_f, keep_g, decays, u_out, v_out, bc_out,
+    place, normed_far, w_far, vals_far, cots_far, rate_far, starts_far, message, factors_out, u_out, v_out, bc_out,
     groups, normed, w_bc, vals, cots, rate, starts, small, first, second, third, fourth,
 ):
     heads = rate.shape[0]
@@ -94,39 +94,35 @@
     down = jnp.where(segment == last_segment, jnp.exp(sums[-1:, :] - sums), 0.0)
     up_wide = spread(up, heads, width)
     down_wide = spread(down, heads, width)
-    for copy in waves[0] + waves[1]:
+    for copy in waves[0] + waves[1] + waves[2] + waves[3]:
         copy.wait()
     bc = dot(normed[...], w_bc[...]).astype(bf16)
     bc_out[...] = bc
-    for copy in waves[2]:
-        copy.wait()
     u_out[...] = (up_wide * cots[...].astype(f32)).astype(bf16)
-    for copy in waves[3]:
-        copy.wait()
     v_out[...] = (down_wide * vals[...].astype(f32)).astype(bf16)
-    bmat, cmat = bc[:, :state], bc[:, state:]
-    slot = groups.shape[1]
-    half, part = width // 2, width // 8
+    factors_out[...] = groups[...]
+    half = width // 2
+    end_states(place, 1, u_out, v_out, bc_out, groups, message, message, message, (0, half, 2 * half))
+
+
+def end_states(place, near_set, u_ref, v_ref, bc_ref, factors, into_f, into_g, into_decays, bases):
+    state = bc_ref.shape[1] // 2
+    half, part, slot = u_ref.shape[1] // 2, u_ref.shape[1] // 8, factors.shape[1]
+    which = lax.rem(place[0] + near_set, 2)
+    columns = pl.ds(pl.multiple_of(which * half, half), half)
     quad = quad_of(place)
-    for near_set in (1, 0):
-        which = lax.rem(place[0] + near_set, 2)
-        columns = pl.ds(pl.multiple_of(which * half, half), half)
-        forward = dot(v_out[:, columns], bmat, (0, 0))
-        backward = dot(u_out[:, columns], cmat, (0, 0))
-        for group in range(4):
-            flip = jnp.bitwise_xor(quad, group)
-            rows = slice(group * part, (group + 1) * part)
-            to = pl.ds(pl.multiple_of(flip * part, part), part)
-            behind = pl.ds(pl.multiple_of(half + flip * part, part), part)
-            factors = groups[which * 4 + group]
-            if near_set == 0:
-                keep_f[to, :] = forward[rows]
-                keep_g[to, :] = backward[rows]
-                decays[pl.ds(pl.multiple_of(flip * slot, slot), slot), :] = factors
-            else:
-                message[to, :] = forward[rows]
-                message[behind, :] = backward[rows]
-                message[pl.ds(pl.multiple_of(2 * half + flip * slot, slot), slot), :] = factors
+    forward = dot(v_ref[:, columns], bc_ref[:, :state], (0, 0))
+    backward = dot(u_ref[:, columns], bc_ref[:, state:], (0, 0))
+    for group in range(4):
+        flip = jnp.bitwise_xor(quad, group)
+        rows = slice(group * part, (group + 1) * part)
+        into_f[pl.ds(pl.multiple_of(bases[0] + flip * part, part), part), :] = forward[rows]
+        into_g[pl.ds(pl.multiple_of(bases[1] + flip * part, part), part), :] = backward[rows]
+        into_decays[pl.ds(pl.multiple_of(bases[2] + flip * slot, slot), slot), :] = factors[which * 4 + group]
+
+
+def keep_body(place, u_ref, v_ref, bc_ref, factors, keep_f, keep_g, decays):
+    end_states(place, 0, u_ref, v_ref, bc_ref, factors, keep_f, keep_g, decays, (0, 0, 0))
 
 
 def local_body(place, vals, cots, rate, starts, bc_ref, grad_out, scale_out, dbc_out):
@@ -213,7 +209,7 @@
         out[k * head:(k + 1) * head, :] = pick(upper, total[1], total[0])
 
 
-def quad_body(size, head, last, place, own, one, two, three, out):
+def quad_body(size, head, last, place, own, three, one, two, out):
     second, later = place[1] == 1, level_bit(place, 0)
     upper = None if last is None else level_bit(place, last)
     for k in range(size):
@@ -229,7 +225,7 @@
         store_total(out, joined(mine, theirs, level_bit(place, bit)), size, head, k, upper)
 
 
-def enter_body(size, head, bits, place, own, one, two, three, *refs):
+def enter_body(size, head, bits, place, own, three, one, two, *refs):
     levels, final, outs = refs[:bits - 2], refs[bits - 2], refs[bits - 1:]
     rows = size * head
     second, later = place[1] == 1, level_bit(place, 0)
@@ -255,7 +251,7 @@
             out[after, :] = state_behind
 
 
-def core_body(chunks, head, place, *refs):
+def core_body(chunks, flips, head, place, *refs):
     count = 4 * len(chunks)
     keep_f, keep_g, decays, recv, send, own = refs[count:]
     base = keep_f.shape[0]
@@ -263,7 +259,7 @@
     slot = decays.shape[0] // 4
     second = place[0] == 1
     for number, (start, size) in enumerate(chunks):
-        for flip, ref in enumerate(refs[number * 4:number * 4 + 4]):
+        for flip, ref in zip((0,) + flips[number], refs[number * 4:number * 4 + 4]):
             for k in range(size):
                 at = flip * rows + (start + k) * head
                 spot = flip * slot + start + k
@@ -279,29 +275,27 @@
                 own[to, :] = (pick(second, 1.0, there) * state + pick(second, 0.0, 1.0) * got).astype(bf16)
 
 
-def cross_body(chunks, head, place, u_ref, v_ref, local_ref, *refs):
-    count = len(chunks)
-    mine, theirs = refs[:count], refs[count:2 * count]
-    out, after, before = refs[2 * count:]
-    group = after.shape[0] // 8
-    state = after.shape[1]
+def cross_body(near_set, last, place, u_ref, v_ref, so_far, states, out, after, before):
+    half = after.shape[0]
+    group, width = half // 4, after.shape[1]
     quad = quad_of(place)
-    for near_set, pieces in ((0, mine), (1, theirs)):
-        for (start, size), piece in zip(chunks, pieces):
-            rows = size * head
-            for flip in range(4):
-                which = lax.rem(place[0] + near_set, 2) * 4 + jnp.bitwise_xor(quad, flip)
-                to = pl.ds(pl.multiple_of(which * group + start * head, head), rows)
-                before[to, :] = piece[flip * rows:(flip + 1) * rows, :].astype(bf16)
-                after[to, :] = piece[(4 + flip) * rows:(5 + flip) * rows, :].astype(bf16)
-    out[:, :state] = (local_ref[:, :state] + dot(v_ref[...], after[...])).astype(bf16).astype(f32)
-    out[:, state:] = (local_ref[:, state:] + dot(u_ref[...], before[...])).astype(bf16).astype(f32)
-
-
-def values_body(place, grad_ref, scale_ref, bc_ref, after, grad_out, done):
+    for flip in range(4):
+        to = pl.ds(pl.multiple_of(jnp.bitwise_xor(quad, flip) * group, group), group)
+        before[to, :] = states[flip * group:(flip + 1) * group, :].astype(bf16)
+        after[to, :] = states[half + flip * group:half + (flip + 1) * group, :].astype(bf16)
+    columns = pl.ds(pl.multiple_of(lax.rem(place[0] + near_set, 2) * half, half), half)
+    for ref, weights, lanes in ((after, v_ref, slice(0, width)), (before, u_ref, slice(width, 2 * width))):
+        total = so_far[:, lanes] + dot(weights[:, columns], ref[...])
+        out[:, lanes] = total.astype(bf16).astype(f32) if last else total
+
+
+def values_body(place, grad_ref, scale_ref, bc_ref, mine, theirs, grad_out, done):
     done[...] = jnp.zeros_like(done)
-    bmat = bc_ref[:, : after.shape[1]]
-    grad_out[...] = (grad_ref[...] + scale_ref[...] * dot(bmat, after[...], (1, 1))).astype(bf16)
+    half = mine.shape[0]
+    bmat = bc_ref[:, : mine.shape[1]]
+    for near_set, after in ((0, mine), (1, theirs)):
+        columns = pl.ds(pl.multiple_of(lax.rem(place[0] + near_set, 2) * half, half), half)
+        grad_out[:, columns] = (grad_ref[:, columns] + scale_ref[:, columns] * dot(bmat, after[...], (1, 1))).astype(bf16)
 
 
 def block_row(quarter, position, levels, rows):
@@ -438,10 +432,10 @@
     def swap_both(array):
         return lax.ppermute(array, ("dp", "seq"), [(d * shards + s, (d ^ 1) * shards + (s ^ 1)) for d in range(packs) for s in range(shards)])
 
-    message, keep_f, keep_g, decays, u, v, bc = kernel(
+    message, factors, u, v, bc = kernel(
         first_body,
         (
-            shape(2 * base + 4 * slot, state), shape(base, state), shape(base, state), shape(4 * slot, state),
+            shape(2 * base + 4 * slot, state), jax.ShapeDtypeStruct((8, slot, LANES), f32),
             shape(length, width, bf16), shape(length, width, bf16), shape(length, 2 * state, bf16),
         ),
         normed, w_bc, values, cotangent, rate_index, starts,
@@ -453,6 +447,9 @@
         vmem=24, far=True,
     )
     recv = swap(message, 1)
+    keep_f, keep_g, decays = kernel(
+        keep_body, (shape(base, state), shape(base, state), shape(4 * slot, state)), u, v, bc, factors, vmem=16,
+    )
 
     direct = packs == 2 and depth % (packs * shards * 16) == 0 and length == 3 * LANES // 2
     rows = depth // (packs * shards)
@@ -472,12 +469,17 @@
     def parcel(size):
         return shape(2 * size * head + padded(size), state)
 
-    def to_quad(arrays):
-        return [swap(array, flip * 2) for flip, array in enumerate(arrays, 1)]
+    def to_quad(arrays, flips=(3, 1, 2)):
+        return [swap(arrays[flip - 1], flip * 2) for flip in flips]
 
     quads = []
     for start, size in chunks:
         waits = quads[-1][1:2] if quads else ()
+        if quads:
+            grad_local, scale, dbc_local = kernel(
+                local_body, (shape(length, width), shape(length, width), shape(length, 2 * state)),
+                vals, cots, rate, starts, bc, vmem=24,
+            )
         own, *sends = kernel(bind(chip_body, start, size, head), (parcel(size),) * 4, keep_f, keep_g, decays, recv, behind=waits)
         quads.append([own] + to_quad(sends))
 
@@ -493,25 +495,26 @@
             out = parcel(size) if last is None else shape(size * head, state)
             totals[number] = kernel(bind(join_body, size, head, bit, last), out, totals[number], arrived[number][-1])
             arrived[number].append(swap(totals[number], 8 << bit))
-    grad_local, scale, dbc_local = kernel(
-        local_body, (shape(length, width), shape(length, width), shape(length, 2 * state)),
-        vals, cots, rate, starts, bc, vmem=24,
-    )
-    states = []
+    states, orders_of = [], []
     for number, ((start, size), group, steps) in enumerate(zip(chunks, quads, arrived)):
-        waits = states[1:2] if states else ([pack_turned] if direct else [])
+        waits = states[1:2] + ([pack_turned] if direct else []) if states else []
         enter, *sends = kernel(
             bind(enter_body, size, head, bits), (shape(2 * size * head, state),) * 4, *group, *steps, behind=waits,
         )
-        states += [enter] + to_quad(sends)
+        orders_of.append((1, 3, 2) if number == 0 else (3, 1, 2))
+        states += [enter] + to_quad(sends, orders_of[-1])
     send, final = kernel(
-        bind(core_body, chunks, head), (shape(2 * base, state), shape(2 * base, state, bf16)), *states, keep_f, keep_g, decays, recv,
+        bind(core_body, chunks, orders_of, head), (shape(2 * base, state), shape(2 * base, state, bf16)), *states, keep_f, keep_g, decays, recv,
     )
     core_recv = swap(send, 1)
-    dbc, after = kernel(
-        bind(cross_body, ((0, eighth),), head), (shape(length, 2 * state), shape(width, state, bf16)),
-        u, v, dbc_local, final, core_recv, scratch=[pltpu.VMEM((width, state), bf16)], vmem=16,
-    )
+    dbc = dbc_local
+    afters = []
+    for near_set, pieces in ((0, final), (1, core_recv)):
+        dbc, after = kernel(
+            bind(cross_body, near_set, near_set == 1), (shape(length, 2 * state), shape(base, state, bf16)),
+            u, v, dbc, pieces, scratch=[pltpu.VMEM((base, state), bf16)], vmem=16,
+        )
+        afters.append(after)
     portion = 1.0 / (packs * shards * length)
     if direct:
         from_pack = swap_pack(dbc)
@@ -519,7 +522,7 @@
         from_both = swap(from_pack, 1)
         beside = swap(kernel(stack_body, shape(2 * wide, LANES), core_turned, pack_turned, vmem=8), 1)
     grad_values, unused_done = kernel(
-        values_body, (shape(length, width, bf16), shape(8, LANES)), grad_local, scale, bc, after, vmem=16,
+        values_body, (shape(length, width, bf16), shape(8, LANES)), grad_local, scale, bc, *afters, vmem=16,
     )
     if not direct:
         product = lax.dot_general(hidden, dbc.astype(bf16), (((0,), (0,)), ((), ())), preferred_element_type=f32)

time: 86.3 us -> 85.5 us (level)
  waiting for transfers between devices: 41.3 us -> 37.2 us
  starting transfers between devices: 30.6 us -> 34.2 us
    ppermute x23, waiting for transfers between devices: 35.7 us -> 30.6 us  [swap(): return lax.ppermute(array, 'seq', [(s, s ^ mask) for s in range(shards)])]
    ppermute x23, starting transfers between devices: 26.5 us -> 30.7 us  [swap(): return lax.ppermute(array, 'seq', [(s, s ^ mask) for s in range(shards)])]
    ppermute x2, waiting for transfers between devices: 5.58 us -> 6.64 us  [swap_pack(): return lax.ppermute(array, 'dp', [(d, d ^ 1) for d in range(packs)])]
    pallas_call x16 -> x18, Pallas kernels: 12.8 us -> 12.4 us  [kernel(): pl.pallas_call(run, in_specs=[there] * count + [pl.BlockSpec(memory_space...]
  transfers between devices with their start and end apart: 25 -> 25, of which waited for: 15 -> 13; matrix products, arithmetic and copies ran while one was open for 0% -> 0% of each run, Pallas kernels for 6% -> 7%
where the time goes in v3:
time: 85.5 us; the launch traced here: 85.4 us
  waiting for transfers between devices  37.2 us (44%)
  starting transfers between devices  34.2 us (40%)
  Pallas kernels  12.4 us (15%)
    ppermute x23, starting transfers between devices, swap(): return lax.ppermute(array, 'seq', [(s, s ^ mask) for s in range(shards)])  30.7 us
    ppermute x23, waiting for transfers between devices, swap(): return lax.ppermute(array, 'seq', [(s, s ^ mask) for s in range(shards)])  30.6 us
    pallas_call x18, Pallas kernels, kernel(): pl.pallas_call(run, in_specs=[there] * count + [pl.BlockSpec(memory_space...  12.4 us
    ppermute x2, waiting for transfers between devices, swap_pack(): return lax.ppermute(array, 'dp', [(d, d ^ 1) for d in range(packs)])  6.64 us
    ppermute x2, starting transfers between devices, swap_pack(): return lax.ppermute(array, 'dp', [(d, d ^ 1) for d in range(packs)])  3.5 us
  transfers between devices with their start and end apart: 25, of which 13 were waited for; matrix products, arithmetic and copies ran while one was open for 0% of the time, Pallas kernels for 7%

profile of v3, /device:TPU:0, one launch (start us, length us, event | category | flops | bytes accessed | tf_op | source)
XLA Modules:
  0.0 85.4 jit_solution(9930754707016793277)
XLA Ops:
  0.6 4.8 %shard_map.77 = (f32[2592,128]{1,0:T(8,128)S(1)}, f32[8,8,128]{2,1,0:T(8,128)S(1)}, bf16[192,2560]{1,0:T(8,128)(2,1)S(1)}, bf16[192,2560]{1,0:T(8,128)(2,1)S(1)}, bf16[192,256]{1,0:T(8,128)(2,1)S(1)}) custom-call(bf16[1,192,2560]{2,1,0:T(8,128)(2,1)} %refs_0_.1, bf16[2560,256]{1,0:T(8,128)(2,1)} %refs_1_.1, bf16[1,192,2560]{2,1,0:T(8,128)(2,1)} %refs_2_.1, ...), custom_call_target="tpu_custom_call" | custom-call | flops 1000 | bytes 1000 | tf_op jit(solution)/shard_map/pallas_call | solution.py:411
  7.3 3.0 %collective-permute-start.12 = (f32[1920,128]{1,0:T(8,128)S(1)}, f32[1920,128]{1,0:T(8,128)S(1)}, u32[]{:S(2)}, u32[]{:S(2)}) collective-permute-start(f32[1920,128]{1,0:T(8,128)S(1)} %get-tuple-element.70), channel_id=1, source_target_pairs={{0,16},{16,0},{1,17},{17,1},{2,18},{18,2},{3,19},{19,3},{4,20},{20... | collective-permute-start | bytes 2949128 | tf_op jit(solution)/shard_map/ppermute | solution.py:430
  10.4 2.6 %collective-permute-start.1 = (f32[392,128]{1,0:T(8,128)S(1)}, f32[392,128]{1,0:T(8,128)S(1)}, u32[]{:S(2)}, u32[]{:S(2)}) collective-permute-start(f32[392,128]{1,0:T(8,128)S(1)} %get-tuple-element.59), channel_id=1, source_target_pairs={{0,6},{1,7},{2,4},{3,5},{4,2},{5,3},{6,0},{7,1},{8,14},{9,15},{10,... | collective-permute-start | bytes 602120 | tf_op jit(solution)/shard_map/ppermute | solution.py:427
  14.0 2.1 %shard_map.81 = (f32[192,2560]{1,0:T(8,128)S(1)}, f32[192,2560]{1,0:T(8,128)S(1)}, f32[192,256]{1,0:T(8,128)S(1)}) custom-call(bf16[192,2560]{1,0:T(8,128)(2,1)S(1)} %bitcast.6, bf16[192,2560]{1,0:T(8,128)(2,1)S(1)} %bitcast.7, s32[40,192]{1,0:T(8,128)S(1)} %bitcast.8, s32[1,192]{1,0:T(1,128)S(1)} %copy-done.4, ...), custom_call_target="tpu_custom_call" | custom-call | flops 1000 | bytes 1000 | tf_op jit(solution)/shard_map/pallas_call | solution.py:411
  16.1 3.2 %collective-permute-done.1.refs_5_.refs_1_ = f32[392,128]{1,0:T(8,128)S(1)} collective-permute-done((f32[392,128]{1,0:T(8,128)S(1)}, f32[392,128]{1,0:T(8,128)S(1)}, u32[]{:S(2)}, u32[]{:S(2)}) %collective-permute-start.1) | collective-permute-done | bytes 200736 | tf_op jit(solution)/shard_map/ppermute | solution.py:427
  19.4 2.6 %collective-permute-start.5 = (f32[264,128]{1,0:T(8,128)S(1)}, f32[264,128]{1,0:T(8,128)S(1)}, u32[]{:S(2)}, u32[]{:S(2)}) collective-permute-start(f32[264,128]{1,0:T(8,128)S(1)} %get-tuple-element.63), channel_id=1, source_target_pairs={{0,6},{1,7},{2,4},{3,5},{4,2},{5,3},{6,0},{7,1},{8,14},{9,15},{10,... | collective-permute-start | bytes 405512 | tf_op jit(solution)/shard_map/ppermute | solution.py:427
  23.7 1.6 %collective-permute-start.7 = (f32[264,128]{1,0:T(8,128)S(1)}, f32[264,128]{1,0:T(8,128)S(1)}, u32[]{:S(2)}, u32[]{:S(2)}) collective-permute-start(f32[264,128]{1,0:T(8,128)S(1)} %get-tuple-element.65), channel_id=1, source_target_pairs={{0,4},{1,5},{2,6},{3,7},{4,0},{5,1},{6,2},{7,3},{8,12},{9,13},{10,... | collective-permute-start | bytes 405512 | tf_op jit(solution)/shard_map/ppermute | solution.py:427
  25.4 2.7 %collective-permute-start.4 = (f32[192,128]{1,0:T(8,128)S(1)}, f32[192,128]{1,0:T(8,128)S(1)}, u32[]{:S(2)}, u32[]{:S(2)}) collective-permute-start(f32[192,128]{1,0:T(8,128)S(1)} %shard_map.83.refs_4_), channel_id=1, source_target_pairs={{0,8},{1,9},{2,10},{3,11},{4,12},{5,13},{6,14},{7,15},{8,0},{9,1},... | collective-permute-start | bytes 294920 | tf_op jit(solution)/shard_map/ppermute | solution.py:427
  28.1 2.1 %collective-permute-done.7.refs_3_ = f32[264,128]{1,0:T(8,128)S(1)} collective-permute-done((f32[264,128]{1,0:T(8,128)S(1)}, f32[264,128]{1,0:T(8,128)S(1)}, u32[]{:S(2)}, u32[]{:S(2)}) %collective-permute-start.7) | collective-permute-done | bytes 135200 | tf_op jit(solution)/shard_map/ppermute | solution.py:427
  30.3 1.7 %collective-permute-done.4.refs_4_ = f32[192,128]{1,0:T(8,128)S(1)} collective-permute-done((f32[192,128]{1,0:T(8,128)S(1)}, f32[192,128]{1,0:T(8,128)S(1)}, u32[]{:S(2)}, u32[]{:S(2)}) %collective-permute-start.4) | collective-permute-done | bytes 98336 | tf_op jit(solution)/shard_map/ppermute | solution.py:427
  32.1 3.4 %collective-permute-start.8 = (f32[384,128]{1,0:T(8,128)S(1)}, f32[384,128]{1,0:T(8,128)S(1)}, u32[]{:S(2)}, u32[]{:S(2)}) collective-permute-start(f32[384,128]{1,0:T(8,128)S(1)} %get-tuple-element.67), channel_id=1, source_target_pairs={{0,2},{1,3},{2,0},{3,1},{4,6},{5,7},{6,4},{7,5},{8,10},{9,11},{10,... | collective-permute-start | bytes 589832 | tf_op jit(solution)/shard_map/ppermute | solution.py:427
  35.5 1.5 %collective-permute-start.11 = (f32[128,128]{1,0:T(8,128)S(1)}, f32[128,128]{1,0:T(8,128)S(1)}, u32[]{:S(2)}, u32[]{:S(2)}) collective-permute-start(f32[128,128]{1,0:T(8,128)S(1)} %shard_map.84.refs_5_), channel_id=1, source_target_pairs={{0,8},{1,9},{2,10},{3,11},{4,12},{5,13},{6,14},{7,15},{8,0},{9,1},... | collective-permute-start | bytes 196616 | tf_op jit(solution)/shard_map/ppermute | solution.py:427
  38.6 2.6 %collective-permute-done.11.refs_4_ = f32[128,128]{1,0:T(8,128)S(1)} collective-permute-done((f32[128,128]{1,0:T(8,128)S(1)}, f32[128,128]{1,0:T(8,128)S(1)}, u32[]{:S(2)}, u32[]{:S(2)}) %collective-permute-start.11) | collective-permute-done | bytes 65568 | tf_op jit(solution)/shard_map/ppermute | solution.py:427
  41.4 5.3 %collective-permute-start.13 = (f32[256,128]{1,0:T(8,128)S(1)}, f32[256,128]{1,0:T(8,128)S(1)}, u32[]{:S(2)}, u32[]{:S(2)}) collective-permute-start(f32[256,128]{1,0:T(8,128)S(1)} %get-tuple-element.72), channel_id=1, source_target_pairs={{0,6},{1,7},{2,4},{3,5},{4,2},{5,3},{6,0},{7,1},{8,14},{9,15},{10,... | collective-permute-start | bytes 393224 | tf_op jit(solution)/shard_map/ppermute | solution.py:427
  46.7 1.6 %collective-permute-start.14 = (f32[256,128]{1,0:T(8,128)S(1)}, f32[256,128]{1,0:T(8,128)S(1)}, u32[]{:S(2)}, u32[]{:S(2)}) collective-permute-start(f32[256,128]{1,0:T(8,128)S(1)} %get-tuple-element.73), channel_id=1, source_target_pairs={{0,2},{1,3},{2,0},{3,1},{4,6},{5,7},{6,4},{7,5},{8,10},{9,11},{10,... | collective-permute-start | bytes 393224 | tf_op jit(solution)/shard_map/ppermute | solution.py:427
  49.6 2.0 %collective-permute-done.14.refs_6_ = f32[256,128]{1,0:T(8,128)S(1)} collective-permute-done((f32[256,128]{1,0:T(8,128)S(1)}, f32[256,128]{1,0:T(8,128)S(1)}, u32[]{:S(2)}, u32[]{:S(2)}) %collective-permute-start.14) | collective-permute-done | bytes 131104 | tf_op jit(solution)/shard_map/ppermute | solution.py:427
  51.7 1.6 %collective-permute-done.15.refs_7_ = f32[256,128]{1,0:T(8,128)S(1)} collective-permute-done((f32[256,128]{1,0:T(8,128)S(1)}, f32[256,128]{1,0:T(8,128)S(1)}, u32[]{:S(2)}, u32[]{:S(2)}) %collective-permute-start.15) | collective-permute-done | bytes 131104 | tf_op jit(solution)/shard_map/ppermute | solution.py:427
  54.1 2.6 %collective-permute-done.16.refs_3_ = f32[2560,128]{1,0:T(8,128)S(1)} collective-permute-done((f32[2560,128]{1,0:T(8,128)S(1)}, f32[2560,128]{1,0:T(8,128)S(1)}, u32[]{:S(2)}, u32[]{:S(2)}) %collective-permute-start.16) | collective-permute-done | bytes 1310752 | tf_op jit(solution)/shard_map/ppermute | solution.py:427
  58.0 6.6 %collective-permute-done.19.refs_3_ = f32[192,256]{1,0:T(8,128)S(1)} collective-permute-done((f32[192,256]{1,0:T(8,128)S(1)}, f32[192,256]{1,0:T(8,128)S(1)}, u32[]{:S(2)}, u32[]{:S(2)}) %collective-permute-start.19) | collective-permute-done | bytes 196640 | tf_op jit(solution)/shard_map/ppermute | solution.py:430
  68.7 1.9 %collective-permute-start.23 = (f32[160,256]{1,0:T(8,128)S(1)}, f32[160,256]{1,0:T(8,128)S(1)}, u32[]{:S(2)}, u32[]{:S(2)}) collective-permute-start(f32[160,256]{1,0:T(8,128)S(1)} %get-tuple-element.87), channel_id=1, source_target_pairs={{0,4},{1,5},{2,6},{3,7},{4,0},{5,1},{6,2},{7,3},{8,12},{9,13},{10,... | collective-permute-start | bytes 491528 | tf_op jit(solution)/shard_map/ppermute | solution.py:427
  70.5 4.5 %collective-permute-done.21.refs_1_ = f32[160,256]{1,0:T(8,128)S(1)} collective-permute-done((f32[160,256]{1,0:T(8,128)S(1)}, f32[160,256]{1,0:T(8,128)S(1)}, u32[]{:S(2)}, u32[]{:S(2)}) %collective-permute-start.21) | collective-permute-done | bytes 163872 | tf_op jit(solution)/shard_map/ppermute | solution.py:427
  75.0 2.8 %collective-permute-done.22.refs_2_ = f32[160,256]{1,0:T(8,128)S(1)} collective-permute-done((f32[160,256]{1,0:T(8,128)S(1)}, f32[160,256]{1,0:T(8,128)S(1)}, u32[]{:S(2)}, u32[]{:S(2)}) %collective-permute-start.22) | collective-permute-done | bytes 163872 | tf_op jit(solution)/shard_map/ppermute | solution.py:427
  77.9 2.0 %collective-permute-start.24 = (f32[80,256]{1,0:T(8,128)S(1)}, f32[80,256]{1,0:T(8,128)S(1)}, u32[]{:S(2)}, u32[]{:S(2)}) collective-permute-start(f32[80,256]{1,0:T(8,128)S(1)} %get-tuple-element.89), channel_id=1, source_target_pairs={{0,8},{1,9},{2,10},{3,11},{4,12},{5,13},{6,14},{7,15},{8,0},{9,1},... | collective-permute-start | bytes 245768 | tf_op jit(solution)/shard_map/ppermute | solution.py:427
  79.8 4.9 %collective-permute-done.24 = f32[80,256]{1,0:T(8,128)S(1)} collective-permute-done((f32[80,256]{1,0:T(8,128)S(1)}, f32[80,256]{1,0:T(8,128)S(1)}, u32[]{:S(2)}, u32[]{:S(2)}) %collective-permute-start.24) | collective-permute-done | bytes 81952 | tf_op jit(solution)/shard_map/ppermute | solution.py:427
  (55 shorter events, 15.1 us)
Async XLA Ops:
  5.4 4.9 %collective-permute-start = (f32[2592,128]{1,0:T(8,128)S(1)}, f32[2592,128]{1,0:T(8,128)S(1)}, u32[]{:S(2)}, u32[]{:S(2)}) collective-permute-start(f32[2592,128]{1,0:T(8,128)S(1)} %get-tuple-element.53), channel_id=1, source_target_pairs={{0,1},{1,0},{2,3},{3,2},{4,5},{5,4},{6,7},{7,6},{8,9},{9,8},{10,11... | collective-permute-start | bytes 3981320 | tf_op jit(solution)/shard_map/ppermute | solution.py:427
  7.3 31.3 %collective-permute-start.12 = (f32[1920,128]{1,0:T(8,128)S(1)}, f32[1920,128]{1,0:T(8,128)S(1)}, u32[]{:S(2)}, u32[]{:S(2)}) collective-permute-start(f32[1920,128]{1,0:T(8,128)S(1)} %get-tuple-element.70), channel_id=1, source_target_pairs={{0,16},{16,0},{1,17},{17,1},{2,18},{18,2},{3,19},{19,3},{4,20},{20... | collective-permute-start | bytes 2949128 | tf_op jit(solution)/shard_map/ppermute | solution.py:430
  10.4 8.9 %collective-permute-start.1 = (f32[392,128]{1,0:T(8,128)S(1)}, f32[392,128]{1,0:T(8,128)S(1)}, u32[]{:S(2)}, u32[]{:S(2)}) collective-permute-start(f32[392,128]{1,0:T(8,128)S(1)} %get-tuple-element.59), channel_id=1, source_target_pairs={{0,6},{1,7},{2,4},{3,5},{4,2},{5,3},{6,0},{7,1},{8,14},{9,15},{10,... | collective-permute-start | bytes 602120 | tf_op jit(solution)/shard_map/ppermute | solution.py:427
  13.0 10.7 %collective-permute-start.2 = (f32[392,128]{1,0:T(8,128)S(1)}, f32[392,128]{1,0:T(8,128)S(1)}, u32[]{:S(2)}, u32[]{:S(2)}) collective-permute-start(f32[392,128]{1,0:T(8,128)S(1)} %get-tuple-element.60), channel_id=1, source_target_pairs={{0,2},{1,3},{2,0},{3,1},{4,6},{5,7},{6,4},{7,5},{8,10},{9,11},{10,... | collective-permute-start | bytes 602120 | tf_op jit(solution)/shard_map/ppermute | solution.py:427
  13.5 11.7 %collective-permute-start.3 = (f32[392,128]{1,0:T(8,128)S(1)}, f32[392,128]{1,0:T(8,128)S(1)}, u32[]{:S(2)}, u32[]{:S(2)}) collective-permute-start(f32[392,128]{1,0:T(8,128)S(1)} %get-tuple-element.61), channel_id=1, source_target_pairs={{0,4},{1,5},{2,6},{3,7},{4,0},{5,1},{6,2},{7,3},{8,12},{9,13},{10,... | collective-permute-start | bytes 602120 | tf_op jit(solution)/shard_map/ppermute | solution.py:427
  19.4 8.7 %collective-permute-start.5 = (f32[264,128]{1,0:T(8,128)S(1)}, f32[264,128]{1,0:T(8,128)S(1)}, u32[]{:S(2)}, u32[]{:S(2)}) collective-permute-start(f32[264,128]{1,0:T(8,128)S(1)} %get-tuple-element.63), channel_id=1, source_target_pairs={{0,6},{1,7},{2,4},{3,5},{4,2},{5,3},{6,0},{7,1},{8,14},{9,15},{10,... | collective-permute-start | bytes 405512 | tf_op jit(solution)/shard_map/ppermute | solution.py:427
  21.9 6.1 %collective-permute-start.6 = (f32[264,128]{1,0:T(8,128)S(1)}, f32[264,128]{1,0:T(8,128)S(1)}, u32[]{:S(2)}, u32[]{:S(2)}) collective-permute-start(f32[264,128]{1,0:T(8,128)S(1)} %get-tuple-element.64), channel_id=1, source_target_pairs={{0,2},{1,3},{2,0},{3,1},{4,6},{5,7},{6,4},{7,5},{8,10},{9,11},{10,... | collective-permute-start | bytes 405512 | tf_op jit(solution)/shard_map/ppermute | solution.py:427
  23.7 6.5 %collective-permute-start.7 = (f32[264,128]{1,0:T(8,128)S(1)}, f32[264,128]{1,0:T(8,128)S(1)}, u32[]{:S(2)}, u32[]{:S(2)}) collective-permute-start(f32[264,128]{1,0:T(8,128)S(1)} %get-tuple-element.65), channel_id=1, source_target_pairs={{0,4},{1,5},{2,6},{3,7},{4,0},{5,1},{6,2},{7,3},{8,12},{9,13},{10,... | collective-permute-start | bytes 405512 | tf_op jit(solution)/shard_map/ppermute | solution.py:427
  25.4 6.6 %collective-permute-start.4 = (f32[192,128]{1,0:T(8,128)S(1)}, f32[192,128]{1,0:T(8,128)S(1)}, u32[]{:S(2)}, u32[]{:S(2)}) collective-permute-start(f32[192,128]{1,0:T(8,128)S(1)} %shard_map.83.refs_4_), channel_id=1, source_target_pairs={{0,8},{1,9},{2,10},{3,11},{4,12},{5,13},{6,14},{7,15},{8,0},{9,1},... | collective-permute-start | bytes 294920 | tf_op jit(solution)/shard_map/ppermute | solution.py:427
  32.1 9.1 %collective-permute-start.8 = (f32[384,128]{1,0:T(8,128)S(1)}, f32[384,128]{1,0:T(8,128)S(1)}, u32[]{:S(2)}, u32[]{:S(2)}) collective-permute-start(f32[384,128]{1,0:T(8,128)S(1)} %get-tuple-element.67), channel_id=1, source_target_pairs={{0,2},{1,3},{2,0},{3,1},{4,6},{5,7},{6,4},{7,5},{8,10},{9,11},{10,... | collective-permute-start | bytes 589832 | tf_op jit(solution)/shard_map/ppermute | solution.py:427
  35.5 5.7 %collective-permute-start.11 = (f32[128,128]{1,0:T(8,128)S(1)}, f32[128,128]{1,0:T(8,128)S(1)}, u32[]{:S(2)}, u32[]{:S(2)}) collective-permute-start(f32[128,128]{1,0:T(8,128)S(1)} %shard_map.84.refs_5_), channel_id=1, source_target_pairs={{0,8},{1,9},{2,10},{3,11},{4,12},{5,13},{6,14},{7,15},{8,0},{9,1},... | collective-permute-start | bytes 196616 | tf_op jit(solution)/shard_map/ppermute | solution.py:427
  37.1 11.2 %collective-permute-start.9 = (f32[384,128]{1,0:T(8,128)S(1)}, f32[384,128]{1,0:T(8,128)S(1)}, u32[]{:S(2)}, u32[]{:S(2)}) collective-permute-start(f32[384,128]{1,0:T(8,128)S(1)} %get-tuple-element.68), channel_id=1, source_target_pairs={{0,6},{1,7},{2,4},{3,5},{4,2},{5,3},{6,0},{7,1},{8,14},{9,15},{10,... | collective-permute-start | bytes 589832 | tf_op jit(solution)/shard_map/ppermute | solution.py:427
  37.6 10.7 %collective-permute-start.10 = (f32[384,128]{1,0:T(8,128)S(1)}, f32[384,128]{1,0:T(8,128)S(1)}, u32[]{:S(2)}, u32[]{:S(2)}) collective-permute-start(f32[384,128]{1,0:T(8,128)S(1)} %get-tuple-element.69), channel_id=1, source_target_pairs={{0,4},{1,5},{2,6},{3,7},{4,0},{5,1},{6,2},{7,3},{8,12},{9,13},{10,... | collective-permute-start | bytes 589832 | tf_op jit(solution)/shard_map/ppermute | solution.py:427
  41.4 8.2 %collective-permute-start.13 = (f32[256,128]{1,0:T(8,128)S(1)}, f32[256,128]{1,0:T(8,128)S(1)}, u32[]{:S(2)}, u32[]{:S(2)}) collective-permute-start(f32[256,128]{1,0:T(8,128)S(1)} %get-tuple-element.72), channel_id=1, source_target_pairs={{0,6},{1,7},{2,4},{3,5},{4,2},{5,3},{6,0},{7,1},{8,14},{9,15},{10,... | collective-permute-start | bytes 393224 | tf_op jit(solution)/shard_map/ppermute | solution.py:427
  46.7 5.0 %collective-permute-start.14 = (f32[256,128]{1,0:T(8,128)S(1)}, f32[256,128]{1,0:T(8,128)S(1)}, u32[]{:S(2)}, u32[]{:S(2)}) collective-permute-start(f32[256,128]{1,0:T(8,128)S(1)} %get-tuple-element.73), channel_id=1, source_target_pairs={{0,2},{1,3},{2,0},{3,1},{4,6},{5,7},{6,4},{7,5},{8,10},{9,11},{10,... | collective-permute-start | bytes 393224 | tf_op jit(solution)/shard_map/ppermute | solution.py:427
  48.3 5.0 %collective-permute-start.15 = (f32[256,128]{1,0:T(8,128)S(1)}, f32[256,128]{1,0:T(8,128)S(1)}, u32[]{:S(2)}, u32[]{:S(2)}) collective-permute-start(f32[256,128]{1,0:T(8,128)S(1)} %get-tuple-element.74), channel_id=1, source_target_pairs={{0,4},{1,5},{2,6},{3,7},{4,0},{5,1},{6,2},{7,3},{8,12},{9,13},{10,... | collective-permute-start | bytes 393224 | tf_op jit(solution)/shard_map/ppermute | solution.py:427
  53.6 3.1 %collective-permute-start.16 = (f32[2560,128]{1,0:T(8,128)S(1)}, f32[2560,128]{1,0:T(8,128)S(1)}, u32[]{:S(2)}, u32[]{:S(2)}) collective-permute-start(f32[2560,128]{1,0:T(8,128)S(1)} %get-tuple-element.76.refs_4_), channel_id=1, source_target_pairs={{0,1},{1,0},{2,3},{3,2},{4,5},{5,4},{6,7},{7,6},{8,9},{9,8},{10,11... | collective-permute-start | bytes 3932168 | tf_op jit(solution)/shard_map/ppermute | solution.py:427
  57.2 8.8 %collective-permute-start.17 = (f32[1920,128]{1,0:T(8,128)S(1)}, f32[1920,128]{1,0:T(8,128)S(1)}, u32[]{:S(2)}, u32[]{:S(2)}) collective-permute-start(f32[1920,128]{1,0:T(8,128)S(1)} %shard_map.90.refs_5_), channel_id=1, source_target_pairs={{0,1},{1,0},{2,3},{3,2},{4,5},{5,4},{6,7},{7,6},{8,9},{9,8},{10,11... | collective-permute-start | bytes 2949128 | tf_op jit(solution)/shard_map/ppermute | solution.py:427
  57.4 7.2 %collective-permute-start.19 = (f32[192,256]{1,0:T(8,128)S(1)}, f32[192,256]{1,0:T(8,128)S(1)}, u32[]{:S(2)}, u32[]{:S(2)}) collective-permute-start(f32[192,256]{1,0:T(8,128)S(1)} %get-tuple-element.81.refs_2_.refs_1_), channel_id=1, source_target_pairs={{0,16},{16,0},{1,17},{17,1},{2,18},{18,2},{3,19},{19,3},{4,20},{20... | collective-permute-start | bytes 589832 | tf_op jit(solution)/shard_map/ppermute | solution.py:430
  57.9 8.5 %collective-permute-start.18 = (f32[192,256]{1,0:T(8,128)S(1)}, f32[192,256]{1,0:T(8,128)S(1)}, u32[]{:S(2)}, u32[]{:S(2)}) collective-permute-start(f32[192,256]{1,0:T(8,128)S(1)} %get-tuple-element.81.refs_2_.refs_1_), channel_id=1, source_target_pairs={{0,1},{1,0},{2,3},{3,2},{4,5},{5,4},{6,7},{7,6},{8,9},{9,8},{10,11... | collective-permute-start | bytes 589832 | tf_op jit(solution)/shard_map/ppermute | solution.py:427
  67.0 8.0 %collective-permute-start.21 = (f32[160,256]{1,0:T(8,128)S(1)}, f32[160,256]{1,0:T(8,128)S(1)}, u32[]{:S(2)}, u32[]{:S(2)}) collective-permute-start(f32[160,256]{1,0:T(8,128)S(1)} %get-tuple-element.85), channel_id=1, source_target_pairs={{0,6},{1,7},{2,4},{3,5},{4,2},{5,3},{6,0},{7,1},{8,14},{9,15},{10,... | collective-permute-start | bytes 491528 | tf_op jit(solution)/shard_map/ppermute | solution.py:427
  68.0 9.9 %collective-permute-start.22 = (f32[160,256]{1,0:T(8,128)S(1)}, f32[160,256]{1,0:T(8,128)S(1)}, u32[]{:S(2)}, u32[]{:S(2)}) collective-permute-start(f32[160,256]{1,0:T(8,128)S(1)} %get-tuple-element.86), channel_id=1, source_target_pairs={{0,2},{1,3},{2,0},{3,1},{4,6},{5,7},{6,4},{7,5},{8,10},{9,11},{10,... | collective-permute-start | bytes 491528 | tf_op jit(solution)/shard_map/ppermute | solution.py:427
  68.7 9.1 %collective-permute-start.23 = (f32[160,256]{1,0:T(8,128)S(1)}, f32[160,256]{1,0:T(8,128)S(1)}, u32[]{:S(2)}, u32[]{:S(2)}) collective-permute-start(f32[160,256]{1,0:T(8,128)S(1)} %get-tuple-element.87), channel_id=1, source_target_pairs={{0,4},{1,5},{2,6},{3,7},{4,0},{5,1},{6,2},{7,3},{8,12},{9,13},{10,... | collective-permute-start | bytes 491528 | tf_op jit(solution)/shard_map/ppermute | solution.py:427
  77.9 6.9 %collective-permute-start.24 = (f32[80,256]{1,0:T(8,128)S(1)}, f32[80,256]{1,0:T(8,128)S(1)}, u32[]{:S(2)}, u32[]{:S(2)}) collective-permute-start(f32[80,256]{1,0:T(8,128)S(1)} %get-tuple-element.89), channel_id=1, source_target_pairs={{0,8},{1,9},{2,10},{3,11},{4,12},{5,13},{6,14},{7,15},{8,0},{9,1},... | collective-permute-start | bytes 245768 | tf_op jit(solution)/shard_map/ppermute | solution.py:427
  (6 other events, 17.8 us)

commit v4 on v3

--- a/solution.py
+++ b/solution.py
@@ -30,12 +30,16 @@
     return -(-rows // 8) * 8
 
 
-def spread(small, heads, width):
-    lane = lax.broadcasted_iota(jnp.int32, (heads, width), 1) // (width // heads)
-    row = lax.broadcasted_iota(jnp.int32, (heads, width), 0)
+def halves_of(small):
+    high = small.astype(bf16).astype(f32)
+    return jnp.concatenate([high, small - high], axis=1).astype(bf16)
+
+
+def spread(halves, first, count, head):
+    heads = halves.shape[1] // 2
+    lane = (lax.broadcasted_iota(jnp.int32, (heads, count), 1) + first) // head
+    row = lax.broadcasted_iota(jnp.int32, (heads, count), 0)
     pattern = jnp.where(lane == row, 1.0, 0.0).astype(bf16)
-    high = small.astype(bf16).astype(f32)
-    halves = jnp.concatenate([high, small - high], axis=1).astype(bf16)
     return dot(halves, jnp.concatenate([pattern, pattern], axis=0))
 
 
@@ -45,8 +49,12 @@
 
 def decay_sums(logs):
     order, other = orders(logs.shape[1])
-    lower = jnp.where(other <= order, 1.0, 0.0).astype(f32)
-    return dot(lower, logs, (1, 1), highest)
+    lower = jnp.where(other <= order, 1.0, 0.0).astype(bf16)
+    high = logs.astype(bf16)
+    rest = logs - high.astype(f32)
+    middle = rest.astype(bf16)
+    low = (rest - middle.astype(f32)).astype(bf16)
+    return dot(lower, low, (1, 1)) + dot(lower, middle, (1, 1)) + dot(lower, high, (1, 1))
 
 
 def segments(flags):
@@ -61,8 +69,8 @@
 
 
 def first_body(
-    place, normed_far, w_far, vals_far, cots_far, rate_far, starts_far, message, factors_out, u_out, v_out, bc_out,
-    groups, normed, w_bc, vals, cots, rate, starts, small, first, second, third, fourth,
+    place, normed_far, w_far, vals_far, cots_far, rate_far, starts_far, message, factors_out, u_out, v_out, bc_out, normed,
+    groups, w_bc, vals, cots, rate, starts, small, first, second, third, fourth,
 ):
     heads = rate.shape[0]
     width = vals.shape[1]
@@ -92,14 +100,15 @@
         groups[group, :eighth, :] = total[group * eighth:(group + 1) * eighth]
     up = jnp.where(segment == 0.0, jnp.exp(sums), 0.0)
     down = jnp.where(segment == last_segment, jnp.exp(sums[-1:, :] - sums), 0.0)
-    up_wide = spread(up, heads, width)
-    down_wide = spread(down, heads, width)
+    up, down = halves_of(up), halves_of(down)
     for copy in waves[0] + waves[1] + waves[2] + waves[3]:
         copy.wait()
-    bc = dot(normed[...], w_bc[...]).astype(bf16)
-    bc_out[...] = bc
-    u_out[...] = (up_wide * cots[...].astype(f32)).astype(bf16)
-    v_out[...] = (down_wide * vals[...].astype(f32)).astype(bf16)
+    bc_out[...] = dot(normed[...], w_bc[...]).astype(bf16)
+    tile = width // 5
+    for first in range(0, width, tile):
+        lanes = slice(first, first + tile)
+        u_out[:, lanes] = (spread(up, first, tile, width // heads) * cots[:, lanes].astype(f32)).astype(bf16)
+        v_out[:, lanes] = (spread(down, first, tile, width // heads) * vals[:, lanes].astype(f32)).astype(bf16)
     factors_out[...] = groups[...]
     half = width // 2
     end_states(place, 1, u_out, v_out, bc_out, groups, message, message, message, (0, half, 2 * half))
@@ -136,8 +145,9 @@
     later = jnp.where(other <= order, flags, 0.0)
     reach = dot(later.astype(bf16), jnp.where(order > other, 1.0, 0.0).astype(bf16))
     inside = jnp.logical_and(order >= other, reach == 0.0)
-    scale = spread(jnp.exp(sums[-1:, :] - sums), heads, width)
-    lifted = (spread(jnp.exp(sums - sums[-1:, :]), heads, width) * cots[...].astype(f32)).astype(bf16)
+    head = width // heads
+    scale = spread(halves_of(jnp.exp(sums[-1:, :] - sums)), 0, width, head)
+    lifted = (spread(halves_of(jnp.exp(sums - sums[-1:, :])), 0, width, head) * cots[...].astype(f32)).astype(bf16)
     weighted = (scale * vals[...].astype(f32)).astype(bf16)
     bmat, cmat = bc_ref[:, :state], bc_ref[:, state:]
     paired = jnp.where(inside, dot(lifted, weighted, (1, 1)), 0.0).astype(bf16)
@@ -251,7 +261,7 @@
             out[after, :] = state_behind
 
 
-def core_body(chunks, flips, head, place, *refs):
+def core_body(chunks, head, place, *refs):
     count = 4 * len(chunks)
     keep_f, keep_g, decays, recv, send, own = refs[count:]
     base = keep_f.shape[0]
@@ -259,7 +269,7 @@
     slot = decays.shape[0] // 4
     second = place[0] == 1
     for number, (start, size) in enumerate(chunks):
-        for flip, ref in zip((0,) + flips[number], refs[number * 4:number * 4 + 4]):
+        for flip, ref in zip((0, 3, 1, 2), refs[number * 4:number * 4 + 4]):
             for k in range(size):
                 at = flip * rows + (start + k) * head
                 spot = flip * slot + start + k
@@ -432,15 +442,15 @@
     def swap_both(array):
         return lax.ppermute(array, ("dp", "seq"), [(d * shards + s, (d ^ 1) * shards + (s ^ 1)) for d in range(packs) for s in range(shards)])
 
-    message, factors, u, v, bc = kernel(
+    message, factors, u, v, bc, near_normed = kernel(
         first_body,
         (
             shape(2 * base + 4 * slot, state), jax.ShapeDtypeStruct((8, slot, LANES), f32),
-            shape(length, width, bf16), shape(length, width, bf16), shape(length, 2 * state, bf16),
+            shape(length, width, bf16), shape(length, width, bf16), shape(length, 2 * state, bf16), shape(length, depth, bf16),
         ),
         normed, w_bc, values, cotangent, rate_index, starts,
         scratch=[
-            pltpu.VMEM((8, slot, LANES), f32), pltpu.VMEM(hidden.shape, bf16), pltpu.VMEM(w_bc.shape, bf16),
+            pltpu.VMEM((8, slot, LANES), f32), pltpu.VMEM(w_bc.shape, bf16),
             pltpu.VMEM(vals.shape, bf16), pltpu.VMEM(cots.shape, bf16), pltpu.VMEM(rate.shape, jnp.int32),
             pltpu.VMEM(starts.shape, jnp.int32),
         ] + [pltpu.SemaphoreType.DMA((count,)) for count in (2, 4, 4, 4, 4)],
@@ -459,7 +469,7 @@
     if direct:
         own_turned, core_turned, message = kernel(
             bind(turn_body, levels, rows), (shape(part, length, bf16), shape(wide, LANES), shape(2 * wide, LANES)),
-            hidden, scratch=[pltpu.VMEM((depth, length), f32)], vmem=16,
+            near_normed, scratch=[pltpu.VMEM((depth, length), f32)], vmem=16,
         )
         pack_turned = swap_pack(message)
 
@@ -469,8 +479,9 @@
     def parcel(size):
         return shape(2 * size * head + padded(size), state)
 
-    def to_quad(arrays, flips=(3, 1, 2)):
-        return [swap(arrays[flip - 1], flip * 2) for flip in flips]
+    def to_quad(arrays):
+        across = swap(arrays[2], 6)
+        return [across, swap(arrays[0], 2), swap(arrays[1], 4)]
 
     quads = []
     for start, size in chunks:
@@ -495,16 +506,15 @@
             out = parcel(size) if last is None else shape(size * head, state)
             totals[number] = kernel(bind(join_body, size, head, bit, last), out, totals[number], arrived[number][-1])
             arrived[number].append(swap(totals[number], 8 << bit))
-    states, orders_of = [], []
+    states = []
     for number, ((start, size), group, steps) in enumerate(zip(chunks, quads, arrived)):
         waits = states[1:2] + ([pack_turned] if direct else []) if states else []
         enter, *sends = kernel(
             bind(enter_body, size, head, bits), (shape(2 * size * head, state),) * 4, *group, *steps, behind=waits,
         )
-        orders_of.append((1, 3, 2) if number == 0 else (3, 1, 2))
-        states += [enter] + to_quad(sends, orders_of[-1])
+        states += [enter] + to_quad(sends)
     send, final = kernel(
-        bind(core_body, chunks, orders_of, head), (shape(2 * base, state), shape(2 * base, state, bf16)), *states, keep_f, keep_g, decays, recv,
+        bind(core_body, chunks, head), (shape(2 * base, state), shape(2 * base, state, bf16)), *states, keep_f, keep_g, decays, recv,
     )
     core_recv = swap(send, 1)
     dbc = dbc_local

time: 85.5 us -> 81.7 us (0.956)
  starting transfers between devices: 34.2 us -> 31.3 us
  Pallas kernels: 12.4 us -> 11.3 us
    ppermute x23, starting transfers between devices: 30.7 us -> 27.1 us  [swap(): return lax.ppermute(array, 'seq', [(s, s ^ mask) for s in range(shards)])]
    ppermute x23, waiting for transfers between devices: 30.6 us -> 32 us  [swap(): return lax.ppermute(array, 'seq', [(s, s ^ mask) for s in range(shards)])]
    pallas_call x18, Pallas kernels: 12.4 us -> 11.3 us  [kernel(): pl.pallas_call(run, in_specs=[there] * count + [pl.BlockSpec(memory_space...]
    ppermute x2, waiting for transfers between devices: 6.64 us -> 5.57 us  [swap_pack(): return lax.ppermute(array, 'dp', [(d, d ^ 1) for d in range(packs)])]
  transfers between devices with their start and end apart: 25 -> 25, of which waited for: 13 -> 16; matrix products, arithmetic and copies ran while one was open for 0% -> 0% of each run, Pallas kernels for 7% -> 7%
where the time goes in v4:
time: 81.7 us; the launch traced here: 81.6 us
  waiting for transfers between devices  37.5 us (46%)
  starting transfers between devices  31.3 us (38%)
  Pallas kernels  11.3 us (14%)
    ppermute x23, waiting for transfers between devices, swap(): return lax.ppermute(array, 'seq', [(s, s ^ mask) for s in range(shards)])  32 us
    ppermute x23, starting transfers between devices, swap(): return lax.ppermute(array, 'seq', [(s, s ^ mask) for s in range(shards)])  27.1 us
    pallas_call x18, Pallas kernels, kernel(): pl.pallas_call(run, in_specs=[there] * count + [pl.BlockSpec(memory_space...  11.3 us
    ppermute x2, waiting for transfers between devices, swap_pack(): return lax.ppermute(array, 'dp', [(d, d ^ 1) for d in range(packs)])  5.57 us
    ppermute x2, starting transfers between devices, swap_pack(): return lax.ppermute(array, 'dp', [(d, d ^ 1) for d in range(packs)])  4.19 us
  transfers between devices with their start and end apart: 25, of which 16 were waited for; matrix products, arithmetic and copies ran while one was open for 0% of the time, Pallas kernels for 7%

profile of v4, /device:TPU:0, one launch (start us, length us, event | category | flops | bytes accessed | tf_op | source)
XLA Modules:
  0.0 81.6 jit_solution(5655560610823134645)
XLA Ops:
  0.6 3.9 %shard_map.77 = (f32[2592,128]{1,0:T(8,128)S(1)}, f32[8,8,128]{2,1,0:T(8,128)S(1)}, bf16[192,2560]{1,0:T(8,128)(2,1)S(1)}, bf16[192,2560]{1,0:T(8,128)(2,1)S(1)}...) custom-call(bf16[1,192,2560]{2,1,0:T(8,128)(2,1)} %refs_0_.1, bf16[2560,256]{1,0:T(8,128)(2,1)} %refs_1_.1, ...), custom_call_target="tpu_custom_call" | custom-call | flops 1000 | bytes 1000 | tf_op jit(solution)/shard_map/pallas_call | solution.py:421
  6.2 2.6 %collective-permute-start.12 = (f32[1920,128]{1,0:T(8,128)S(1)}, f32[1920,128]{1,0:T(8,128)S(1)}, u32[]{:S(2)}, u32[]{:S(2)}) collective-permute-start(f32[1920,128]{1,0:T(8,128)S(1)} %get-tuple-element.72), channel_id=1, source_target_pairs={{0,16},{16,0},{1,17},{17,1},{2,18},{18,2},{3,19},{19,3},{4,20},{20... | collective-permute-start | bytes 2949128 | tf_op jit(solution)/shard_map/ppermute | solution.py:440
  9.0 2.8 %collective-permute-start.1 = (f32[392,128]{1,0:T(8,128)S(1)}, f32[392,128]{1,0:T(8,128)S(1)}, u32[]{:S(2)}, u32[]{:S(2)}) collective-permute-start(f32[392,128]{1,0:T(8,128)S(1)} %get-tuple-element.61), channel_id=1, source_target_pairs={{0,6},{1,7},{2,4},{3,5},{4,2},{5,3},{6,0},{7,1},{8,14},{9,15},{10,... | collective-permute-start | bytes 602120 | tf_op jit(solution)/shard_map/ppermute | solution.py:437
  12.6 1.9 %shard_map.81 = (f32[192,2560]{1,0:T(8,128)S(1)}, f32[192,2560]{1,0:T(8,128)S(1)}, f32[192,256]{1,0:T(8,128)S(1)}) custom-call(bf16[192,2560]{1,0:T(8,128)(2,1)S(1)} %bitcast.4, bf16[192,2560]{1,0:T(8,128)(2,1)S(1)} %bitcast.5, s32[40,192]{1,0:T(8,128)S(1)} %bitcast.6, s32[1,192]{1,0:T(1,128)S(1)} %copy-done.3, ...), custom_call_target="tpu_custom_call" | custom-call | flops 1000 | bytes 1000 | tf_op jit(solution)/shard_map/pallas_call | solution.py:421
  14.5 3.3 %collective-permute-done.1.refs_5_.refs_1_ = f32[392,128]{1,0:T(8,128)S(1)} collective-permute-done((f32[392,128]{1,0:T(8,128)S(1)}, f32[392,128]{1,0:T(8,128)S(1)}, u32[]{:S(2)}, u32[]{:S(2)}) %collective-permute-start.1) | collective-permute-done | bytes 200736 | tf_op jit(solution)/shard_map/ppermute | solution.py:437
  17.9 2.8 %collective-permute-start.5 = (f32[264,128]{1,0:T(8,128)S(1)}, f32[264,128]{1,0:T(8,128)S(1)}, u32[]{:S(2)}, u32[]{:S(2)}) collective-permute-start(f32[264,128]{1,0:T(8,128)S(1)} %get-tuple-element.65), channel_id=1, source_target_pairs={{0,6},{1,7},{2,4},{3,5},{4,2},{5,3},{6,0},{7,1},{8,14},{9,15},{10,... | collective-permute-start | bytes 405512 | tf_op jit(solution)/shard_map/ppermute | solution.py:437
  22.2 1.8 %collective-permute-start.7 = (f32[264,128]{1,0:T(8,128)S(1)}, f32[264,128]{1,0:T(8,128)S(1)}, u32[]{:S(2)}, u32[]{:S(2)}) collective-permute-start(f32[264,128]{1,0:T(8,128)S(1)} %get-tuple-element.67), channel_id=1, source_target_pairs={{0,4},{1,5},{2,6},{3,7},{4,0},{5,1},{6,2},{7,3},{8,12},{9,13},{10,... | collective-permute-start | bytes 405512 | tf_op jit(solution)/shard_map/ppermute | solution.py:437
  24.1 2.7 %collective-permute-start.4 = (f32[192,128]{1,0:T(8,128)S(1)}, f32[192,128]{1,0:T(8,128)S(1)}, u32[]{:S(2)}, u32[]{:S(2)}) collective-permute-start(f32[192,128]{1,0:T(8,128)S(1)} %shard_map.83.refs_4_), channel_id=1, source_target_pairs={{0,8},{1,9},{2,10},{3,11},{4,12},{5,13},{6,14},{7,15},{8,0},{9,1},... | collective-permute-start | bytes 294920 | tf_op jit(solution)/shard_map/ppermute | solution.py:437
  27.2 1.4 %collective-permute-done.7.refs_3_ = f32[264,128]{1,0:T(8,128)S(1)} collective-permute-done((f32[264,128]{1,0:T(8,128)S(1)}, f32[264,128]{1,0:T(8,128)S(1)}, u32[]{:S(2)}, u32[]{:S(2)}) %collective-permute-start.7) | collective-permute-done | bytes 135200 | tf_op jit(solution)/shard_map/ppermute | solution.py:437
  28.6 2.0 %collective-permute-done.4.refs_4_ = f32[192,128]{1,0:T(8,128)S(1)} collective-permute-done((f32[192,128]{1,0:T(8,128)S(1)}, f32[192,128]{1,0:T(8,128)S(1)}, u32[]{:S(2)}, u32[]{:S(2)}) %collective-permute-start.4) | collective-permute-done | bytes 98336 | tf_op jit(solution)/shard_map/ppermute | solution.py:437
  30.8 2.7 %collective-permute-start.8 = (f32[384,128]{1,0:T(8,128)S(1)}, f32[384,128]{1,0:T(8,128)S(1)}, u32[]{:S(2)}, u32[]{:S(2)}) collective-permute-start(f32[384,128]{1,0:T(8,128)S(1)} %get-tuple-element.69), channel_id=1, source_target_pairs={{0,6},{1,7},{2,4},{3,5},{4,2},{5,3},{6,0},{7,1},{8,14},{9,15},{10,... | collective-permute-start | bytes 589832 | tf_op jit(solution)/shard_map/ppermute | solution.py:437
  33.5 1.9 %collective-permute-start.11 = (f32[128,128]{1,0:T(8,128)S(1)}, f32[128,128]{1,0:T(8,128)S(1)}, u32[]{:S(2)}, u32[]{:S(2)}) collective-permute-start(f32[128,128]{1,0:T(8,128)S(1)} %shard_map.84.refs_5_), channel_id=1, source_target_pairs={{0,8},{1,9},{2,10},{3,11},{4,12},{5,13},{6,14},{7,15},{8,0},{9,1},... | collective-permute-start | bytes 196616 | tf_op jit(solution)/shard_map/ppermute | solution.py:437
  36.3 4.0 %collective-permute-done.11.refs_4_ = f32[128,128]{1,0:T(8,128)S(1)} collective-permute-done((f32[128,128]{1,0:T(8,128)S(1)}, f32[128,128]{1,0:T(8,128)S(1)}, u32[]{:S(2)}, u32[]{:S(2)}) %collective-permute-start.11) | collective-permute-done | bytes 65568 | tf_op jit(solution)/shard_map/ppermute | solution.py:437
  40.5 2.3 %collective-permute-start.13 = (f32[256,128]{1,0:T(8,128)S(1)}, f32[256,128]{1,0:T(8,128)S(1)}, u32[]{:S(2)}, u32[]{:S(2)}) collective-permute-start(f32[256,128]{1,0:T(8,128)S(1)} %get-tuple-element.74), channel_id=1, source_target_pairs={{0,6},{1,7},{2,4},{3,5},{4,2},{5,3},{6,0},{7,1},{8,14},{9,15},{10,... | collective-permute-start | bytes 393224 | tf_op jit(solution)/shard_map/ppermute | solution.py:437
  45.2 2.2 %collective-permute-done.13.refs_5_ = f32[256,128]{1,0:T(8,128)S(1)} collective-permute-done((f32[256,128]{1,0:T(8,128)S(1)}, f32[256,128]{1,0:T(8,128)S(1)}, u32[]{:S(2)}, u32[]{:S(2)}) %collective-permute-start.13) | collective-permute-done | bytes 131104 | tf_op jit(solution)/shard_map/ppermute | solution.py:437
  49.8 2.6 %collective-permute-done.16.refs_3_ = f32[2560,128]{1,0:T(8,128)S(1)} collective-permute-done((f32[2560,128]{1,0:T(8,128)S(1)}, f32[2560,128]{1,0:T(8,128)S(1)}, u32[]{:S(2)}, u32[]{:S(2)}) %collective-permute-start.16) | collective-permute-done | bytes 1310752 | tf_op jit(solution)/shard_map/ppermute | solution.py:437
  53.1 1.5 %collective-permute-start.19 = (f32[192,256]{1,0:T(8,128)S(1)}, f32[192,256]{1,0:T(8,128)S(1)}, u32[]{:S(2)}, u32[]{:S(2)}) collective-permute-start(f32[192,256]{1,0:T(8,128)S(1)} %get-tuple-element.83.refs_2_.refs_1_), channel_id=1, source_target_pairs={{0,16},{16,0},{1,17},{17,1},{2,18},{18,2},{3,19},{19,3},{4,20},{20... | collective-permute-start | bytes 589832 | tf_op jit(solution)/shard_map/ppermute | solution.py:440
  54.8 5.6 %collective-permute-done.19.refs_3_ = f32[192,256]{1,0:T(8,128)S(1)} collective-permute-done((f32[192,256]{1,0:T(8,128)S(1)}, f32[192,256]{1,0:T(8,128)S(1)}, u32[]{:S(2)}, u32[]{:S(2)}) %collective-permute-start.19) | collective-permute-done | bytes 196640 | tf_op jit(solution)/shard_map/ppermute | solution.py:440
  60.3 1.4 %shard_map.91 = (bf16[192,2560]{1,0:T(8,128)(2,1)}, f32[8,128]{1,0:T(8,128)S(1)}) custom-call(f32[192,2560]{1,0:T(8,128)S(1)} %get-tuple-element.58.refs_0_, f32[192,2560]{1,0:T(8,128)S(1)} %get-tuple-element.59.refs_1_, bf16[192,256]{1,0:T(8,128)(2,1)S(1)} %get-tuple-element.47.refs_2_.refs_4_, bf16[1280,128]{1,0:T(8,128)(2,1)S(1)} %get-tuple-element.79.refs_3_, ...), custom_call_target="tpu_custom_call" | custom-call | flops 1000 | bytes 1000 | tf_op jit(solution)/shard_map/pallas_call | solution.py:421
  62.7 1.6 %collective-permute-start.21 = (f32[160,256]{1,0:T(8,128)S(1)}, f32[160,256]{1,0:T(8,128)S(1)}, u32[]{:S(2)}, u32[]{:S(2)}) collective-permute-start(f32[160,256]{1,0:T(8,128)S(1)} %get-tuple-element.87), channel_id=1, source_target_pairs={{0,6},{1,7},{2,4},{3,5},{4,2},{5,3},{6,0},{7,1},{8,14},{9,15},{10,... | collective-permute-start | bytes 491528 | tf_op jit(solution)/shard_map/ppermute | solution.py:437
  66.3 4.4 %collective-permute-done.21.refs_1_ = f32[160,256]{1,0:T(8,128)S(1)} collective-permute-done((f32[160,256]{1,0:T(8,128)S(1)}, f32[160,256]{1,0:T(8,128)S(1)}, u32[]{:S(2)}, u32[]{:S(2)}) %collective-permute-start.21) | collective-permute-done | bytes 163872 | tf_op jit(solution)/shard_map/ppermute | solution.py:437
  70.7 3.1 %collective-permute-done.22.refs_2_ = f32[160,256]{1,0:T(8,128)S(1)} collective-permute-done((f32[160,256]{1,0:T(8,128)S(1)}, f32[160,256]{1,0:T(8,128)S(1)}, u32[]{:S(2)}, u32[]{:S(2)}) %collective-permute-start.22) | collective-permute-done | bytes 163872 | tf_op jit(solution)/shard_map/ppermute | solution.py:437
  73.8 2.3 %collective-permute-start.24 = (f32[80,256]{1,0:T(8,128)S(1)}, f32[80,256]{1,0:T(8,128)S(1)}, u32[]{:S(2)}, u32[]{:S(2)}) collective-permute-start(f32[80,256]{1,0:T(8,128)S(1)} %get-tuple-element.91), channel_id=1, source_target_pairs={{0,8},{1,9},{2,10},{3,11},{4,12},{5,13},{6,14},{7,15},{8,0},{9,1},... | collective-permute-start | bytes 245768 | tf_op jit(solution)/shard_map/ppermute | solution.py:437
  76.1 4.8 %collective-permute-done.24 = f32[80,256]{1,0:T(8,128)S(1)} collective-permute-done((f32[80,256]{1,0:T(8,128)S(1)}, f32[80,256]{1,0:T(8,128)S(1)}, u32[]{:S(2)}, u32[]{:S(2)}) %collective-permute-start.24) | collective-permute-done | bytes 81952 | tf_op jit(solution)/shard_map/ppermute | solution.py:437
  (53 shorter events, 15.2 us)
Async XLA Ops:
  4.5 4.4 %collective-permute-start = (f32[2592,128]{1,0:T(8,128)S(1)}, f32[2592,128]{1,0:T(8,128)S(1)}, u32[]{:S(2)}, u32[]{:S(2)}) collective-permute-start(f32[2592,128]{1,0:T(8,128)S(1)} %get-tuple-element.54), channel_id=1, source_target_pairs={{0,1},{1,0},{2,3},{3,2},{4,5},{5,4},{6,7},{7,6},{8,9},{9,8},{10,11... | collective-permute-start | bytes 3981320 | tf_op jit(solution)/shard_map/ppermute | solution.py:437
  6.2 30.1 %collective-permute-start.12 = (f32[1920,128]{1,0:T(8,128)S(1)}, f32[1920,128]{1,0:T(8,128)S(1)}, u32[]{:S(2)}, u32[]{:S(2)}) collective-permute-start(f32[1920,128]{1,0:T(8,128)S(1)} %get-tuple-element.72), channel_id=1, source_target_pairs={{0,16},{16,0},{1,17},{17,1},{2,18},{18,2},{3,19},{19,3},{4,20},{20... | collective-permute-start | bytes 2949128 | tf_op jit(solution)/shard_map/ppermute | solution.py:440
  9.0 8.8 %collective-permute-start.1 = (f32[392,128]{1,0:T(8,128)S(1)}, f32[392,128]{1,0:T(8,128)S(1)}, u32[]{:S(2)}, u32[]{:S(2)}) collective-permute-start(f32[392,128]{1,0:T(8,128)S(1)} %get-tuple-element.61), channel_id=1, source_target_pairs={{0,6},{1,7},{2,4},{3,5},{4,2},{5,3},{6,0},{7,1},{8,14},{9,15},{10,... | collective-permute-start | bytes 602120 | tf_op jit(solution)/shard_map/ppermute | solution.py:437
  11.8 10.4 %collective-permute-start.2 = (f32[392,128]{1,0:T(8,128)S(1)}, f32[392,128]{1,0:T(8,128)S(1)}, u32[]{:S(2)}, u32[]{:S(2)}) collective-permute-start(f32[392,128]{1,0:T(8,128)S(1)} %get-tuple-element.62), channel_id=1, source_target_pairs={{0,2},{1,3},{2,0},{3,1},{4,6},{5,7},{6,4},{7,5},{8,10},{9,11},{10,... | collective-permute-start | bytes 602120 | tf_op jit(solution)/shard_map/ppermute | solution.py:437
  12.3 11.7 %collective-permute-start.3 = (f32[392,128]{1,0:T(8,128)S(1)}, f32[392,128]{1,0:T(8,128)S(1)}, u32[]{:S(2)}, u32[]{:S(2)}) collective-permute-start(f32[392,128]{1,0:T(8,128)S(1)} %get-tuple-element.63), channel_id=1, source_target_pairs={{0,4},{1,5},{2,6},{3,7},{4,0},{5,1},{6,2},{7,3},{8,12},{9,13},{10,... | collective-permute-start | bytes 602120 | tf_op jit(solution)/shard_map/ppermute | solution.py:437
  17.9 8.8 %collective-permute-start.5 = (f32[264,128]{1,0:T(8,128)S(1)}, f32[264,128]{1,0:T(8,128)S(1)}, u32[]{:S(2)}, u32[]{:S(2)}) collective-permute-start(f32[264,128]{1,0:T(8,128)S(1)} %get-tuple-element.65), channel_id=1, source_target_pairs={{0,6},{1,7},{2,4},{3,5},{4,2},{5,3},{6,0},{7,1},{8,14},{9,15},{10,... | collective-permute-start | bytes 405512 | tf_op jit(solution)/shard_map/ppermute | solution.py:437
  20.7 6.5 %collective-permute-start.6 = (f32[264,128]{1,0:T(8,128)S(1)}, f32[264,128]{1,0:T(8,128)S(1)}, u32[]{:S(2)}, u32[]{:S(2)}) collective-permute-start(f32[264,128]{1,0:T(8,128)S(1)} %get-tuple-element.66), channel_id=1, source_target_pairs={{0,2},{1,3},{2,0},{3,1},{4,6},{5,7},{6,4},{7,5},{8,10},{9,11},{10,... | collective-permute-start | bytes 405512 | tf_op jit(solution)/shard_map/ppermute | solution.py:437
  22.2 6.4 %collective-permute-start.7 = (f32[264,128]{1,0:T(8,128)S(1)}, f32[264,128]{1,0:T(8,128)S(1)}, u32[]{:S(2)}, u32[]{:S(2)}) collective-permute-start(f32[264,128]{1,0:T(8,128)S(1)} %get-tuple-element.67), channel_id=1, source_target_pairs={{0,4},{1,5},{2,6},{3,7},{4,0},{5,1},{6,2},{7,3},{8,12},{9,13},{10,... | collective-permute-start | bytes 405512 | tf_op jit(solution)/shard_map/ppermute | solution.py:437
  24.1 6.6 %collective-permute-start.4 = (f32[192,128]{1,0:T(8,128)S(1)}, f32[192,128]{1,0:T(8,128)S(1)}, u32[]{:S(2)}, u32[]{:S(2)}) collective-permute-start(f32[192,128]{1,0:T(8,128)S(1)} %shard_map.83.refs_4_), channel_id=1, source_target_pairs={{0,8},{1,9},{2,10},{3,11},{4,12},{5,13},{6,14},{7,15},{8,0},{9,1},... | collective-permute-start | bytes 294920 | tf_op jit(solution)/shard_map/ppermute | solution.py:437
  30.8 9.5 %collective-permute-start.8 = (f32[384,128]{1,0:T(8,128)S(1)}, f32[384,128]{1,0:T(8,128)S(1)}, u32[]{:S(2)}, u32[]{:S(2)}) collective-permute-start(f32[384,128]{1,0:T(8,128)S(1)} %get-tuple-element.69), channel_id=1, source_target_pairs={{0,6},{1,7},{2,4},{3,5},{4,2},{5,3},{6,0},{7,1},{8,14},{9,15},{10,... | collective-permute-start | bytes 589832 | tf_op jit(solution)/shard_map/ppermute | solution.py:437
  33.5 6.8 %collective-permute-start.11 = (f32[128,128]{1,0:T(8,128)S(1)}, f32[128,128]{1,0:T(8,128)S(1)}, u32[]{:S(2)}, u32[]{:S(2)}) collective-permute-start(f32[128,128]{1,0:T(8,128)S(1)} %shard_map.84.refs_5_), channel_id=1, source_target_pairs={{0,8},{1,9},{2,10},{3,11},{4,12},{5,13},{6,14},{7,15},{8,0},{9,1},... | collective-permute-start | bytes 196616 | tf_op jit(solution)/shard_map/ppermute | solution.py:437
  35.4 9.1 %collective-permute-start.9 = (f32[384,128]{1,0:T(8,128)S(1)}, f32[384,128]{1,0:T(8,128)S(1)}, u32[]{:S(2)}, u32[]{:S(2)}) collective-permute-start(f32[384,128]{1,0:T(8,128)S(1)} %get-tuple-element.70), channel_id=1, source_target_pairs={{0,2},{1,3},{2,0},{3,1},{4,6},{5,7},{6,4},{7,5},{8,10},{9,11},{10,... | collective-permute-start | bytes 589832 | tf_op jit(solution)/shard_map/ppermute | solution.py:437
  36.3 8.8 %collective-permute-start.10 = (f32[384,128]{1,0:T(8,128)S(1)}, f32[384,128]{1,0:T(8,128)S(1)}, u32[]{:S(2)}, u32[]{:S(2)}) collective-permute-start(f32[384,128]{1,0:T(8,128)S(1)} %get-tuple-element.71), channel_id=1, source_target_pairs={{0,4},{1,5},{2,6},{3,7},{4,0},{5,1},{6,2},{7,3},{8,12},{9,13},{10,... | collective-permute-start | bytes 589832 | tf_op jit(solution)/shard_map/ppermute | solution.py:437
  40.5 6.9 %collective-permute-start.13 = (f32[256,128]{1,0:T(8,128)S(1)}, f32[256,128]{1,0:T(8,128)S(1)}, u32[]{:S(2)}, u32[]{:S(2)}) collective-permute-start(f32[256,128]{1,0:T(8,128)S(1)} %get-tuple-element.74), channel_id=1, source_target_pairs={{0,6},{1,7},{2,4},{3,5},{4,2},{5,3},{6,0},{7,1},{8,14},{9,15},{10,... | collective-permute-start | bytes 393224 | tf_op jit(solution)/shard_map/ppermute | solution.py:437
  42.8 5.7 %collective-permute-start.14 = (f32[256,128]{1,0:T(8,128)S(1)}, f32[256,128]{1,0:T(8,128)S(1)}, u32[]{:S(2)}, u32[]{:S(2)}) collective-permute-start(f32[256,128]{1,0:T(8,128)S(1)} %get-tuple-element.75), channel_id=1, source_target_pairs={{0,2},{1,3},{2,0},{3,1},{4,6},{5,7},{6,4},{7,5},{8,10},{9,11},{10,... | collective-permute-start | bytes 393224 | tf_op jit(solution)/shard_map/ppermute | solution.py:437
  44.0 5.0 %collective-permute-start.15 = (f32[256,128]{1,0:T(8,128)S(1)}, f32[256,128]{1,0:T(8,128)S(1)}, u32[]{:S(2)}, u32[]{:S(2)}) collective-permute-start(f32[256,128]{1,0:T(8,128)S(1)} %get-tuple-element.76), channel_id=1, source_target_pairs={{0,4},{1,5},{2,6},{3,7},{4,0},{5,1},{6,2},{7,3},{8,12},{9,13},{10,... | collective-permute-start | bytes 393224 | tf_op jit(solution)/shard_map/ppermute | solution.py:437
  49.3 3.1 %collective-permute-start.16 = (f32[2560,128]{1,0:T(8,128)S(1)}, f32[2560,128]{1,0:T(8,128)S(1)}, u32[]{:S(2)}, u32[]{:S(2)}) collective-permute-start(f32[2560,128]{1,0:T(8,128)S(1)} %get-tuple-element.78.refs_4_), channel_id=1, source_target_pairs={{0,1},{1,0},{2,3},{3,2},{4,5},{5,4},{6,7},{7,6},{8,9},{9,8},{10,11... | collective-permute-start | bytes 3932168 | tf_op jit(solution)/shard_map/ppermute | solution.py:437
  52.9 8.8 %collective-permute-start.17 = (f32[1920,128]{1,0:T(8,128)S(1)}, f32[1920,128]{1,0:T(8,128)S(1)}, u32[]{:S(2)}, u32[]{:S(2)}) collective-permute-start(f32[1920,128]{1,0:T(8,128)S(1)} %shard_map.90.refs_5_), channel_id=1, source_target_pairs={{0,1},{1,0},{2,3},{3,2},{4,5},{5,4},{6,7},{7,6},{8,9},{9,8},{10,11... | collective-permute-start | bytes 2949128 | tf_op jit(solution)/shard_map/ppermute | solution.py:437
  53.1 7.2 %collective-permute-start.19 = (f32[192,256]{1,0:T(8,128)S(1)}, f32[192,256]{1,0:T(8,128)S(1)}, u32[]{:S(2)}, u32[]{:S(2)}) collective-permute-start(f32[192,256]{1,0:T(8,128)S(1)} %get-tuple-element.83.refs_2_.refs_1_), channel_id=1, source_target_pairs={{0,16},{16,0},{1,17},{17,1},{2,18},{18,2},{3,19},{19,3},{4,20},{20... | collective-permute-start | bytes 589832 | tf_op jit(solution)/shard_map/ppermute | solution.py:440
  54.7 7.4 %collective-permute-start.18 = (f32[192,256]{1,0:T(8,128)S(1)}, f32[192,256]{1,0:T(8,128)S(1)}, u32[]{:S(2)}, u32[]{:S(2)}) collective-permute-start(f32[192,256]{1,0:T(8,128)S(1)} %get-tuple-element.83.refs_2_.refs_1_), channel_id=1, source_target_pairs={{0,1},{1,0},{2,3},{3,2},{4,5},{5,4},{6,7},{7,6},{8,9},{9,8},{10,11... | collective-permute-start | bytes 589832 | tf_op jit(solution)/shard_map/ppermute | solution.py:437
  62.7 8.0 %collective-permute-start.21 = (f32[160,256]{1,0:T(8,128)S(1)}, f32[160,256]{1,0:T(8,128)S(1)}, u32[]{:S(2)}, u32[]{:S(2)}) collective-permute-start(f32[160,256]{1,0:T(8,128)S(1)} %get-tuple-element.87), channel_id=1, source_target_pairs={{0,6},{1,7},{2,4},{3,5},{4,2},{5,3},{6,0},{7,1},{8,14},{9,15},{10,... | collective-permute-start | bytes 491528 | tf_op jit(solution)/shard_map/ppermute | solution.py:437
  64.3 9.5 %collective-permute-start.22 = (f32[160,256]{1,0:T(8,128)S(1)}, f32[160,256]{1,0:T(8,128)S(1)}, u32[]{:S(2)}, u32[]{:S(2)}) collective-permute-start(f32[160,256]{1,0:T(8,128)S(1)} %get-tuple-element.88), channel_id=1, source_target_pairs={{0,2},{1,3},{2,0},{3,1},{4,6},{5,7},{6,4},{7,5},{8,10},{9,11},{10,... | collective-permute-start | bytes 491528 | tf_op jit(solution)/shard_map/ppermute | solution.py:437
  65.5 8.3 %collective-permute-start.23 = (f32[160,256]{1,0:T(8,128)S(1)}, f32[160,256]{1,0:T(8,128)S(1)}, u32[]{:S(2)}, u32[]{:S(2)}) collective-permute-start(f32[160,256]{1,0:T(8,128)S(1)} %get-tuple-element.89), channel_id=1, source_target_pairs={{0,4},{1,5},{2,6},{3,7},{4,0},{5,1},{6,2},{7,3},{8,12},{9,13},{10,... | collective-permute-start | bytes 491528 | tf_op jit(solution)/shard_map/ppermute | solution.py:437
  73.8 7.1 %collective-permute-start.24 = (f32[80,256]{1,0:T(8,128)S(1)}, f32[80,256]{1,0:T(8,128)S(1)}, u32[]{:S(2)}, u32[]{:S(2)}) collective-permute-start(f32[80,256]{1,0:T(8,128)S(1)} %get-tuple-element.91), channel_id=1, source_target_pairs={{0,8},{1,9},{2,10},{3,11},{4,12},{5,13},{6,14},{7,15},{8,0},{9,1},... | collective-permute-start | bytes 245768 | tf_op jit(solution)/shard_map/ppermute | solution.py:437
  (5 other events, 16.6 us)

commit v5 on v4

--- a/solution.py
+++ b/solution.py
@@ -78,7 +78,7 @@
     early = [pltpu.make_async_copy(rate_far.at[0], rate, small.at[0]), pltpu.make_async_copy(starts_far, starts, small.at[1])]
     waves = []
     for source, target, sems in (
-        (normed_far.at[0], normed, first), (w_far, w_bc, second), (cots_far.at[0], cots, third), (vals_far.at[0], vals, fourth),
+        (cots_far.at[0], cots, first), (vals_far.at[0], vals, second), (normed_far.at[0], normed, third), (w_far, w_bc, fourth),
     ):
         waves.append([
             pltpu.make_async_copy(source.at[rows], target.at[rows], sems.at[i])
@@ -101,14 +101,16 @@
     up = jnp.where(segment == 0.0, jnp.exp(sums), 0.0)
     down = jnp.where(segment == last_segment, jnp.exp(sums[-1:, :] - sums), 0.0)
     up, down = halves_of(up), halves_of(down)
-    for copy in waves[0] + waves[1] + waves[2] + waves[3]:
+    for copy in waves[0] + waves[1]:
         copy.wait()
-    bc_out[...] = dot(normed[...], w_bc[...]).astype(bf16)
     tile = width // 5
     for first in range(0, width, tile):
         lanes = slice(first, first + tile)
         u_out[:, lanes] = (spread(up, first, tile, width // heads) * cots[:, lanes].astype(f32)).astype(bf16)
         v_out[:, lanes] = (spread(down, first, tile, width // heads) * vals[:, lanes].astype(f32)).astype(bf16)
+    for copy in waves[2] + waves[3]:
+        copy.wait()
+    bc_out[...] = dot(normed[...], w_bc[...]).astype(bf16)
     factors_out[...] = groups[...]
     half = width // 2
     end_states(place, 1, u_out, v_out, bc_out, groups, message, message, message, (0, half, 2 * half))

time: 81.7 us -> 82.4 us (level)
  no operation moved by 1% of the time
where the time goes in v5:
time: 82.4 us; the launch traced here: 82.3 us
  waiting for transfers between devices  37.5 us (46%)
  starting transfers between devices  31.3 us (38%)
  Pallas kernels  12 us (15%)
    ppermute x23, waiting for transfers between devices, swap(): return lax.ppermute(array, 'seq', [(s, s ^ mask) for s in range(shards)])  32 us
    ppermute x23, starting transfers between devices, swap(): return lax.ppermute(array, 'seq', [(s, s ^ mask) for s in range(shards)])  27.1 us
    pallas_call x18, Pallas kernels, kernel(): pl.pallas_call(run, in_specs=[there] * count + [pl.BlockSpec(memory_space...  12 us
    ppermute x2, waiting for transfers between devices, swap_pack(): return lax.ppermute(array, 'dp', [(d, d ^ 1) for d in range(packs)])  5.56 us
    ppermute x2, starting transfers between devices, swap_pack(): return lax.ppermute(array, 'dp', [(d, d ^ 1) for d in range(packs)])  4.15 us
  transfers between devices with their start and end apart: 25, of which 16 were waited for; matrix products, arithmetic and copies ran while one was open for 0% of the time, Pallas kernels for 7%

profile of v5, /device:TPU:0, one launch (start us, length us, event | category | flops | bytes accessed | tf_op | source)
XLA Modules:
  0.0 82.3 jit_solution(11166992141645913086)
XLA Ops:
  0.6 4.5 %shard_map.77 = (f32[2592,128]{1,0:T(8,128)S(1)}, f32[8,8,128]{2,1,0:T(8,128)S(1)}, bf16[192,2560]{1,0:T(8,128)(2,1)S(1)}, bf16[192,2560]{1,0:T(8,128)(2,1)S(1)}...) custom-call(bf16[1,192,2560]{2,1,0:T(8,128)(2,1)} %refs_0_.1, bf16[2560,256]{1,0:T(8,128)(2,1)} %refs_1_.1, ...), custom_call_target="tpu_custom_call" | custom-call | flops 1000 | bytes 1000 | tf_op jit(solution)/shard_map/pallas_call | solution.py:423
  6.9 2.6 %collective-permute-start.12 = (f32[1920,128]{1,0:T(8,128)S(1)}, f32[1920,128]{1,0:T(8,128)S(1)}, u32[]{:S(2)}, u32[]{:S(2)}) collective-permute-start(f32[1920,128]{1,0:T(8,128)S(1)} %get-tuple-element.72), channel_id=1, source_target_pairs={{0,16},{16,0},{1,17},{17,1},{2,18},{18,2},{3,19},{19,3},{4,20},{20... | collective-permute-start | bytes 2949128 | tf_op jit(solution)/shard_map/ppermute | solution.py:442
  9.7 2.8 %collective-permute-start.1 = (f32[392,128]{1,0:T(8,128)S(1)}, f32[392,128]{1,0:T(8,128)S(1)}, u32[]{:S(2)}, u32[]{:S(2)}) collective-permute-start(f32[392,128]{1,0:T(8,128)S(1)} %get-tuple-element.61), channel_id=1, source_target_pairs={{0,6},{1,7},{2,4},{3,5},{4,2},{5,3},{6,0},{7,1},{8,14},{9,15},{10,... | collective-permute-start | bytes 602120 | tf_op jit(solution)/shard_map/ppermute | solution.py:439
  13.2 1.9 %shard_map.81 = (f32[192,2560]{1,0:T(8,128)S(1)}, f32[192,2560]{1,0:T(8,128)S(1)}, f32[192,256]{1,0:T(8,128)S(1)}) custom-call(bf16[192,2560]{1,0:T(8,128)(2,1)S(1)} %bitcast.4, bf16[192,2560]{1,0:T(8,128)(2,1)S(1)} %bitcast.5, s32[40,192]{1,0:T(8,128)S(1)} %bitcast.6, s32[1,192]{1,0:T(1,128)S(1)} %copy-done.3, ...), custom_call_target="tpu_custom_call" | custom-call | flops 1000 | bytes 1000 | tf_op jit(solution)/shard_map/pallas_call | solution.py:423
  15.1 3.3 %collective-permute-done.1.refs_5_.refs_1_ = f32[392,128]{1,0:T(8,128)S(1)} collective-permute-done((f32[392,128]{1,0:T(8,128)S(1)}, f32[392,128]{1,0:T(8,128)S(1)}, u32[]{:S(2)}, u32[]{:S(2)}) %collective-permute-start.1) | collective-permute-done | bytes 200736 | tf_op jit(solution)/shard_map/ppermute | solution.py:439
  18.6 2.8 %collective-permute-start.5 = (f32[264,128]{1,0:T(8,128)S(1)}, f32[264,128]{1,0:T(8,128)S(1)}, u32[]{:S(2)}, u32[]{:S(2)}) collective-permute-start(f32[264,128]{1,0:T(8,128)S(1)} %get-tuple-element.65), channel_id=1, source_target_pairs={{0,6},{1,7},{2,4},{3,5},{4,2},{5,3},{6,0},{7,1},{8,14},{9,15},{10,... | collective-permute-start | bytes 405512 | tf_op jit(solution)/shard_map/ppermute | solution.py:439
  22.9 1.8 %collective-permute-start.7 = (f32[264,128]{1,0:T(8,128)S(1)}, f32[264,128]{1,0:T(8,128)S(1)}, u32[]{:S(2)}, u32[]{:S(2)}) collective-permute-start(f32[264,128]{1,0:T(8,128)S(1)} %get-tuple-element.67), channel_id=1, source_target_pairs={{0,4},{1,5},{2,6},{3,7},{4,0},{5,1},{6,2},{7,3},{8,12},{9,13},{10,... | collective-permute-start | bytes 405512 | tf_op jit(solution)/shard_map/ppermute | solution.py:439
  24.8 2.7 %collective-permute-start.4 = (f32[192,128]{1,0:T(8,128)S(1)}, f32[192,128]{1,0:T(8,128)S(1)}, u32[]{:S(2)}, u32[]{:S(2)}) collective-permute-start(f32[192,128]{1,0:T(8,128)S(1)} %shard_map.83.refs_4_), channel_id=1, source_target_pairs={{0,8},{1,9},{2,10},{3,11},{4,12},{5,13},{6,14},{7,15},{8,0},{9,1},... | collective-permute-start | bytes 294920 | tf_op jit(solution)/shard_map/ppermute | solution.py:439
  27.8 1.4 %collective-permute-done.7.refs_3_ = f32[264,128]{1,0:T(8,128)S(1)} collective-permute-done((f32[264,128]{1,0:T(8,128)S(1)}, f32[264,128]{1,0:T(8,128)S(1)}, u32[]{:S(2)}, u32[]{:S(2)}) %collective-permute-start.7) | collective-permute-done | bytes 135200 | tf_op jit(solution)/shard_map/ppermute | solution.py:439
  29.3 2.0 %collective-permute-done.4.refs_4_ = f32[192,128]{1,0:T(8,128)S(1)} collective-permute-done((f32[192,128]{1,0:T(8,128)S(1)}, f32[192,128]{1,0:T(8,128)S(1)}, u32[]{:S(2)}, u32[]{:S(2)}) %collective-permute-start.4) | collective-permute-done | bytes 98336 | tf_op jit(solution)/shard_map/ppermute | solution.py:439
  31.5 2.7 %collective-permute-start.8 = (f32[384,128]{1,0:T(8,128)S(1)}, f32[384,128]{1,0:T(8,128)S(1)}, u32[]{:S(2)}, u32[]{:S(2)}) collective-permute-start(f32[384,128]{1,0:T(8,128)S(1)} %get-tuple-element.69), channel_id=1, source_target_pairs={{0,6},{1,7},{2,4},{3,5},{4,2},{5,3},{6,0},{7,1},{8,14},{9,15},{10,... | collective-permute-start | bytes 589832 | tf_op jit(solution)/shard_map/ppermute | solution.py:439
  34.2 1.9 %collective-permute-start.11 = (f32[128,128]{1,0:T(8,128)S(1)}, f32[128,128]{1,0:T(8,128)S(1)}, u32[]{:S(2)}, u32[]{:S(2)}) collective-permute-start(f32[128,128]{1,0:T(8,128)S(1)} %shard_map.84.refs_5_), channel_id=1, source_target_pairs={{0,8},{1,9},{2,10},{3,11},{4,12},{5,13},{6,14},{7,15},{8,0},{9,1},... | collective-permute-start | bytes 196616 | tf_op jit(solution)/shard_map/ppermute | solution.py:439
  37.0 4.0 %collective-permute-done.11.refs_4_ = f32[128,128]{1,0:T(8,128)S(1)} collective-permute-done((f32[128,128]{1,0:T(8,128)S(1)}, f32[128,128]{1,0:T(8,128)S(1)}, u32[]{:S(2)}, u32[]{:S(2)}) %collective-permute-start.11) | collective-permute-done | bytes 65568 | tf_op jit(solution)/shard_map/ppermute | solution.py:439
  41.1 2.3 %collective-permute-start.13 = (f32[256,128]{1,0:T(8,128)S(1)}, f32[256,128]{1,0:T(8,128)S(1)}, u32[]{:S(2)}, u32[]{:S(2)}) collective-permute-start(f32[256,128]{1,0:T(8,128)S(1)} %get-tuple-element.74), channel_id=1, source_target_pairs={{0,6},{1,7},{2,4},{3,5},{4,2},{5,3},{6,0},{7,1},{8,14},{9,15},{10,... | collective-permute-start | bytes 393224 | tf_op jit(solution)/shard_map/ppermute | solution.py:439
  45.8 2.2 %collective-permute-done.13.refs_5_ = f32[256,128]{1,0:T(8,128)S(1)} collective-permute-done((f32[256,128]{1,0:T(8,128)S(1)}, f32[256,128]{1,0:T(8,128)S(1)}, u32[]{:S(2)}, u32[]{:S(2)}) %collective-permute-start.13) | collective-permute-done | bytes 131104 | tf_op jit(solution)/shard_map/ppermute | solution.py:439
  50.5 2.6 %collective-permute-done.16.refs_3_ = f32[2560,128]{1,0:T(8,128)S(1)} collective-permute-done((f32[2560,128]{1,0:T(8,128)S(1)}, f32[2560,128]{1,0:T(8,128)S(1)}, u32[]{:S(2)}, u32[]{:S(2)}) %collective-permute-start.16) | collective-permute-done | bytes 1310752 | tf_op jit(solution)/shard_map/ppermute | solution.py:439
  53.8 1.5 %collective-permute-start.19 = (f32[192,256]{1,0:T(8,128)S(1)}, f32[192,256]{1,0:T(8,128)S(1)}, u32[]{:S(2)}, u32[]{:S(2)}) collective-permute-start(f32[192,256]{1,0:T(8,128)S(1)} %get-tuple-element.83.refs_2_.refs_1_), channel_id=1, source_target_pairs={{0,16},{16,0},{1,17},{17,1},{2,18},{18,2},{3,19},{19,3},{4,20},{20... | collective-permute-start | bytes 589832 | tf_op jit(solution)/shard_map/ppermute | solution.py:442
  55.4 5.6 %collective-permute-done.19.refs_3_ = f32[192,256]{1,0:T(8,128)S(1)} collective-permute-done((f32[192,256]{1,0:T(8,128)S(1)}, f32[192,256]{1,0:T(8,128)S(1)}, u32[]{:S(2)}, u32[]{:S(2)}) %collective-permute-start.19) | collective-permute-done | bytes 196640 | tf_op jit(solution)/shard_map/ppermute | solution.py:442
  61.0 1.4 %shard_map.91 = (bf16[192,2560]{1,0:T(8,128)(2,1)}, f32[8,128]{1,0:T(8,128)S(1)}) custom-call(f32[192,2560]{1,0:T(8,128)S(1)} %get-tuple-element.58.refs_0_, f32[192,2560]{1,0:T(8,128)S(1)} %get-tuple-element.59.refs_1_, bf16[192,256]{1,0:T(8,128)(2,1)S(1)} %get-tuple-element.47.refs_2_.refs_4_, bf16[1280,128]{1,0:T(8,128)(2,1)S(1)} %get-tuple-element.79.refs_3_, ...), custom_call_target="tpu_custom_call" | custom-call | flops 1000 | bytes 1000 | tf_op jit(solution)/shard_map/pallas_call | solution.py:423
  63.4 1.6 %collective-permute-start.21 = (f32[160,256]{1,0:T(8,128)S(1)}, f32[160,256]{1,0:T(8,128)S(1)}, u32[]{:S(2)}, u32[]{:S(2)}) collective-permute-start(f32[160,256]{1,0:T(8,128)S(1)} %get-tuple-element.87), channel_id=1, source_target_pairs={{0,6},{1,7},{2,4},{3,5},{4,2},{5,3},{6,0},{7,1},{8,14},{9,15},{10,... | collective-permute-start | bytes 491528 | tf_op jit(solution)/shard_map/ppermute | solution.py:439
  66.9 4.4 %collective-permute-done.21.refs_1_ = f32[160,256]{1,0:T(8,128)S(1)} collective-permute-done((f32[160,256]{1,0:T(8,128)S(1)}, f32[160,256]{1,0:T(8,128)S(1)}, u32[]{:S(2)}, u32[]{:S(2)}) %collective-permute-start.21) | collective-permute-done | bytes 163872 | tf_op jit(solution)/shard_map/ppermute | solution.py:439
  71.4 3.1 %collective-permute-done.22.refs_2_ = f32[160,256]{1,0:T(8,128)S(1)} collective-permute-done((f32[160,256]{1,0:T(8,128)S(1)}, f32[160,256]{1,0:T(8,128)S(1)}, u32[]{:S(2)}, u32[]{:S(2)}) %collective-permute-start.22) | collective-permute-done | bytes 163872 | tf_op jit(solution)/shard_map/ppermute | solution.py:439
  74.5 2.3 %collective-permute-start.24 = (f32[80,256]{1,0:T(8,128)S(1)}, f32[80,256]{1,0:T(8,128)S(1)}, u32[]{:S(2)}, u32[]{:S(2)}) collective-permute-start(f32[80,256]{1,0:T(8,128)S(1)} %get-tuple-element.91), channel_id=1, source_target_pairs={{0,8},{1,9},{2,10},{3,11},{4,12},{5,13},{6,14},{7,15},{8,0},{9,1},... | collective-permute-start | bytes 245768 | tf_op jit(solution)/shard_map/ppermute | solution.py:439
  76.8 4.8 %collective-permute-done.24 = f32[80,256]{1,0:T(8,128)S(1)} collective-permute-done((f32[80,256]{1,0:T(8,128)S(1)}, f32[80,256]{1,0:T(8,128)S(1)}, u32[]{:S(2)}, u32[]{:S(2)}) %collective-permute-start.24) | collective-permute-done | bytes 81952 | tf_op jit(solution)/shard_map/ppermute | solution.py:439
  (53 shorter events, 15.2 us)
Async XLA Ops:
  5.2 4.4 %collective-permute-start = (f32[2592,128]{1,0:T(8,128)S(1)}, f32[2592,128]{1,0:T(8,128)S(1)}, u32[]{:S(2)}, u32[]{:S(2)}) collective-permute-start(f32[2592,128]{1,0:T(8,128)S(1)} %get-tuple-element.54), channel_id=1, source_target_pairs={{0,1},{1,0},{2,3},{3,2},{4,5},{5,4},{6,7},{7,6},{8,9},{9,8},{10,11... | collective-permute-start | bytes 3981320 | tf_op jit(solution)/shard_map/ppermute | solution.py:439
  6.9 30.1 %collective-permute-start.12 = (f32[1920,128]{1,0:T(8,128)S(1)}, f32[1920,128]{1,0:T(8,128)S(1)}, u32[]{:S(2)}, u32[]{:S(2)}) collective-permute-start(f32[1920,128]{1,0:T(8,128)S(1)} %get-tuple-element.72), channel_id=1, source_target_pairs={{0,16},{16,0},{1,17},{17,1},{2,18},{18,2},{3,19},{19,3},{4,20},{20... | collective-permute-start | bytes 2949128 | tf_op jit(solution)/shard_map/ppermute | solution.py:442
  9.7 8.8 %collective-permute-start.1 = (f32[392,128]{1,0:T(8,128)S(1)}, f32[392,128]{1,0:T(8,128)S(1)}, u32[]{:S(2)}, u32[]{:S(2)}) collective-permute-start(f32[392,128]{1,0:T(8,128)S(1)} %get-tuple-element.61), channel_id=1, source_target_pairs={{0,6},{1,7},{2,4},{3,5},{4,2},{5,3},{6,0},{7,1},{8,14},{9,15},{10,... | collective-permute-start | bytes 602120 | tf_op jit(solution)/shard_map/ppermute | solution.py:439
  12.4 10.4 %collective-permute-start.2 = (f32[392,128]{1,0:T(8,128)S(1)}, f32[392,128]{1,0:T(8,128)S(1)}, u32[]{:S(2)}, u32[]{:S(2)}) collective-permute-start(f32[392,128]{1,0:T(8,128)S(1)} %get-tuple-element.62), channel_id=1, source_target_pairs={{0,2},{1,3},{2,0},{3,1},{4,6},{5,7},{6,4},{7,5},{8,10},{9,11},{10,... | collective-permute-start | bytes 602120 | tf_op jit(solution)/shard_map/ppermute | solution.py:439
  13.0 11.7 %collective-permute-start.3 = (f32[392,128]{1,0:T(8,128)S(1)}, f32[392,128]{1,0:T(8,128)S(1)}, u32[]{:S(2)}, u32[]{:S(2)}) collective-permute-start(f32[392,128]{1,0:T(8,128)S(1)} %get-tuple-element.63), channel_id=1, source_target_pairs={{0,4},{1,5},{2,6},{3,7},{4,0},{5,1},{6,2},{7,3},{8,12},{9,13},{10,... | collective-permute-start | bytes 602120 | tf_op jit(solution)/shard_map/ppermute | solution.py:439
  18.6 8.8 %collective-permute-start.5 = (f32[264,128]{1,0:T(8,128)S(1)}, f32[264,128]{1,0:T(8,128)S(1)}, u32[]{:S(2)}, u32[]{:S(2)}) collective-permute-start(f32[264,128]{1,0:T(8,128)S(1)} %get-tuple-element.65), channel_id=1, source_target_pairs={{0,6},{1,7},{2,4},{3,5},{4,2},{5,3},{6,0},{7,1},{8,14},{9,15},{10,... | collective-permute-start | bytes 405512 | tf_op jit(solution)/shard_map/ppermute | solution.py:439
  21.4 6.5 %collective-permute-start.6 = (f32[264,128]{1,0:T(8,128)S(1)}, f32[264,128]{1,0:T(8,128)S(1)}, u32[]{:S(2)}, u32[]{:S(2)}) collective-permute-start(f32[264,128]{1,0:T(8,128)S(1)} %get-tuple-element.66), channel_id=1, source_target_pairs={{0,2},{1,3},{2,0},{3,1},{4,6},{5,7},{6,4},{7,5},{8,10},{9,11},{10,... | collective-permute-start | bytes 405512 | tf_op jit(solution)/shard_map/ppermute | solution.py:439
  22.9 6.4 %collective-permute-start.7 = (f32[264,128]{1,0:T(8,128)S(1)}, f32[264,128]{1,0:T(8,128)S(1)}, u32[]{:S(2)}, u32[]{:S(2)}) collective-permute-start(f32[264,128]{1,0:T(8,128)S(1)} %get-tuple-element.67), channel_id=1, source_target_pairs={{0,4},{1,5},{2,6},{3,7},{4,0},{5,1},{6,2},{7,3},{8,12},{9,13},{10,... | collective-permute-start | bytes 405512 | tf_op jit(solution)/shard_map/ppermute | solution.py:439
  24.8 6.6 %collective-permute-start.4 = (f32[192,128]{1,0:T(8,128)S(1)}, f32[192,128]{1,0:T(8,128)S(1)}, u32[]{:S(2)}, u32[]{:S(2)}) collective-permute-start(f32[192,128]{1,0:T(8,128)S(1)} %shard_map.83.refs_4_), channel_id=1, source_target_pairs={{0,8},{1,9},{2,10},{3,11},{4,12},{5,13},{6,14},{7,15},{8,0},{9,1},... | collective-permute-start | bytes 294920 | tf_op jit(solution)/shard_map/ppermute | solution.py:439
  31.5 9.5 %collective-permute-start.8 = (f32[384,128]{1,0:T(8,128)S(1)}, f32[384,128]{1,0:T(8,128)S(1)}, u32[]{:S(2)}, u32[]{:S(2)}) collective-permute-start(f32[384,128]{1,0:T(8,128)S(1)} %get-tuple-element.69), channel_id=1, source_target_pairs={{0,6},{1,7},{2,4},{3,5},{4,2},{5,3},{6,0},{7,1},{8,14},{9,15},{10,... | collective-permute-start | bytes 589832 | tf_op jit(solution)/shard_map/ppermute | solution.py:439
  34.2 6.8 %collective-permute-start.11 = (f32[128,128]{1,0:T(8,128)S(1)}, f32[128,128]{1,0:T(8,128)S(1)}, u32[]{:S(2)}, u32[]{:S(2)}) collective-permute-start(f32[128,128]{1,0:T(8,128)S(1)} %shard_map.84.refs_5_), channel_id=1, source_target_pairs={{0,8},{1,9},{2,10},{3,11},{4,12},{5,13},{6,14},{7,15},{8,0},{9,1},... | collective-permute-start | bytes 196616 | tf_op jit(solution)/shard_map/ppermute | solution.py:439
  36.1 9.1 %collective-permute-start.9 = (f32[384,128]{1,0:T(8,128)S(1)}, f32[384,128]{1,0:T(8,128)S(1)}, u32[]{:S(2)}, u32[]{:S(2)}) collective-permute-start(f32[384,128]{1,0:T(8,128)S(1)} %get-tuple-element.70), channel_id=1, source_target_pairs={{0,2},{1,3},{2,0},{3,1},{4,6},{5,7},{6,4},{7,5},{8,10},{9,11},{10,... | collective-permute-start | bytes 589832 | tf_op jit(solution)/shard_map/ppermute | solution.py:439
  37.0 8.8 %collective-permute-start.10 = (f32[384,128]{1,0:T(8,128)S(1)}, f32[384,128]{1,0:T(8,128)S(1)}, u32[]{:S(2)}, u32[]{:S(2)}) collective-permute-start(f32[384,128]{1,0:T(8,128)S(1)} %get-tuple-element.71), channel_id=1, source_target_pairs={{0,4},{1,5},{2,6},{3,7},{4,0},{5,1},{6,2},{7,3},{8,12},{9,13},{10,... | collective-permute-start | bytes 589832 | tf_op jit(solution)/shard_map/ppermute | solution.py:439
  41.1 6.9 %collective-permute-start.13 = (f32[256,128]{1,0:T(8,128)S(1)}, f32[256,128]{1,0:T(8,128)S(1)}, u32[]{:S(2)}, u32[]{:S(2)}) collective-permute-start(f32[256,128]{1,0:T(8,128)S(1)} %get-tuple-element.74), channel_id=1, source_target_pairs={{0,6},{1,7},{2,4},{3,5},{4,2},{5,3},{6,0},{7,1},{8,14},{9,15},{10,... | collective-permute-start | bytes 393224 | tf_op jit(solution)/shard_map/ppermute | solution.py:439
  43.5 5.7 %collective-permute-start.14 = (f32[256,128]{1,0:T(8,128)S(1)}, f32[256,128]{1,0:T(8,128)S(1)}, u32[]{:S(2)}, u32[]{:S(2)}) collective-permute-start(f32[256,128]{1,0:T(8,128)S(1)} %get-tuple-element.75), channel_id=1, source_target_pairs={{0,2},{1,3},{2,0},{3,1},{4,6},{5,7},{6,4},{7,5},{8,10},{9,11},{10,... | collective-permute-start | bytes 393224 | tf_op jit(solution)/shard_map/ppermute | solution.py:439
  44.7 5.0 %collective-permute-start.15 = (f32[256,128]{1,0:T(8,128)S(1)}, f32[256,128]{1,0:T(8,128)S(1)}, u32[]{:S(2)}, u32[]{:S(2)}) collective-permute-start(f32[256,128]{1,0:T(8,128)S(1)} %get-tuple-element.76), channel_id=1, source_target_pairs={{0,4},{1,5},{2,6},{3,7},{4,0},{5,1},{6,2},{7,3},{8,12},{9,13},{10,... | collective-permute-start | bytes 393224 | tf_op jit(solution)/shard_map/ppermute | solution.py:439
  50.0 3.1 %collective-permute-start.16 = (f32[2560,128]{1,0:T(8,128)S(1)}, f32[2560,128]{1,0:T(8,128)S(1)}, u32[]{:S(2)}, u32[]{:S(2)}) collective-permute-start(f32[2560,128]{1,0:T(8,128)S(1)} %get-tuple-element.78.refs_4_), channel_id=1, source_target_pairs={{0,1},{1,0},{2,3},{3,2},{4,5},{5,4},{6,7},{7,6},{8,9},{9,8},{10,11... | collective-permute-start | bytes 3932168 | tf_op jit(solution)/shard_map/ppermute | solution.py:439
  53.6 8.8 %collective-permute-start.17 = (f32[1920,128]{1,0:T(8,128)S(1)}, f32[1920,128]{1,0:T(8,128)S(1)}, u32[]{:S(2)}, u32[]{:S(2)}) collective-permute-start(f32[1920,128]{1,0:T(8,128)S(1)} %shard_map.90.refs_5_), channel_id=1, source_target_pairs={{0,1},{1,0},{2,3},{3,2},{4,5},{5,4},{6,7},{7,6},{8,9},{9,8},{10,11... | collective-permute-start | bytes 2949128 | tf_op jit(solution)/shard_map/ppermute | solution.py:439
  53.8 7.2 %collective-permute-start.19 = (f32[192,256]{1,0:T(8,128)S(1)}, f32[192,256]{1,0:T(8,128)S(1)}, u32[]{:S(2)}, u32[]{:S(2)}) collective-permute-start(f32[192,256]{1,0:T(8,128)S(1)} %get-tuple-element.83.refs_2_.refs_1_), channel_id=1, source_target_pairs={{0,16},{16,0},{1,17},{17,1},{2,18},{18,2},{3,19},{19,3},{4,20},{20... | collective-permute-start | bytes 589832 | tf_op jit(solution)/shard_map/ppermute | solution.py:442
  55.3 7.4 %collective-permute-start.18 = (f32[192,256]{1,0:T(8,128)S(1)}, f32[192,256]{1,0:T(8,128)S(1)}, u32[]{:S(2)}, u32[]{:S(2)}) collective-permute-start(f32[192,256]{1,0:T(8,128)S(1)} %get-tuple-element.83.refs_2_.refs_1_), channel_id=1, source_target_pairs={{0,1},{1,0},{2,3},{3,2},{4,5},{5,4},{6,7},{7,6},{8,9},{9,8},{10,11... | collective-permute-start | bytes 589832 | tf_op jit(solution)/shard_map/ppermute | solution.py:439
  63.4 8.0 %collective-permute-start.21 = (f32[160,256]{1,0:T(8,128)S(1)}, f32[160,256]{1,0:T(8,128)S(1)}, u32[]{:S(2)}, u32[]{:S(2)}) collective-permute-start(f32[160,256]{1,0:T(8,128)S(1)} %get-tuple-element.87), channel_id=1, source_target_pairs={{0,6},{1,7},{2,4},{3,5},{4,2},{5,3},{6,0},{7,1},{8,14},{9,15},{10,... | collective-permute-start | bytes 491528 | tf_op jit(solution)/shard_map/ppermute | solution.py:439
  65.0 9.5 %collective-permute-start.22 = (f32[160,256]{1,0:T(8,128)S(1)}, f32[160,256]{1,0:T(8,128)S(1)}, u32[]{:S(2)}, u32[]{:S(2)}) collective-permute-start(f32[160,256]{1,0:T(8,128)S(1)} %get-tuple-element.88), channel_id=1, source_target_pairs={{0,2},{1,3},{2,0},{3,1},{4,6},{5,7},{6,4},{7,5},{8,10},{9,11},{10,... | collective-permute-start | bytes 491528 | tf_op jit(solution)/shard_map/ppermute | solution.py:439
  66.2 8.3 %collective-permute-start.23 = (f32[160,256]{1,0:T(8,128)S(1)}, f32[160,256]{1,0:T(8,128)S(1)}, u32[]{:S(2)}, u32[]{:S(2)}) collective-permute-start(f32[160,256]{1,0:T(8,128)S(1)} %get-tuple-element.89), channel_id=1, source_target_pairs={{0,4},{1,5},{2,6},{3,7},{4,0},{5,1},{6,2},{7,3},{8,12},{9,13},{10,... | collective-permute-start | bytes 491528 | tf_op jit(solution)/shard_map/ppermute | solution.py:439
  74.5 7.1 %collective-permute-start.24 = (f32[80,256]{1,0:T(8,128)S(1)}, f32[80,256]{1,0:T(8,128)S(1)}, u32[]{:S(2)}, u32[]{:S(2)}) collective-permute-start(f32[80,256]{1,0:T(8,128)S(1)} %get-tuple-element.91), channel_id=1, source_target_pairs={{0,8},{1,9},{2,10},{3,11},{4,12},{5,13},{6,14},{7,15},{8,0},{9,1},... | collective-permute-start | bytes 245768 | tf_op jit(solution)/shard_map/ppermute | solution.py:439
  (5 other events, 16.6 us)

commit v6 on v4

--- a/solution.py
+++ b/solution.py
@@ -104,7 +104,7 @@
     for copy in waves[0] + waves[1] + waves[2] + waves[3]:
         copy.wait()
     bc_out[...] = dot(normed[...], w_bc[...]).astype(bf16)
-    tile = width // 5
+    tile = width // 10
     for first in range(0, width, tile):
         lanes = slice(first, first + tile)
         u_out[:, lanes] = (spread(up, first, tile, width // heads) * cots[:, lanes].astype(f32)).astype(bf16)
@@ -453,7 +453,7 @@
             pltpu.VMEM((8, slot, LANES), f32), pltpu.VMEM(w_bc.shape, bf16),
             pltpu.VMEM(vals.shape, bf16), pltpu.VMEM(cots.shape, bf16), pltpu.VMEM(rate.shape, jnp.int32),
             pltpu.VMEM(starts.shape, jnp.int32),
-        ] + [pltpu.SemaphoreType.DMA((count,)) for count in (2, 4, 4, 4, 4)],
+        ] + [pltpu.SemaphoreType.DMA((count,)) for count in (2, 6, 8, 6, 6)],
         vmem=24, far=True,
     )
     recv = swap(message, 1)

time: 81.7 us -> 82 us (level)
  no operation moved by 1% of the time
where the time goes in v6:
time: 82 us; the launch traced here: 81.8 us
  waiting for transfers between devices  37.6 us (46%)
  starting transfers between devices  31.3 us (38%)
  Pallas kernels  11.5 us (14%)
    ppermute x23, waiting for transfers between devices, swap(): return lax.ppermute(array, 'seq', [(s, s ^ mask) for s in range(shards)])  32 us
    ppermute x23, starting transfers between devices, swap(): return lax.ppermute(array, 'seq', [(s, s ^ mask) for s in range(shards)])  27.1 us
    pallas_call x18, Pallas kernels, kernel(): pl.pallas_call(run, in_specs=[there] * count + [pl.BlockSpec(memory_space...  11.5 us
    ppermute x2, waiting for transfers between devices, swap_pack(): return lax.ppermute(array, 'dp', [(d, d ^ 1) for d in range(packs)])  5.57 us
    ppermute x2, starting transfers between devices, swap_pack(): return lax.ppermute(array, 'dp', [(d, d ^ 1) for d in range(packs)])  4.17 us
  transfers between devices with their start and end apart: 25, of which 16 were waited for; matrix products, arithmetic and copies ran while one was open for 0% of the time, Pallas kernels for 7%

profile of v6, /device:TPU:0, one launch (start us, length us, event | category | flops | bytes accessed | tf_op | source)
XLA Modules:
  0.0 81.8 jit_solution(7871957780721798056)
XLA Ops:
  0.6 4.1 %shard_map.77 = (f32[2592,128]{1,0:T(8,128)S(1)}, f32[8,8,128]{2,1,0:T(8,128)S(1)}, bf16[192,2560]{1,0:T(8,128)(2,1)S(1)}, bf16[192,2560]{1,0:T(8,128)(2,1)S(1)}...) custom-call(bf16[1,192,2560]{2,1,0:T(8,128)(2,1)} %refs_0_.1, bf16[2560,256]{1,0:T(8,128)(2,1)} %refs_1_.1, ...), custom_call_target="tpu_custom_call" | custom-call | flops 1000 | bytes 1000 | tf_op jit(solution)/shard_map/pallas_call | solution.py:421
  6.4 2.6 %collective-permute-start.12 = (f32[1920,128]{1,0:T(8,128)S(1)}, f32[1920,128]{1,0:T(8,128)S(1)}, u32[]{:S(2)}, u32[]{:S(2)}) collective-permute-start(f32[1920,128]{1,0:T(8,128)S(1)} %get-tuple-element.72), channel_id=1, source_target_pairs={{0,16},{16,0},{1,17},{17,1},{2,18},{18,2},{3,19},{19,3},{4,20},{20... | collective-permute-start | bytes 2949128 | tf_op jit(solution)/shard_map/ppermute | solution.py:440
  9.2 2.8 %collective-permute-start.1 = (f32[392,128]{1,0:T(8,128)S(1)}, f32[392,128]{1,0:T(8,128)S(1)}, u32[]{:S(2)}, u32[]{:S(2)}) collective-permute-start(f32[392,128]{1,0:T(8,128)S(1)} %get-tuple-element.61), channel_id=1, source_target_pairs={{0,6},{1,7},{2,4},{3,5},{4,2},{5,3},{6,0},{7,1},{8,14},{9,15},{10,... | collective-permute-start | bytes 602120 | tf_op jit(solution)/shard_map/ppermute | solution.py:437
  12.8 1.9 %shard_map.81 = (f32[192,2560]{1,0:T(8,128)S(1)}, f32[192,2560]{1,0:T(8,128)S(1)}, f32[192,256]{1,0:T(8,128)S(1)}) custom-call(bf16[192,2560]{1,0:T(8,128)(2,1)S(1)} %bitcast.4, bf16[192,2560]{1,0:T(8,128)(2,1)S(1)} %bitcast.5, s32[40,192]{1,0:T(8,128)S(1)} %bitcast.6, s32[1,192]{1,0:T(1,128)S(1)} %copy-done.3, ...), custom_call_target="tpu_custom_call" | custom-call | flops 1000 | bytes 1000 | tf_op jit(solution)/shard_map/pallas_call | solution.py:421
  14.7 3.4 %collective-permute-done.1.refs_5_.refs_1_ = f32[392,128]{1,0:T(8,128)S(1)} collective-permute-done((f32[392,128]{1,0:T(8,128)S(1)}, f32[392,128]{1,0:T(8,128)S(1)}, u32[]{:S(2)}, u32[]{:S(2)}) %collective-permute-start.1) | collective-permute-done | bytes 200736 | tf_op jit(solution)/shard_map/ppermute | solution.py:437
  18.1 2.8 %collective-permute-start.5 = (f32[264,128]{1,0:T(8,128)S(1)}, f32[264,128]{1,0:T(8,128)S(1)}, u32[]{:S(2)}, u32[]{:S(2)}) collective-permute-start(f32[264,128]{1,0:T(8,128)S(1)} %get-tuple-element.65), channel_id=1, source_target_pairs={{0,6},{1,7},{2,4},{3,5},{4,2},{5,3},{6,0},{7,1},{8,14},{9,15},{10,... | collective-permute-start | bytes 405512 | tf_op jit(solution)/shard_map/ppermute | solution.py:437
  22.4 1.8 %collective-permute-start.7 = (f32[264,128]{1,0:T(8,128)S(1)}, f32[264,128]{1,0:T(8,128)S(1)}, u32[]{:S(2)}, u32[]{:S(2)}) collective-permute-start(f32[264,128]{1,0:T(8,128)S(1)} %get-tuple-element.67), channel_id=1, source_target_pairs={{0,4},{1,5},{2,6},{3,7},{4,0},{5,1},{6,2},{7,3},{8,12},{9,13},{10,... | collective-permute-start | bytes 405512 | tf_op jit(solution)/shard_map/ppermute | solution.py:437
  24.3 2.7 %collective-permute-start.4 = (f32[192,128]{1,0:T(8,128)S(1)}, f32[192,128]{1,0:T(8,128)S(1)}, u32[]{:S(2)}, u32[]{:S(2)}) collective-permute-start(f32[192,128]{1,0:T(8,128)S(1)} %shard_map.83.refs_4_), channel_id=1, source_target_pairs={{0,8},{1,9},{2,10},{3,11},{4,12},{5,13},{6,14},{7,15},{8,0},{9,1},... | collective-permute-start | bytes 294920 | tf_op jit(solution)/shard_map/ppermute | solution.py:437
  27.4 1.4 %collective-permute-done.7.refs_3_ = f32[264,128]{1,0:T(8,128)S(1)} collective-permute-done((f32[264,128]{1,0:T(8,128)S(1)}, f32[264,128]{1,0:T(8,128)S(1)}, u32[]{:S(2)}, u32[]{:S(2)}) %collective-permute-start.7) | collective-permute-done | bytes 135200 | tf_op jit(solution)/shard_map/ppermute | solution.py:437
  28.8 2.0 %collective-permute-done.4.refs_4_ = f32[192,128]{1,0:T(8,128)S(1)} collective-permute-done((f32[192,128]{1,0:T(8,128)S(1)}, f32[192,128]{1,0:T(8,128)S(1)}, u32[]{:S(2)}, u32[]{:S(2)}) %collective-permute-start.4) | collective-permute-done | bytes 98336 | tf_op jit(solution)/shard_map/ppermute | solution.py:437
  31.0 2.7 %collective-permute-start.8 = (f32[384,128]{1,0:T(8,128)S(1)}, f32[384,128]{1,0:T(8,128)S(1)}, u32[]{:S(2)}, u32[]{:S(2)}) collective-permute-start(f32[384,128]{1,0:T(8,128)S(1)} %get-tuple-element.69), channel_id=1, source_target_pairs={{0,6},{1,7},{2,4},{3,5},{4,2},{5,3},{6,0},{7,1},{8,14},{9,15},{10,... | collective-permute-start | bytes 589832 | tf_op jit(solution)/shard_map/ppermute | solution.py:437
  33.8 1.9 %collective-permute-start.11 = (f32[128,128]{1,0:T(8,128)S(1)}, f32[128,128]{1,0:T(8,128)S(1)}, u32[]{:S(2)}, u32[]{:S(2)}) collective-permute-start(f32[128,128]{1,0:T(8,128)S(1)} %shard_map.84.refs_5_), channel_id=1, source_target_pairs={{0,8},{1,9},{2,10},{3,11},{4,12},{5,13},{6,14},{7,15},{8,0},{9,1},... | collective-permute-start | bytes 196616 | tf_op jit(solution)/shard_map/ppermute | solution.py:437
  36.5 4.0 %collective-permute-done.11.refs_4_ = f32[128,128]{1,0:T(8,128)S(1)} collective-permute-done((f32[128,128]{1,0:T(8,128)S(1)}, f32[128,128]{1,0:T(8,128)S(1)}, u32[]{:S(2)}, u32[]{:S(2)}) %collective-permute-start.11) | collective-permute-done | bytes 65568 | tf_op jit(solution)/shard_map/ppermute | solution.py:437
  40.7 2.3 %collective-permute-start.13 = (f32[256,128]{1,0:T(8,128)S(1)}, f32[256,128]{1,0:T(8,128)S(1)}, u32[]{:S(2)}, u32[]{:S(2)}) collective-permute-start(f32[256,128]{1,0:T(8,128)S(1)} %get-tuple-element.74), channel_id=1, source_target_pairs={{0,6},{1,7},{2,4},{3,5},{4,2},{5,3},{6,0},{7,1},{8,14},{9,15},{10,... | collective-permute-start | bytes 393224 | tf_op jit(solution)/shard_map/ppermute | solution.py:437
  45.4 2.2 %collective-permute-done.13.refs_5_ = f32[256,128]{1,0:T(8,128)S(1)} collective-permute-done((f32[256,128]{1,0:T(8,128)S(1)}, f32[256,128]{1,0:T(8,128)S(1)}, u32[]{:S(2)}, u32[]{:S(2)}) %collective-permute-start.13) | collective-permute-done | bytes 131104 | tf_op jit(solution)/shard_map/ppermute | solution.py:437
  50.0 2.6 %collective-permute-done.16.refs_3_ = f32[2560,128]{1,0:T(8,128)S(1)} collective-permute-done((f32[2560,128]{1,0:T(8,128)S(1)}, f32[2560,128]{1,0:T(8,128)S(1)}, u32[]{:S(2)}, u32[]{:S(2)}) %collective-permute-start.16) | collective-permute-done | bytes 1310752 | tf_op jit(solution)/shard_map/ppermute | solution.py:437
  53.3 1.5 %collective-permute-start.19 = (f32[192,256]{1,0:T(8,128)S(1)}, f32[192,256]{1,0:T(8,128)S(1)}, u32[]{:S(2)}, u32[]{:S(2)}) collective-permute-start(f32[192,256]{1,0:T(8,128)S(1)} %get-tuple-element.83.refs_2_.refs_1_), channel_id=1, source_target_pairs={{0,16},{16,0},{1,17},{17,1},{2,18},{18,2},{3,19},{19,3},{4,20},{20... | collective-permute-start | bytes 589832 | tf_op jit(solution)/shard_map/ppermute | solution.py:440
  55.0 5.6 %collective-permute-done.19.refs_3_ = f32[192,256]{1,0:T(8,128)S(1)} collective-permute-done((f32[192,256]{1,0:T(8,128)S(1)}, f32[192,256]{1,0:T(8,128)S(1)}, u32[]{:S(2)}, u32[]{:S(2)}) %collective-permute-start.19) | collective-permute-done | bytes 196640 | tf_op jit(solution)/shard_map/ppermute | solution.py:440
  60.5 1.4 %shard_map.91 = (bf16[192,2560]{1,0:T(8,128)(2,1)}, f32[8,128]{1,0:T(8,128)S(1)}) custom-call(f32[192,2560]{1,0:T(8,128)S(1)} %get-tuple-element.58.refs_0_, f32[192,2560]{1,0:T(8,128)S(1)} %get-tuple-element.59.refs_1_, bf16[192,256]{1,0:T(8,128)(2,1)S(1)} %get-tuple-element.47.refs_2_.refs_4_, bf16[1280,128]{1,0:T(8,128)(2,1)S(1)} %get-tuple-element.79.refs_3_, ...), custom_call_target="tpu_custom_call" | custom-call | flops 1000 | bytes 1000 | tf_op jit(solution)/shard_map/pallas_call | solution.py:421
  62.9 1.6 %collective-permute-start.21 = (f32[160,256]{1,0:T(8,128)S(1)}, f32[160,256]{1,0:T(8,128)S(1)}, u32[]{:S(2)}, u32[]{:S(2)}) collective-permute-start(f32[160,256]{1,0:T(8,128)S(1)} %get-tuple-element.87), channel_id=1, source_target_pairs={{0,6},{1,7},{2,4},{3,5},{4,2},{5,3},{6,0},{7,1},{8,14},{9,15},{10,... | collective-permute-start | bytes 491528 | tf_op jit(solution)/shard_map/ppermute | solution.py:437
  66.5 4.4 %collective-permute-done.21.refs_1_ = f32[160,256]{1,0:T(8,128)S(1)} collective-permute-done((f32[160,256]{1,0:T(8,128)S(1)}, f32[160,256]{1,0:T(8,128)S(1)}, u32[]{:S(2)}, u32[]{:S(2)}) %collective-permute-start.21) | collective-permute-done | bytes 163872 | tf_op jit(solution)/shard_map/ppermute | solution.py:437
  70.9 3.1 %collective-permute-done.22.refs_2_ = f32[160,256]{1,0:T(8,128)S(1)} collective-permute-done((f32[160,256]{1,0:T(8,128)S(1)}, f32[160,256]{1,0:T(8,128)S(1)}, u32[]{:S(2)}, u32[]{:S(2)}) %collective-permute-start.22) | collective-permute-done | bytes 163872 | tf_op jit(solution)/shard_map/ppermute | solution.py:437
  74.0 2.3 %collective-permute-start.24 = (f32[80,256]{1,0:T(8,128)S(1)}, f32[80,256]{1,0:T(8,128)S(1)}, u32[]{:S(2)}, u32[]{:S(2)}) collective-permute-start(f32[80,256]{1,0:T(8,128)S(1)} %get-tuple-element.91), channel_id=1, source_target_pairs={{0,8},{1,9},{2,10},{3,11},{4,12},{5,13},{6,14},{7,15},{8,0},{9,1},... | collective-permute-start | bytes 245768 | tf_op jit(solution)/shard_map/ppermute | solution.py:437
  76.3 4.8 %collective-permute-done.24 = f32[80,256]{1,0:T(8,128)S(1)} collective-permute-done((f32[80,256]{1,0:T(8,128)S(1)}, f32[80,256]{1,0:T(8,128)S(1)}, u32[]{:S(2)}, u32[]{:S(2)}) %collective-permute-start.24) | collective-permute-done | bytes 81952 | tf_op jit(solution)/shard_map/ppermute | solution.py:437
  (53 shorter events, 15.2 us)
Async XLA Ops:
  4.7 4.4 %collective-permute-start = (f32[2592,128]{1,0:T(8,128)S(1)}, f32[2592,128]{1,0:T(8,128)S(1)}, u32[]{:S(2)}, u32[]{:S(2)}) collective-permute-start(f32[2592,128]{1,0:T(8,128)S(1)} %get-tuple-element.54), channel_id=1, source_target_pairs={{0,1},{1,0},{2,3},{3,2},{4,5},{5,4},{6,7},{7,6},{8,9},{9,8},{10,11... | collective-permute-start | bytes 3981320 | tf_op jit(solution)/shard_map/ppermute | solution.py:437
  6.4 30.1 %collective-permute-start.12 = (f32[1920,128]{1,0:T(8,128)S(1)}, f32[1920,128]{1,0:T(8,128)S(1)}, u32[]{:S(2)}, u32[]{:S(2)}) collective-permute-start(f32[1920,128]{1,0:T(8,128)S(1)} %get-tuple-element.72), channel_id=1, source_target_pairs={{0,16},{16,0},{1,17},{17,1},{2,18},{18,2},{3,19},{19,3},{4,20},{20... | collective-permute-start | bytes 2949128 | tf_op jit(solution)/shard_map/ppermute | solution.py:440
  9.2 8.8 %collective-permute-start.1 = (f32[392,128]{1,0:T(8,128)S(1)}, f32[392,128]{1,0:T(8,128)S(1)}, u32[]{:S(2)}, u32[]{:S(2)}) collective-permute-start(f32[392,128]{1,0:T(8,128)S(1)} %get-tuple-element.61), channel_id=1, source_target_pairs={{0,6},{1,7},{2,4},{3,5},{4,2},{5,3},{6,0},{7,1},{8,14},{9,15},{10,... | collective-permute-start | bytes 602120 | tf_op jit(solution)/shard_map/ppermute | solution.py:437
  12.0 10.4 %collective-permute-start.2 = (f32[392,128]{1,0:T(8,128)S(1)}, f32[392,128]{1,0:T(8,128)S(1)}, u32[]{:S(2)}, u32[]{:S(2)}) collective-permute-start(f32[392,128]{1,0:T(8,128)S(1)} %get-tuple-element.62), channel_id=1, source_target_pairs={{0,2},{1,3},{2,0},{3,1},{4,6},{5,7},{6,4},{7,5},{8,10},{9,11},{10,... | collective-permute-start | bytes 602120 | tf_op jit(solution)/shard_map/ppermute | solution.py:437
  12.5 11.7 %collective-permute-start.3 = (f32[392,128]{1,0:T(8,128)S(1)}, f32[392,128]{1,0:T(8,128)S(1)}, u32[]{:S(2)}, u32[]{:S(2)}) collective-permute-start(f32[392,128]{1,0:T(8,128)S(1)} %get-tuple-element.63), channel_id=1, source_target_pairs={{0,4},{1,5},{2,6},{3,7},{4,0},{5,1},{6,2},{7,3},{8,12},{9,13},{10,... | collective-permute-start | bytes 602120 | tf_op jit(solution)/shard_map/ppermute | solution.py:437
  18.1 8.8 %collective-permute-start.5 = (f32[264,128]{1,0:T(8,128)S(1)}, f32[264,128]{1,0:T(8,128)S(1)}, u32[]{:S(2)}, u32[]{:S(2)}) collective-permute-start(f32[264,128]{1,0:T(8,128)S(1)} %get-tuple-element.65), channel_id=1, source_target_pairs={{0,6},{1,7},{2,4},{3,5},{4,2},{5,3},{6,0},{7,1},{8,14},{9,15},{10,... | collective-permute-start | bytes 405512 | tf_op jit(solution)/shard_map/ppermute | solution.py:437
  20.9 6.5 %collective-permute-start.6 = (f32[264,128]{1,0:T(8,128)S(1)}, f32[264,128]{1,0:T(8,128)S(1)}, u32[]{:S(2)}, u32[]{:S(2)}) collective-permute-start(f32[264,128]{1,0:T(8,128)S(1)} %get-tuple-element.66), channel_id=1, source_target_pairs={{0,2},{1,3},{2,0},{3,1},{4,6},{5,7},{6,4},{7,5},{8,10},{9,11},{10,... | collective-permute-start | bytes 405512 | tf_op jit(solution)/shard_map/ppermute | solution.py:437
  22.4 6.4 %collective-permute-start.7 = (f32[264,128]{1,0:T(8,128)S(1)}, f32[264,128]{1,0:T(8,128)S(1)}, u32[]{:S(2)}, u32[]{:S(2)}) collective-permute-start(f32[264,128]{1,0:T(8,128)S(1)} %get-tuple-element.67), channel_id=1, source_target_pairs={{0,4},{1,5},{2,6},{3,7},{4,0},{5,1},{6,2},{7,3},{8,12},{9,13},{10,... | collective-permute-start | bytes 405512 | tf_op jit(solution)/shard_map/ppermute | solution.py:437
  24.3 6.6 %collective-permute-start.4 = (f32[192,128]{1,0:T(8,128)S(1)}, f32[192,128]{1,0:T(8,128)S(1)}, u32[]{:S(2)}, u32[]{:S(2)}) collective-permute-start(f32[192,128]{1,0:T(8,128)S(1)} %shard_map.83.refs_4_), channel_id=1, source_target_pairs={{0,8},{1,9},{2,10},{3,11},{4,12},{5,13},{6,14},{7,15},{8,0},{9,1},... | collective-permute-start | bytes 294920 | tf_op jit(solution)/shard_map/ppermute | solution.py:437
  31.0 9.5 %collective-permute-start.8 = (f32[384,128]{1,0:T(8,128)S(1)}, f32[384,128]{1,0:T(8,128)S(1)}, u32[]{:S(2)}, u32[]{:S(2)}) collective-permute-start(f32[384,128]{1,0:T(8,128)S(1)} %get-tuple-element.69), channel_id=1, source_target_pairs={{0,6},{1,7},{2,4},{3,5},{4,2},{5,3},{6,0},{7,1},{8,14},{9,15},{10,... | collective-permute-start | bytes 589832 | tf_op jit(solution)/shard_map/ppermute | solution.py:437
  33.8 6.8 %collective-permute-start.11 = (f32[128,128]{1,0:T(8,128)S(1)}, f32[128,128]{1,0:T(8,128)S(1)}, u32[]{:S(2)}, u32[]{:S(2)}) collective-permute-start(f32[128,128]{1,0:T(8,128)S(1)} %shard_map.84.refs_5_), channel_id=1, source_target_pairs={{0,8},{1,9},{2,10},{3,11},{4,12},{5,13},{6,14},{7,15},{8,0},{9,1},... | collective-permute-start | bytes 196616 | tf_op jit(solution)/shard_map/ppermute | solution.py:437
  35.6 9.1 %collective-permute-start.9 = (f32[384,128]{1,0:T(8,128)S(1)}, f32[384,128]{1,0:T(8,128)S(1)}, u32[]{:S(2)}, u32[]{:S(2)}) collective-permute-start(f32[384,128]{1,0:T(8,128)S(1)} %get-tuple-element.70), channel_id=1, source_target_pairs={{0,2},{1,3},{2,0},{3,1},{4,6},{5,7},{6,4},{7,5},{8,10},{9,11},{10,... | collective-permute-start | bytes 589832 | tf_op jit(solution)/shard_map/ppermute | solution.py:437
  36.5 8.8 %collective-permute-start.10 = (f32[384,128]{1,0:T(8,128)S(1)}, f32[384,128]{1,0:T(8,128)S(1)}, u32[]{:S(2)}, u32[]{:S(2)}) collective-permute-start(f32[384,128]{1,0:T(8,128)S(1)} %get-tuple-element.71), channel_id=1, source_target_pairs={{0,4},{1,5},{2,6},{3,7},{4,0},{5,1},{6,2},{7,3},{8,12},{9,13},{10,... | collective-permute-start | bytes 589832 | tf_op jit(solution)/shard_map/ppermute | solution.py:437
  40.7 6.9 %collective-permute-start.13 = (f32[256,128]{1,0:T(8,128)S(1)}, f32[256,128]{1,0:T(8,128)S(1)}, u32[]{:S(2)}, u32[]{:S(2)}) collective-permute-start(f32[256,128]{1,0:T(8,128)S(1)} %get-tuple-element.74), channel_id=1, source_target_pairs={{0,6},{1,7},{2,4},{3,5},{4,2},{5,3},{6,0},{7,1},{8,14},{9,15},{10,... | collective-permute-start | bytes 393224 | tf_op jit(solution)/shard_map/ppermute | solution.py:437
  43.0 5.7 %collective-permute-start.14 = (f32[256,128]{1,0:T(8,128)S(1)}, f32[256,128]{1,0:T(8,128)S(1)}, u32[]{:S(2)}, u32[]{:S(2)}) collective-permute-start(f32[256,128]{1,0:T(8,128)S(1)} %get-tuple-element.75), channel_id=1, source_target_pairs={{0,2},{1,3},{2,0},{3,1},{4,6},{5,7},{6,4},{7,5},{8,10},{9,11},{10,... | collective-permute-start | bytes 393224 | tf_op jit(solution)/shard_map/ppermute | solution.py:437
  44.2 5.0 %collective-permute-start.15 = (f32[256,128]{1,0:T(8,128)S(1)}, f32[256,128]{1,0:T(8,128)S(1)}, u32[]{:S(2)}, u32[]{:S(2)}) collective-permute-start(f32[256,128]{1,0:T(8,128)S(1)} %get-tuple-element.76), channel_id=1, source_target_pairs={{0,4},{1,5},{2,6},{3,7},{4,0},{5,1},{6,2},{7,3},{8,12},{9,13},{10,... | collective-permute-start | bytes 393224 | tf_op jit(solution)/shard_map/ppermute | solution.py:437
  49.5 3.1 %collective-permute-start.16 = (f32[2560,128]{1,0:T(8,128)S(1)}, f32[2560,128]{1,0:T(8,128)S(1)}, u32[]{:S(2)}, u32[]{:S(2)}) collective-permute-start(f32[2560,128]{1,0:T(8,128)S(1)} %get-tuple-element.78.refs_4_), channel_id=1, source_target_pairs={{0,1},{1,0},{2,3},{3,2},{4,5},{5,4},{6,7},{7,6},{8,9},{9,8},{10,11... | collective-permute-start | bytes 3932168 | tf_op jit(solution)/shard_map/ppermute | solution.py:437
  53.1 8.8 %collective-permute-start.17 = (f32[1920,128]{1,0:T(8,128)S(1)}, f32[1920,128]{1,0:T(8,128)S(1)}, u32[]{:S(2)}, u32[]{:S(2)}) collective-permute-start(f32[1920,128]{1,0:T(8,128)S(1)} %shard_map.90.refs_5_), channel_id=1, source_target_pairs={{0,1},{1,0},{2,3},{3,2},{4,5},{5,4},{6,7},{7,6},{8,9},{9,8},{10,11... | collective-permute-start | bytes 2949128 | tf_op jit(solution)/shard_map/ppermute | solution.py:437
  53.3 7.2 %collective-permute-start.19 = (f32[192,256]{1,0:T(8,128)S(1)}, f32[192,256]{1,0:T(8,128)S(1)}, u32[]{:S(2)}, u32[]{:S(2)}) collective-permute-start(f32[192,256]{1,0:T(8,128)S(1)} %get-tuple-element.83.refs_2_.refs_1_), channel_id=1, source_target_pairs={{0,16},{16,0},{1,17},{17,1},{2,18},{18,2},{3,19},{19,3},{4,20},{20... | collective-permute-start | bytes 589832 | tf_op jit(solution)/shard_map/ppermute | solution.py:440
  54.9 7.4 %collective-permute-start.18 = (f32[192,256]{1,0:T(8,128)S(1)}, f32[192,256]{1,0:T(8,128)S(1)}, u32[]{:S(2)}, u32[]{:S(2)}) collective-permute-start(f32[192,256]{1,0:T(8,128)S(1)} %get-tuple-element.83.refs_2_.refs_1_), channel_id=1, source_target_pairs={{0,1},{1,0},{2,3},{3,2},{4,5},{5,4},{6,7},{7,6},{8,9},{9,8},{10,11... | collective-permute-start | bytes 589832 | tf_op jit(solution)/shard_map/ppermute | solution.py:437
  62.9 8.0 %collective-permute-start.21 = (f32[160,256]{1,0:T(8,128)S(1)}, f32[160,256]{1,0:T(8,128)S(1)}, u32[]{:S(2)}, u32[]{:S(2)}) collective-permute-start(f32[160,256]{1,0:T(8,128)S(1)} %get-tuple-element.87), channel_id=1, source_target_pairs={{0,6},{1,7},{2,4},{3,5},{4,2},{5,3},{6,0},{7,1},{8,14},{9,15},{10,... | collective-permute-start | bytes 491528 | tf_op jit(solution)/shard_map/ppermute | solution.py:437
  64.5 9.5 %collective-permute-start.22 = (f32[160,256]{1,0:T(8,128)S(1)}, f32[160,256]{1,0:T(8,128)S(1)}, u32[]{:S(2)}, u32[]{:S(2)}) collective-permute-start(f32[160,256]{1,0:T(8,128)S(1)} %get-tuple-element.88), channel_id=1, source_target_pairs={{0,2},{1,3},{2,0},{3,1},{4,6},{5,7},{6,4},{7,5},{8,10},{9,11},{10,... | collective-permute-start | bytes 491528 | tf_op jit(solution)/shard_map/ppermute | solution.py:437
  65.7 8.3 %collective-permute-start.23 = (f32[160,256]{1,0:T(8,128)S(1)}, f32[160,256]{1,0:T(8,128)S(1)}, u32[]{:S(2)}, u32[]{:S(2)}) collective-permute-start(f32[160,256]{1,0:T(8,128)S(1)} %get-tuple-element.89), channel_id=1, source_target_pairs={{0,4},{1,5},{2,6},{3,7},{4,0},{5,1},{6,2},{7,3},{8,12},{9,13},{10,... | collective-permute-start | bytes 491528 | tf_op jit(solution)/shard_map/ppermute | solution.py:437
  74.0 7.1 %collective-permute-start.24 = (f32[80,256]{1,0:T(8,128)S(1)}, f32[80,256]{1,0:T(8,128)S(1)}, u32[]{:S(2)}, u32[]{:S(2)}) collective-permute-start(f32[80,256]{1,0:T(8,128)S(1)} %get-tuple-element.91), channel_id=1, source_target_pairs={{0,8},{1,9},{2,10},{3,11},{4,12},{5,13},{6,14},{7,15},{8,0},{9,1},... | collective-permute-start | bytes 245768 | tf_op jit(solution)/shard_map/ppermute | solution.py:437
  (5 other events, 16.6 us)

commit v7 on v4

--- a/solution.py
+++ b/solution.py
@@ -453,7 +453,7 @@
             pltpu.VMEM((8, slot, LANES), f32), pltpu.VMEM(w_bc.shape, bf16),
             pltpu.VMEM(vals.shape, bf16), pltpu.VMEM(cots.shape, bf16), pltpu.VMEM(rate.shape, jnp.int32),
             pltpu.VMEM(starts.shape, jnp.int32),
-        ] + [pltpu.SemaphoreType.DMA((count,)) for count in (2, 4, 4, 4, 4)],
+        ] + [pltpu.SemaphoreType.DMA((count,)) for count in (2, 2, 2, 2, 2)],
         vmem=24, far=True,
     )
     recv = swap(message, 1)

time: 81.7 us -> 81.7 us (level)
  no operation moved by 1% of the time
where the time goes in v7:
time: 81.7 us; the launch traced here: 81.5 us
  waiting for transfers between devices  37.6 us (46%)
  starting transfers between devices  31.3 us (38%)
  Pallas kernels  11.2 us (14%)
    ppermute x23, waiting for transfers between devices, swap(): return lax.ppermute(array, 'seq', [(s, s ^ mask) for s in range(shards)])  32 us
    ppermute x23, starting transfers between devices, swap(): return lax.ppermute(array, 'seq', [(s, s ^ mask) for s in range(shards)])  27.1 us
    pallas_call x18, Pallas kernels, kernel(): pl.pallas_call(run, in_specs=[there] * count + [pl.BlockSpec(memory_space...  11.2 us
    ppermute x2, waiting for transfers between devices, swap_pack(): return lax.ppermute(array, 'dp', [(d, d ^ 1) for d in range(packs)])  5.57 us
    ppermute x2, starting transfers between devices, swap_pack(): return lax.ppermute(array, 'dp', [(d, d ^ 1) for d in range(packs)])  4.19 us
  transfers between devices with their start and end apart: 25, of which 16 were waited for; matrix products, arithmetic and copies ran while one was open for 0% of the time, Pallas kernels for 7%

profile of v7, /device:TPU:0, one launch (start us, length us, event | category | flops | bytes accessed | tf_op | source)
XLA Modules:
  0.0 81.5 jit_solution(17986872065173663357)
XLA Ops:
  0.6 3.8 %shard_map.77 = (f32[2592,128]{1,0:T(8,128)S(1)}, f32[8,8,128]{2,1,0:T(8,128)S(1)}, bf16[192,2560]{1,0:T(8,128)(2,1)S(1)}, bf16[192,2560]{1,0:T(8,128)(2,1)S(1)}...) custom-call(bf16[1,192,2560]{2,1,0:T(8,128)(2,1)} %refs_0_.1, bf16[2560,256]{1,0:T(8,128)(2,1)} %refs_1_.1, ...), custom_call_target="tpu_custom_call" | custom-call | flops 1000 | bytes 1000 | tf_op jit(solution)/shard_map/pallas_call | solution.py:421
  6.1 2.7 %collective-permute-start.12 = (f32[1920,128]{1,0:T(8,128)S(1)}, f32[1920,128]{1,0:T(8,128)S(1)}, u32[]{:S(2)}, u32[]{:S(2)}) collective-permute-start(f32[1920,128]{1,0:T(8,128)S(1)} %get-tuple-element.72), channel_id=1, source_target_pairs={{0,16},{16,0},{1,17},{17,1},{2,18},{18,2},{3,19},{19,3},{4,20},{20... | collective-permute-start | bytes 2949128 | tf_op jit(solution)/shard_map/ppermute | solution.py:440
  8.9 2.8 %collective-permute-start.1 = (f32[392,128]{1,0:T(8,128)S(1)}, f32[392,128]{1,0:T(8,128)S(1)}, u32[]{:S(2)}, u32[]{:S(2)}) collective-permute-start(f32[392,128]{1,0:T(8,128)S(1)} %get-tuple-element.61), channel_id=1, source_target_pairs={{0,6},{1,7},{2,4},{3,5},{4,2},{5,3},{6,0},{7,1},{8,14},{9,15},{10,... | collective-permute-start | bytes 602120 | tf_op jit(solution)/shard_map/ppermute | solution.py:437
  12.5 1.9 %shard_map.81 = (f32[192,2560]{1,0:T(8,128)S(1)}, f32[192,2560]{1,0:T(8,128)S(1)}, f32[192,256]{1,0:T(8,128)S(1)}) custom-call(bf16[192,2560]{1,0:T(8,128)(2,1)S(1)} %bitcast.4, bf16[192,2560]{1,0:T(8,128)(2,1)S(1)} %bitcast.5, s32[40,192]{1,0:T(8,128)S(1)} %bitcast.6, s32[1,192]{1,0:T(1,128)S(1)} %copy-done.3, ...), custom_call_target="tpu_custom_call" | custom-call | flops 1000 | bytes 1000 | tf_op jit(solution)/shard_map/pallas_call | solution.py:421
  14.4 3.3 %collective-permute-done.1.refs_5_.refs_1_ = f32[392,128]{1,0:T(8,128)S(1)} collective-permute-done((f32[392,128]{1,0:T(8,128)S(1)}, f32[392,128]{1,0:T(8,128)S(1)}, u32[]{:S(2)}, u32[]{:S(2)}) %collective-permute-start.1) | collective-permute-done | bytes 200736 | tf_op jit(solution)/shard_map/ppermute | solution.py:437
  17.8 2.8 %collective-permute-start.5 = (f32[264,128]{1,0:T(8,128)S(1)}, f32[264,128]{1,0:T(8,128)S(1)}, u32[]{:S(2)}, u32[]{:S(2)}) collective-permute-start(f32[264,128]{1,0:T(8,128)S(1)} %get-tuple-element.65), channel_id=1, source_target_pairs={{0,6},{1,7},{2,4},{3,5},{4,2},{5,3},{6,0},{7,1},{8,14},{9,15},{10,... | collective-permute-start | bytes 405512 | tf_op jit(solution)/shard_map/ppermute | solution.py:437
  22.1 1.8 %collective-permute-start.7 = (f32[264,128]{1,0:T(8,128)S(1)}, f32[264,128]{1,0:T(8,128)S(1)}, u32[]{:S(2)}, u32[]{:S(2)}) collective-permute-start(f32[264,128]{1,0:T(8,128)S(1)} %get-tuple-element.67), channel_id=1, source_target_pairs={{0,4},{1,5},{2,6},{3,7},{4,0},{5,1},{6,2},{7,3},{8,12},{9,13},{10,... | collective-permute-start | bytes 405512 | tf_op jit(solution)/shard_map/ppermute | solution.py:437
  24.0 2.7 %collective-permute-start.4 = (f32[192,128]{1,0:T(8,128)S(1)}, f32[192,128]{1,0:T(8,128)S(1)}, u32[]{:S(2)}, u32[]{:S(2)}) collective-permute-start(f32[192,128]{1,0:T(8,128)S(1)} %shard_map.83.refs_4_), channel_id=1, source_target_pairs={{0,8},{1,9},{2,10},{3,11},{4,12},{5,13},{6,14},{7,15},{8,0},{9,1},... | collective-permute-start | bytes 294920 | tf_op jit(solution)/shard_map/ppermute | solution.py:437
  27.1 1.4 %collective-permute-done.7.refs_3_ = f32[264,128]{1,0:T(8,128)S(1)} collective-permute-done((f32[264,128]{1,0:T(8,128)S(1)}, f32[264,128]{1,0:T(8,128)S(1)}, u32[]{:S(2)}, u32[]{:S(2)}) %collective-permute-start.7) | collective-permute-done | bytes 135200 | tf_op jit(solution)/shard_map/ppermute | solution.py:437
  28.5 2.0 %collective-permute-done.4.refs_4_ = f32[192,128]{1,0:T(8,128)S(1)} collective-permute-done((f32[192,128]{1,0:T(8,128)S(1)}, f32[192,128]{1,0:T(8,128)S(1)}, u32[]{:S(2)}, u32[]{:S(2)}) %collective-permute-start.4) | collective-permute-done | bytes 98336 | tf_op jit(solution)/shard_map/ppermute | solution.py:437
  30.7 2.7 %collective-permute-start.8 = (f32[384,128]{1,0:T(8,128)S(1)}, f32[384,128]{1,0:T(8,128)S(1)}, u32[]{:S(2)}, u32[]{:S(2)}) collective-permute-start(f32[384,128]{1,0:T(8,128)S(1)} %get-tuple-element.69), channel_id=1, source_target_pairs={{0,6},{1,7},{2,4},{3,5},{4,2},{5,3},{6,0},{7,1},{8,14},{9,15},{10,... | collective-permute-start | bytes 589832 | tf_op jit(solution)/shard_map/ppermute | solution.py:437
  33.5 1.9 %collective-permute-start.11 = (f32[128,128]{1,0:T(8,128)S(1)}, f32[128,128]{1,0:T(8,128)S(1)}, u32[]{:S(2)}, u32[]{:S(2)}) collective-permute-start(f32[128,128]{1,0:T(8,128)S(1)} %shard_map.84.refs_5_), channel_id=1, source_target_pairs={{0,8},{1,9},{2,10},{3,11},{4,12},{5,13},{6,14},{7,15},{8,0},{9,1},... | collective-permute-start | bytes 196616 | tf_op jit(solution)/shard_map/ppermute | solution.py:437
  36.2 4.0 %collective-permute-done.11.refs_4_ = f32[128,128]{1,0:T(8,128)S(1)} collective-permute-done((f32[128,128]{1,0:T(8,128)S(1)}, f32[128,128]{1,0:T(8,128)S(1)}, u32[]{:S(2)}, u32[]{:S(2)}) %collective-permute-start.11) | collective-permute-done | bytes 65568 | tf_op jit(solution)/shard_map/ppermute | solution.py:437
  40.4 2.3 %collective-permute-start.13 = (f32[256,128]{1,0:T(8,128)S(1)}, f32[256,128]{1,0:T(8,128)S(1)}, u32[]{:S(2)}, u32[]{:S(2)}) collective-permute-start(f32[256,128]{1,0:T(8,128)S(1)} %get-tuple-element.74), channel_id=1, source_target_pairs={{0,6},{1,7},{2,4},{3,5},{4,2},{5,3},{6,0},{7,1},{8,14},{9,15},{10,... | collective-permute-start | bytes 393224 | tf_op jit(solution)/shard_map/ppermute | solution.py:437
  45.1 2.2 %collective-permute-done.13.refs_5_ = f32[256,128]{1,0:T(8,128)S(1)} collective-permute-done((f32[256,128]{1,0:T(8,128)S(1)}, f32[256,128]{1,0:T(8,128)S(1)}, u32[]{:S(2)}, u32[]{:S(2)}) %collective-permute-start.13) | collective-permute-done | bytes 131104 | tf_op jit(solution)/shard_map/ppermute | solution.py:437
  49.7 2.6 %collective-permute-done.16.refs_3_ = f32[2560,128]{1,0:T(8,128)S(1)} collective-permute-done((f32[2560,128]{1,0:T(8,128)S(1)}, f32[2560,128]{1,0:T(8,128)S(1)}, u32[]{:S(2)}, u32[]{:S(2)}) %collective-permute-start.16) | collective-permute-done | bytes 1310752 | tf_op jit(solution)/shard_map/ppermute | solution.py:437
  53.0 1.5 %collective-permute-start.19 = (f32[192,256]{1,0:T(8,128)S(1)}, f32[192,256]{1,0:T(8,128)S(1)}, u32[]{:S(2)}, u32[]{:S(2)}) collective-permute-start(f32[192,256]{1,0:T(8,128)S(1)} %get-tuple-element.83.refs_2_.refs_1_), channel_id=1, source_target_pairs={{0,16},{16,0},{1,17},{17,1},{2,18},{18,2},{3,19},{19,3},{4,20},{20... | collective-permute-start | bytes 589832 | tf_op jit(solution)/shard_map/ppermute | solution.py:440
  54.7 5.6 %collective-permute-done.19.refs_3_ = f32[192,256]{1,0:T(8,128)S(1)} collective-permute-done((f32[192,256]{1,0:T(8,128)S(1)}, f32[192,256]{1,0:T(8,128)S(1)}, u32[]{:S(2)}, u32[]{:S(2)}) %collective-permute-start.19) | collective-permute-done | bytes 196640 | tf_op jit(solution)/shard_map/ppermute | solution.py:440
  60.2 1.4 %shard_map.91 = (bf16[192,2560]{1,0:T(8,128)(2,1)}, f32[8,128]{1,0:T(8,128)S(1)}) custom-call(f32[192,2560]{1,0:T(8,128)S(1)} %get-tuple-element.58.refs_0_, f32[192,2560]{1,0:T(8,128)S(1)} %get-tuple-element.59.refs_1_, bf16[192,256]{1,0:T(8,128)(2,1)S(1)} %get-tuple-element.47.refs_2_.refs_4_, bf16[1280,128]{1,0:T(8,128)(2,1)S(1)} %get-tuple-element.79.refs_3_, ...), custom_call_target="tpu_custom_call" | custom-call | flops 1000 | bytes 1000 | tf_op jit(solution)/shard_map/pallas_call | solution.py:421
  62.6 1.6 %collective-permute-start.21 = (f32[160,256]{1,0:T(8,128)S(1)}, f32[160,256]{1,0:T(8,128)S(1)}, u32[]{:S(2)}, u32[]{:S(2)}) collective-permute-start(f32[160,256]{1,0:T(8,128)S(1)} %get-tuple-element.87), channel_id=1, source_target_pairs={{0,6},{1,7},{2,4},{3,5},{4,2},{5,3},{6,0},{7,1},{8,14},{9,15},{10,... | collective-permute-start | bytes 491528 | tf_op jit(solution)/shard_map/ppermute | solution.py:437
  66.2 4.4 %collective-permute-done.21.refs_1_ = f32[160,256]{1,0:T(8,128)S(1)} collective-permute-done((f32[160,256]{1,0:T(8,128)S(1)}, f32[160,256]{1,0:T(8,128)S(1)}, u32[]{:S(2)}, u32[]{:S(2)}) %collective-permute-start.21) | collective-permute-done | bytes 163872 | tf_op jit(solution)/shard_map/ppermute | solution.py:437
  70.6 3.1 %collective-permute-done.22.refs_2_ = f32[160,256]{1,0:T(8,128)S(1)} collective-permute-done((f32[160,256]{1,0:T(8,128)S(1)}, f32[160,256]{1,0:T(8,128)S(1)}, u32[]{:S(2)}, u32[]{:S(2)}) %collective-permute-start.22) | collective-permute-done | bytes 163872 | tf_op jit(solution)/shard_map/ppermute | solution.py:437
  73.7 2.3 %collective-permute-start.24 = (f32[80,256]{1,0:T(8,128)S(1)}, f32[80,256]{1,0:T(8,128)S(1)}, u32[]{:S(2)}, u32[]{:S(2)}) collective-permute-start(f32[80,256]{1,0:T(8,128)S(1)} %get-tuple-element.91), channel_id=1, source_target_pairs={{0,8},{1,9},{2,10},{3,11},{4,12},{5,13},{6,14},{7,15},{8,0},{9,1},... | collective-permute-start | bytes 245768 | tf_op jit(solution)/shard_map/ppermute | solution.py:437
  76.0 4.8 %collective-permute-done.24 = f32[80,256]{1,0:T(8,128)S(1)} collective-permute-done((f32[80,256]{1,0:T(8,128)S(1)}, f32[80,256]{1,0:T(8,128)S(1)}, u32[]{:S(2)}, u32[]{:S(2)}) %collective-permute-start.24) | collective-permute-done | bytes 81952 | tf_op jit(solution)/shard_map/ppermute | solution.py:437
  (53 shorter events, 15.2 us)
Async XLA Ops:
  4.4 4.4 %collective-permute-start = (f32[2592,128]{1,0:T(8,128)S(1)}, f32[2592,128]{1,0:T(8,128)S(1)}, u32[]{:S(2)}, u32[]{:S(2)}) collective-permute-start(f32[2592,128]{1,0:T(8,128)S(1)} %get-tuple-element.54), channel_id=1, source_target_pairs={{0,1},{1,0},{2,3},{3,2},{4,5},{5,4},{6,7},{7,6},{8,9},{9,8},{10,11... | collective-permute-start | bytes 3981320 | tf_op jit(solution)/shard_map/ppermute | solution.py:437
  6.1 30.1 %collective-permute-start.12 = (f32[1920,128]{1,0:T(8,128)S(1)}, f32[1920,128]{1,0:T(8,128)S(1)}, u32[]{:S(2)}, u32[]{:S(2)}) collective-permute-start(f32[1920,128]{1,0:T(8,128)S(1)} %get-tuple-element.72), channel_id=1, source_target_pairs={{0,16},{16,0},{1,17},{17,1},{2,18},{18,2},{3,19},{19,3},{4,20},{20... | collective-permute-start | bytes 2949128 | tf_op jit(solution)/shard_map/ppermute | solution.py:440
  8.9 8.8 %collective-permute-start.1 = (f32[392,128]{1,0:T(8,128)S(1)}, f32[392,128]{1,0:T(8,128)S(1)}, u32[]{:S(2)}, u32[]{:S(2)}) collective-permute-start(f32[392,128]{1,0:T(8,128)S(1)} %get-tuple-element.61), channel_id=1, source_target_pairs={{0,6},{1,7},{2,4},{3,5},{4,2},{5,3},{6,0},{7,1},{8,14},{9,15},{10,... | collective-permute-start | bytes 602120 | tf_op jit(solution)/shard_map/ppermute | solution.py:437
  11.7 10.4 %collective-permute-start.2 = (f32[392,128]{1,0:T(8,128)S(1)}, f32[392,128]{1,0:T(8,128)S(1)}, u32[]{:S(2)}, u32[]{:S(2)}) collective-permute-start(f32[392,128]{1,0:T(8,128)S(1)} %get-tuple-element.62), channel_id=1, source_target_pairs={{0,2},{1,3},{2,0},{3,1},{4,6},{5,7},{6,4},{7,5},{8,10},{9,11},{10,... | collective-permute-start | bytes 602120 | tf_op jit(solution)/shard_map/ppermute | solution.py:437
  12.2 11.7 %collective-permute-start.3 = (f32[392,128]{1,0:T(8,128)S(1)}, f32[392,128]{1,0:T(8,128)S(1)}, u32[]{:S(2)}, u32[]{:S(2)}) collective-permute-start(f32[392,128]{1,0:T(8,128)S(1)} %get-tuple-element.63), channel_id=1, source_target_pairs={{0,4},{1,5},{2,6},{3,7},{4,0},{5,1},{6,2},{7,3},{8,12},{9,13},{10,... | collective-permute-start | bytes 602120 | tf_op jit(solution)/shard_map/ppermute | solution.py:437
  17.8 8.8 %collective-permute-start.5 = (f32[264,128]{1,0:T(8,128)S(1)}, f32[264,128]{1,0:T(8,128)S(1)}, u32[]{:S(2)}, u32[]{:S(2)}) collective-permute-start(f32[264,128]{1,0:T(8,128)S(1)} %get-tuple-element.65), channel_id=1, source_target_pairs={{0,6},{1,7},{2,4},{3,5},{4,2},{5,3},{6,0},{7,1},{8,14},{9,15},{10,... | collective-permute-start | bytes 405512 | tf_op jit(solution)/shard_map/ppermute | solution.py:437
  20.6 6.5 %collective-permute-start.6 = (f32[264,128]{1,0:T(8,128)S(1)}, f32[264,128]{1,0:T(8,128)S(1)}, u32[]{:S(2)}, u32[]{:S(2)}) collective-permute-start(f32[264,128]{1,0:T(8,128)S(1)} %get-tuple-element.66), channel_id=1, source_target_pairs={{0,2},{1,3},{2,0},{3,1},{4,6},{5,7},{6,4},{7,5},{8,10},{9,11},{10,... | collective-permute-start | bytes 405512 | tf_op jit(solution)/shard_map/ppermute | solution.py:437
  22.1 6.4 %collective-permute-start.7 = (f32[264,128]{1,0:T(8,128)S(1)}, f32[264,128]{1,0:T(8,128)S(1)}, u32[]{:S(2)}, u32[]{:S(2)}) collective-permute-start(f32[264,128]{1,0:T(8,128)S(1)} %get-tuple-element.67), channel_id=1, source_target_pairs={{0,4},{1,5},{2,6},{3,7},{4,0},{5,1},{6,2},{7,3},{8,12},{9,13},{10,... | collective-permute-start | bytes 405512 | tf_op jit(solution)/shard_map/ppermute | solution.py:437
  24.0 6.6 %collective-permute-start.4 = (f32[192,128]{1,0:T(8,128)S(1)}, f32[192,128]{1,0:T(8,128)S(1)}, u32[]{:S(2)}, u32[]{:S(2)}) collective-permute-start(f32[192,128]{1,0:T(8,128)S(1)} %shard_map.83.refs_4_), channel_id=1, source_target_pairs={{0,8},{1,9},{2,10},{3,11},{4,12},{5,13},{6,14},{7,15},{8,0},{9,1},... | collective-permute-start | bytes 294920 | tf_op jit(solution)/shard_map/ppermute | solution.py:437
  30.7 9.5 %collective-permute-start.8 = (f32[384,128]{1,0:T(8,128)S(1)}, f32[384,128]{1,0:T(8,128)S(1)}, u32[]{:S(2)}, u32[]{:S(2)}) collective-permute-start(f32[384,128]{1,0:T(8,128)S(1)} %get-tuple-element.69), channel_id=1, source_target_pairs={{0,6},{1,7},{2,4},{3,5},{4,2},{5,3},{6,0},{7,1},{8,14},{9,15},{10,... | collective-permute-start | bytes 589832 | tf_op jit(solution)/shard_map/ppermute | solution.py:437
  33.5 6.8 %collective-permute-start.11 = (f32[128,128]{1,0:T(8,128)S(1)}, f32[128,128]{1,0:T(8,128)S(1)}, u32[]{:S(2)}, u32[]{:S(2)}) collective-permute-start(f32[128,128]{1,0:T(8,128)S(1)} %shard_map.84.refs_5_), channel_id=1, source_target_pairs={{0,8},{1,9},{2,10},{3,11},{4,12},{5,13},{6,14},{7,15},{8,0},{9,1},... | collective-permute-start | bytes 196616 | tf_op jit(solution)/shard_map/ppermute | solution.py:437
  35.3 9.1 %collective-permute-start.9 = (f32[384,128]{1,0:T(8,128)S(1)}, f32[384,128]{1,0:T(8,128)S(1)}, u32[]{:S(2)}, u32[]{:S(2)}) collective-permute-start(f32[384,128]{1,0:T(8,128)S(1)} %get-tuple-element.70), channel_id=1, source_target_pairs={{0,2},{1,3},{2,0},{3,1},{4,6},{5,7},{6,4},{7,5},{8,10},{9,11},{10,... | collective-permute-start | bytes 589832 | tf_op jit(solution)/shard_map/ppermute | solution.py:437
  36.2 8.8 %collective-permute-start.10 = (f32[384,128]{1,0:T(8,128)S(1)}, f32[384,128]{1,0:T(8,128)S(1)}, u32[]{:S(2)}, u32[]{:S(2)}) collective-permute-start(f32[384,128]{1,0:T(8,128)S(1)} %get-tuple-element.71), channel_id=1, source_target_pairs={{0,4},{1,5},{2,6},{3,7},{4,0},{5,1},{6,2},{7,3},{8,12},{9,13},{10,... | collective-permute-start | bytes 589832 | tf_op jit(solution)/shard_map/ppermute | solution.py:437
  40.4 6.9 %collective-permute-start.13 = (f32[256,128]{1,0:T(8,128)S(1)}, f32[256,128]{1,0:T(8,128)S(1)}, u32[]{:S(2)}, u32[]{:S(2)}) collective-permute-start(f32[256,128]{1,0:T(8,128)S(1)} %get-tuple-element.74), channel_id=1, source_target_pairs={{0,6},{1,7},{2,4},{3,5},{4,2},{5,3},{6,0},{7,1},{8,14},{9,15},{10,... | collective-permute-start | bytes 393224 | tf_op jit(solution)/shard_map/ppermute | solution.py:437
  42.7 5.7 %collective-permute-start.14 = (f32[256,128]{1,0:T(8,128)S(1)}, f32[256,128]{1,0:T(8,128)S(1)}, u32[]{:S(2)}, u32[]{:S(2)}) collective-permute-start(f32[256,128]{1,0:T(8,128)S(1)} %get-tuple-element.75), channel_id=1, source_target_pairs={{0,2},{1,3},{2,0},{3,1},{4,6},{5,7},{6,4},{7,5},{8,10},{9,11},{10,... | collective-permute-start | bytes 393224 | tf_op jit(solution)/shard_map/ppermute | solution.py:437
  43.9 5.0 %collective-permute-start.15 = (f32[256,128]{1,0:T(8,128)S(1)}, f32[256,128]{1,0:T(8,128)S(1)}, u32[]{:S(2)}, u32[]{:S(2)}) collective-permute-start(f32[256,128]{1,0:T(8,128)S(1)} %get-tuple-element.76), channel_id=1, source_target_pairs={{0,4},{1,5},{2,6},{3,7},{4,0},{5,1},{6,2},{7,3},{8,12},{9,13},{10,... | collective-permute-start | bytes 393224 | tf_op jit(solution)/shard_map/ppermute | solution.py:437
  49.2 3.1 %collective-permute-start.16 = (f32[2560,128]{1,0:T(8,128)S(1)}, f32[2560,128]{1,0:T(8,128)S(1)}, u32[]{:S(2)}, u32[]{:S(2)}) collective-permute-start(f32[2560,128]{1,0:T(8,128)S(1)} %get-tuple-element.78.refs_4_), channel_id=1, source_target_pairs={{0,1},{1,0},{2,3},{3,2},{4,5},{5,4},{6,7},{7,6},{8,9},{9,8},{10,11... | collective-permute-start | bytes 3932168 | tf_op jit(solution)/shard_map/ppermute | solution.py:437
  52.8 8.8 %collective-permute-start.17 = (f32[1920,128]{1,0:T(8,128)S(1)}, f32[1920,128]{1,0:T(8,128)S(1)}, u32[]{:S(2)}, u32[]{:S(2)}) collective-permute-start(f32[1920,128]{1,0:T(8,128)S(1)} %shard_map.90.refs_5_), channel_id=1, source_target_pairs={{0,1},{1,0},{2,3},{3,2},{4,5},{5,4},{6,7},{7,6},{8,9},{9,8},{10,11... | collective-permute-start | bytes 2949128 | tf_op jit(solution)/shard_map/ppermute | solution.py:437
  53.0 7.2 %collective-permute-start.19 = (f32[192,256]{1,0:T(8,128)S(1)}, f32[192,256]{1,0:T(8,128)S(1)}, u32[]{:S(2)}, u32[]{:S(2)}) collective-permute-start(f32[192,256]{1,0:T(8,128)S(1)} %get-tuple-element.83.refs_2_.refs_1_), channel_id=1, source_target_pairs={{0,16},{16,0},{1,17},{17,1},{2,18},{18,2},{3,19},{19,3},{4,20},{20... | collective-permute-start | bytes 589832 | tf_op jit(solution)/shard_map/ppermute | solution.py:440
  54.6 7.4 %collective-permute-start.18 = (f32[192,256]{1,0:T(8,128)S(1)}, f32[192,256]{1,0:T(8,128)S(1)}, u32[]{:S(2)}, u32[]{:S(2)}) collective-permute-start(f32[192,256]{1,0:T(8,128)S(1)} %get-tuple-element.83.refs_2_.refs_1_), channel_id=1, source_target_pairs={{0,1},{1,0},{2,3},{3,2},{4,5},{5,4},{6,7},{7,6},{8,9},{9,8},{10,11... | collective-permute-start | bytes 589832 | tf_op jit(solution)/shard_map/ppermute | solution.py:437
  62.6 8.0 %collective-permute-start.21 = (f32[160,256]{1,0:T(8,128)S(1)}, f32[160,256]{1,0:T(8,128)S(1)}, u32[]{:S(2)}, u32[]{:S(2)}) collective-permute-start(f32[160,256]{1,0:T(8,128)S(1)} %get-tuple-element.87), channel_id=1, source_target_pairs={{0,6},{1,7},{2,4},{3,5},{4,2},{5,3},{6,0},{7,1},{8,14},{9,15},{10,... | collective-permute-start | bytes 491528 | tf_op jit(solution)/shard_map/ppermute | solution.py:437
  64.2 9.5 %collective-permute-start.22 = (f32[160,256]{1,0:T(8,128)S(1)}, f32[160,256]{1,0:T(8,128)S(1)}, u32[]{:S(2)}, u32[]{:S(2)}) collective-permute-start(f32[160,256]{1,0:T(8,128)S(1)} %get-tuple-element.88), channel_id=1, source_target_pairs={{0,2},{1,3},{2,0},{3,1},{4,6},{5,7},{6,4},{7,5},{8,10},{9,11},{10,... | collective-permute-start | bytes 491528 | tf_op jit(solution)/shard_map/ppermute | solution.py:437
  65.4 8.3 %collective-permute-start.23 = (f32[160,256]{1,0:T(8,128)S(1)}, f32[160,256]{1,0:T(8,128)S(1)}, u32[]{:S(2)}, u32[]{:S(2)}) collective-permute-start(f32[160,256]{1,0:T(8,128)S(1)} %get-tuple-element.89), channel_id=1, source_target_pairs={{0,4},{1,5},{2,6},{3,7},{4,0},{5,1},{6,2},{7,3},{8,12},{9,13},{10,... | collective-permute-start | bytes 491528 | tf_op jit(solution)/shard_map/ppermute | solution.py:437
  73.7 7.1 %collective-permute-start.24 = (f32[80,256]{1,0:T(8,128)S(1)}, f32[80,256]{1,0:T(8,128)S(1)}, u32[]{:S(2)}, u32[]{:S(2)}) collective-permute-start(f32[80,256]{1,0:T(8,128)S(1)} %get-tuple-element.91), channel_id=1, source_target_pairs={{0,8},{1,9},{2,10},{3,11},{4,12},{5,13},{6,14},{7,15},{8,0},{9,1},... | collective-permute-start | bytes 245768 | tf_op jit(solution)/shard_map/ppermute | solution.py:437
  (5 other events, 16.6 us)

commit v8 on v7

--- a/solution.py
+++ b/solution.py
@@ -485,7 +485,7 @@
 
     quads = []
     for start, size in chunks:
-        waits = quads[-1][1:2] if quads else ()
+        waits = quads[-1][1:3] if quads else ()
         if quads:
             grad_local, scale, dbc_local = kernel(
                 local_body, (shape(length, width), shape(length, width), shape(length, 2 * state)),

time: 81.7 us -> 84.4 us (1.033)
  waiting for transfers between devices: 37.6 us -> 42.3 us
  starting transfers between devices: 31.3 us -> 29.3 us
    ppermute x23, waiting for transfers between devices: 32 us -> 36.7 us  [swap(): return lax.ppermute(array, 'seq', [(s, s ^ mask) for s in range(shards)])]
    ppermute x23, starting transfers between devices: 27.1 us -> 25.1 us  [swap(): return lax.ppermute(array, 'seq', [(s, s ^ mask) for s in range(shards)])]
  transfers between devices with their start and end apart: 25 -> 25, of which waited for: 16 -> 15; matrix products, arithmetic and copies ran while one was open for 0% -> 0% of each run, Pallas kernels for 7% -> 7%
where the time goes in v8:
time: 84.4 us; the launch traced here: 84.2 us
  waiting for transfers between devices  42.3 us (50%)
  starting transfers between devices  29.3 us (35%)
  Pallas kernels  11.2 us (13%)
    ppermute x23, waiting for transfers between devices, swap(): return lax.ppermute(array, 'seq', [(s, s ^ mask) for s in range(shards)])  36.7 us
    ppermute x23, starting transfers between devices, swap(): return lax.ppermute(array, 'seq', [(s, s ^ mask) for s in range(shards)])  25.1 us
    pallas_call x18, Pallas kernels, kernel(): pl.pallas_call(run, in_specs=[there] * count + [pl.BlockSpec(memory_space...  11.2 us
    ppermute x2, waiting for transfers between devices, swap_pack(): return lax.ppermute(array, 'dp', [(d, d ^ 1) for d in range(packs)])  5.57 us
    ppermute x2, starting transfers between devices, swap_pack(): return lax.ppermute(array, 'dp', [(d, d ^ 1) for d in range(packs)])  4.19 us
  transfers between devices with their start and end apart: 25, of which 15 were waited for; matrix products, arithmetic and copies ran while one was open for 0% of the time, Pallas kernels for 7%

profile of v8, /device:TPU:0, one launch (start us, length us, event | category | flops | bytes accessed | tf_op | source)
XLA Modules:
  0.0 84.2 jit_solution(4677534416807970768)
XLA Ops:
  0.6 3.8 %shard_map.77 = (f32[2592,128]{1,0:T(8,128)S(1)}, f32[8,8,128]{2,1,0:T(8,128)S(1)}, bf16[192,2560]{1,0:T(8,128)(2,1)S(1)}, bf16[192,2560]{1,0:T(8,128)(2,1)S(1)}...) custom-call(bf16[1,192,2560]{2,1,0:T(8,128)(2,1)} %refs_0_.1, bf16[2560,256]{1,0:T(8,128)(2,1)} %refs_1_.1, ...), custom_call_target="tpu_custom_call" | custom-call | flops 1000 | bytes 1000 | tf_op jit(solution)/shard_map/pallas_call | solution.py:421
  6.1 2.7 %collective-permute-start.12 = (f32[1920,128]{1,0:T(8,128)S(1)}, f32[1920,128]{1,0:T(8,128)S(1)}, u32[]{:S(2)}, u32[]{:S(2)}) collective-permute-start(f32[1920,128]{1,0:T(8,128)S(1)} %get-tuple-element.72), channel_id=1, source_target_pairs={{0,16},{16,0},{1,17},{17,1},{2,18},{18,2},{3,19},{19,3},{4,20},{20... | collective-permute-start | bytes 2949128 | tf_op jit(solution)/shard_map/ppermute | solution.py:440
  8.9 2.8 %collective-permute-start.1 = (f32[392,128]{1,0:T(8,128)S(1)}, f32[392,128]{1,0:T(8,128)S(1)}, u32[]{:S(2)}, u32[]{:S(2)}) collective-permute-start(f32[392,128]{1,0:T(8,128)S(1)} %get-tuple-element.61), channel_id=1, source_target_pairs={{0,6},{1,7},{2,4},{3,5},{4,2},{5,3},{6,0},{7,1},{8,14},{9,15},{10,... | collective-permute-start | bytes 602120 | tf_op jit(solution)/shard_map/ppermute | solution.py:437
  12.5 1.9 %shard_map.81 = (f32[192,2560]{1,0:T(8,128)S(1)}, f32[192,2560]{1,0:T(8,128)S(1)}, f32[192,256]{1,0:T(8,128)S(1)}) custom-call(bf16[192,2560]{1,0:T(8,128)(2,1)S(1)} %bitcast.4, bf16[192,2560]{1,0:T(8,128)(2,1)S(1)} %bitcast.5, s32[40,192]{1,0:T(8,128)S(1)} %bitcast.6, s32[1,192]{1,0:T(1,128)S(1)} %copy-done.3, ...), custom_call_target="tpu_custom_call" | custom-call | flops 1000 | bytes 1000 | tf_op jit(solution)/shard_map/pallas_call | solution.py:421
  14.4 3.3 %collective-permute-done.1.refs_5_.refs_1_ = f32[392,128]{1,0:T(8,128)S(1)} collective-permute-done((f32[392,128]{1,0:T(8,128)S(1)}, f32[392,128]{1,0:T(8,128)S(1)}, u32[]{:S(2)}, u32[]{:S(2)}) %collective-permute-start.1) | collective-permute-done | bytes 200736 | tf_op jit(solution)/shard_map/ppermute | solution.py:437
  17.7 3.5 %collective-permute-done.2.refs_6_.refs_2_ = f32[392,128]{1,0:T(8,128)S(1)} collective-permute-done((f32[392,128]{1,0:T(8,128)S(1)}, f32[392,128]{1,0:T(8,128)S(1)}, u32[]{:S(2)}, u32[]{:S(2)}) %collective-permute-start.2) | collective-permute-done | bytes 200736 | tf_op jit(solution)/shard_map/ppermute | solution.py:437
  21.3 1.9 %collective-permute-start.5 = (f32[264,128]{1,0:T(8,128)S(1)}, f32[264,128]{1,0:T(8,128)S(1)}, u32[]{:S(2)}, u32[]{:S(2)}) collective-permute-start(f32[264,128]{1,0:T(8,128)S(1)} %get-tuple-element.65), channel_id=1, source_target_pairs={{0,6},{1,7},{2,4},{3,5},{4,2},{5,3},{6,0},{7,1},{8,14},{9,15},{10,... | collective-permute-start | bytes 405512 | tf_op jit(solution)/shard_map/ppermute | solution.py:437
  25.0 2.8 %collective-permute-start.4 = (f32[192,128]{1,0:T(8,128)S(1)}, f32[192,128]{1,0:T(8,128)S(1)}, u32[]{:S(2)}, u32[]{:S(2)}) collective-permute-start(f32[192,128]{1,0:T(8,128)S(1)} %shard_map.83.refs_4_), channel_id=1, source_target_pairs={{0,8},{1,9},{2,10},{3,11},{4,12},{5,13},{6,14},{7,15},{8,0},{9,1},... | collective-permute-start | bytes 294920 | tf_op jit(solution)/shard_map/ppermute | solution.py:437
  28.8 1.9 %collective-permute-done.6.refs_2_ = f32[264,128]{1,0:T(8,128)S(1)} collective-permute-done((f32[264,128]{1,0:T(8,128)S(1)}, f32[264,128]{1,0:T(8,128)S(1)}, u32[]{:S(2)}, u32[]{:S(2)}) %collective-permute-start.6) | collective-permute-done | bytes 135200 | tf_op jit(solution)/shard_map/ppermute | solution.py:437
  30.7 2.3 %collective-permute-done.7.refs_3_ = f32[264,128]{1,0:T(8,128)S(1)} collective-permute-done((f32[264,128]{1,0:T(8,128)S(1)}, f32[264,128]{1,0:T(8,128)S(1)}, u32[]{:S(2)}, u32[]{:S(2)}) %collective-permute-start.7) | collective-permute-done | bytes 135200 | tf_op jit(solution)/shard_map/ppermute | solution.py:437
  33.3 2.6 %collective-permute-start.8 = (f32[384,128]{1,0:T(8,128)S(1)}, f32[384,128]{1,0:T(8,128)S(1)}, u32[]{:S(2)}, u32[]{:S(2)}) collective-permute-start(f32[384,128]{1,0:T(8,128)S(1)} %get-tuple-element.69), channel_id=1, source_target_pairs={{0,6},{1,7},{2,4},{3,5},{4,2},{5,3},{6,0},{7,1},{8,14},{9,15},{10,... | collective-permute-start | bytes 589832 | tf_op jit(solution)/shard_map/ppermute | solution.py:437
  35.8 1.6 %collective-permute-start.11 = (f32[128,128]{1,0:T(8,128)S(1)}, f32[128,128]{1,0:T(8,128)S(1)}, u32[]{:S(2)}, u32[]{:S(2)}) collective-permute-start(f32[128,128]{1,0:T(8,128)S(1)} %shard_map.84.refs_5_), channel_id=1, source_target_pairs={{0,8},{1,9},{2,10},{3,11},{4,12},{5,13},{6,14},{7,15},{8,0},{9,1},... | collective-permute-start | bytes 196616 | tf_op jit(solution)/shard_map/ppermute | solution.py:437
  38.2 4.4 %collective-permute-done.11.refs_4_ = f32[128,128]{1,0:T(8,128)S(1)} collective-permute-done((f32[128,128]{1,0:T(8,128)S(1)}, f32[128,128]{1,0:T(8,128)S(1)}, u32[]{:S(2)}, u32[]{:S(2)}) %collective-permute-start.11) | collective-permute-done | bytes 65568 | tf_op jit(solution)/shard_map/ppermute | solution.py:437
  42.8 2.3 %collective-permute-start.13 = (f32[256,128]{1,0:T(8,128)S(1)}, f32[256,128]{1,0:T(8,128)S(1)}, u32[]{:S(2)}, u32[]{:S(2)}) collective-permute-start(f32[256,128]{1,0:T(8,128)S(1)} %get-tuple-element.74), channel_id=1, source_target_pairs={{0,6},{1,7},{2,4},{3,5},{4,2},{5,3},{6,0},{7,1},{8,14},{9,15},{10,... | collective-permute-start | bytes 393224 | tf_op jit(solution)/shard_map/ppermute | solution.py:437
  45.1 1.6 %collective-permute-start.14 = (f32[256,128]{1,0:T(8,128)S(1)}, f32[256,128]{1,0:T(8,128)S(1)}, u32[]{:S(2)}, u32[]{:S(2)}) collective-permute-start(f32[256,128]{1,0:T(8,128)S(1)} %get-tuple-element.75), channel_id=1, source_target_pairs={{0,2},{1,3},{2,0},{3,1},{4,6},{5,7},{6,4},{7,5},{8,10},{9,11},{10,... | collective-permute-start | bytes 393224 | tf_op jit(solution)/shard_map/ppermute | solution.py:437
  47.3 2.9 %collective-permute-done.13.refs_5_ = f32[256,128]{1,0:T(8,128)S(1)} collective-permute-done((f32[256,128]{1,0:T(8,128)S(1)}, f32[256,128]{1,0:T(8,128)S(1)}, u32[]{:S(2)}, u32[]{:S(2)}) %collective-permute-start.13) | collective-permute-done | bytes 131104 | tf_op jit(solution)/shard_map/ppermute | solution.py:437
  52.5 2.6 %collective-permute-done.16.refs_3_ = f32[2560,128]{1,0:T(8,128)S(1)} collective-permute-done((f32[2560,128]{1,0:T(8,128)S(1)}, f32[2560,128]{1,0:T(8,128)S(1)}, u32[]{:S(2)}, u32[]{:S(2)}) %collective-permute-start.16) | collective-permute-done | bytes 1310752 | tf_op jit(solution)/shard_map/ppermute | solution.py:437
  55.8 1.5 %collective-permute-start.19 = (f32[192,256]{1,0:T(8,128)S(1)}, f32[192,256]{1,0:T(8,128)S(1)}, u32[]{:S(2)}, u32[]{:S(2)}) collective-permute-start(f32[192,256]{1,0:T(8,128)S(1)} %get-tuple-element.83.refs_2_.refs_1_), channel_id=1, source_target_pairs={{0,16},{16,0},{1,17},{17,1},{2,18},{18,2},{3,19},{19,3},{4,20},{20... | collective-permute-start | bytes 589832 | tf_op jit(solution)/shard_map/ppermute | solution.py:440
  57.4 5.6 %collective-permute-done.19.refs_3_ = f32[192,256]{1,0:T(8,128)S(1)} collective-permute-done((f32[192,256]{1,0:T(8,128)S(1)}, f32[192,256]{1,0:T(8,128)S(1)}, u32[]{:S(2)}, u32[]{:S(2)}) %collective-permute-start.19) | collective-permute-done | bytes 196640 | tf_op jit(solution)/shard_map/ppermute | solution.py:440
  65.3 2.5 %collective-permute-start.21 = (f32[160,256]{1,0:T(8,128)S(1)}, f32[160,256]{1,0:T(8,128)S(1)}, u32[]{:S(2)}, u32[]{:S(2)}) collective-permute-start(f32[160,256]{1,0:T(8,128)S(1)} %get-tuple-element.87), channel_id=1, source_target_pairs={{0,6},{1,7},{2,4},{3,5},{4,2},{5,3},{6,0},{7,1},{8,14},{9,15},{10,... | collective-permute-start | bytes 491528 | tf_op jit(solution)/shard_map/ppermute | solution.py:437
  68.9 4.5 %collective-permute-done.21.refs_1_ = f32[160,256]{1,0:T(8,128)S(1)} collective-permute-done((f32[160,256]{1,0:T(8,128)S(1)}, f32[160,256]{1,0:T(8,128)S(1)}, u32[]{:S(2)}, u32[]{:S(2)}) %collective-permute-start.21) | collective-permute-done | bytes 163872 | tf_op jit(solution)/shard_map/ppermute | solution.py:437
  73.3 3.1 %collective-permute-done.22.refs_2_ = f32[160,256]{1,0:T(8,128)S(1)} collective-permute-done((f32[160,256]{1,0:T(8,128)S(1)}, f32[160,256]{1,0:T(8,128)S(1)}, u32[]{:S(2)}, u32[]{:S(2)}) %collective-permute-start.22) | collective-permute-done | bytes 163872 | tf_op jit(solution)/shard_map/ppermute | solution.py:437
  76.5 2.0 %collective-permute-start.24 = (f32[80,256]{1,0:T(8,128)S(1)}, f32[80,256]{1,0:T(8,128)S(1)}, u32[]{:S(2)}, u32[]{:S(2)}) collective-permute-start(f32[80,256]{1,0:T(8,128)S(1)} %get-tuple-element.91), channel_id=1, source_target_pairs={{0,8},{1,9},{2,10},{3,11},{4,12},{5,13},{6,14},{7,15},{8,0},{9,1},... | collective-permute-start | bytes 245768 | tf_op jit(solution)/shard_map/ppermute | solution.py:437
  78.5 5.1 %collective-permute-done.24 = f32[80,256]{1,0:T(8,128)S(1)} collective-permute-done((f32[80,256]{1,0:T(8,128)S(1)}, f32[80,256]{1,0:T(8,128)S(1)}, u32[]{:S(2)}, u32[]{:S(2)}) %collective-permute-start.24) | collective-permute-done | bytes 81952 | tf_op jit(solution)/shard_map/ppermute | solution.py:437
  (53 shorter events, 14.5 us)
Async XLA Ops:
  4.4 4.4 %collective-permute-start = (f32[2592,128]{1,0:T(8,128)S(1)}, f32[2592,128]{1,0:T(8,128)S(1)}, u32[]{:S(2)}, u32[]{:S(2)}) collective-permute-start(f32[2592,128]{1,0:T(8,128)S(1)} %get-tuple-element.54), channel_id=1, source_target_pairs={{0,1},{1,0},{2,3},{3,2},{4,5},{5,4},{6,7},{7,6},{8,9},{9,8},{10,11... | collective-permute-start | bytes 3981320 | tf_op jit(solution)/shard_map/ppermute | solution.py:437
  6.1 32.1 %collective-permute-start.12 = (f32[1920,128]{1,0:T(8,128)S(1)}, f32[1920,128]{1,0:T(8,128)S(1)}, u32[]{:S(2)}, u32[]{:S(2)}) collective-permute-start(f32[1920,128]{1,0:T(8,128)S(1)} %get-tuple-element.72), channel_id=1, source_target_pairs={{0,16},{16,0},{1,17},{17,1},{2,18},{18,2},{3,19},{19,3},{4,20},{20... | collective-permute-start | bytes 2949128 | tf_op jit(solution)/shard_map/ppermute | solution.py:440
  8.9 8.8 %collective-permute-start.1 = (f32[392,128]{1,0:T(8,128)S(1)}, f32[392,128]{1,0:T(8,128)S(1)}, u32[]{:S(2)}, u32[]{:S(2)}) collective-permute-start(f32[392,128]{1,0:T(8,128)S(1)} %get-tuple-element.61), channel_id=1, source_target_pairs={{0,6},{1,7},{2,4},{3,5},{4,2},{5,3},{6,0},{7,1},{8,14},{9,15},{10,... | collective-permute-start | bytes 602120 | tf_op jit(solution)/shard_map/ppermute | solution.py:437
  11.7 9.6 %collective-permute-start.2 = (f32[392,128]{1,0:T(8,128)S(1)}, f32[392,128]{1,0:T(8,128)S(1)}, u32[]{:S(2)}, u32[]{:S(2)}) collective-permute-start(f32[392,128]{1,0:T(8,128)S(1)} %get-tuple-element.62), channel_id=1, source_target_pairs={{0,2},{1,3},{2,0},{3,1},{4,6},{5,7},{6,4},{7,5},{8,10},{9,11},{10,... | collective-permute-start | bytes 602120 | tf_op jit(solution)/shard_map/ppermute | solution.py:437
  12.2 12.7 %collective-permute-start.3 = (f32[392,128]{1,0:T(8,128)S(1)}, f32[392,128]{1,0:T(8,128)S(1)}, u32[]{:S(2)}, u32[]{:S(2)}) collective-permute-start(f32[392,128]{1,0:T(8,128)S(1)} %get-tuple-element.63), channel_id=1, source_target_pairs={{0,4},{1,5},{2,6},{3,7},{4,0},{5,1},{6,2},{7,3},{8,12},{9,13},{10,... | collective-permute-start | bytes 602120 | tf_op jit(solution)/shard_map/ppermute | solution.py:437
  21.3 7.4 %collective-permute-start.5 = (f32[264,128]{1,0:T(8,128)S(1)}, f32[264,128]{1,0:T(8,128)S(1)}, u32[]{:S(2)}, u32[]{:S(2)}) collective-permute-start(f32[264,128]{1,0:T(8,128)S(1)} %get-tuple-element.65), channel_id=1, source_target_pairs={{0,6},{1,7},{2,4},{3,5},{4,2},{5,3},{6,0},{7,1},{8,14},{9,15},{10,... | collective-permute-start | bytes 405512 | tf_op jit(solution)/shard_map/ppermute | solution.py:437
  23.2 7.5 %collective-permute-start.6 = (f32[264,128]{1,0:T(8,128)S(1)}, f32[264,128]{1,0:T(8,128)S(1)}, u32[]{:S(2)}, u32[]{:S(2)}) collective-permute-start(f32[264,128]{1,0:T(8,128)S(1)} %get-tuple-element.66), channel_id=1, source_target_pairs={{0,2},{1,3},{2,0},{3,1},{4,6},{5,7},{6,4},{7,5},{8,10},{9,11},{10,... | collective-permute-start | bytes 405512 | tf_op jit(solution)/shard_map/ppermute | solution.py:437
  24.6 8.4 %collective-permute-start.7 = (f32[264,128]{1,0:T(8,128)S(1)}, f32[264,128]{1,0:T(8,128)S(1)}, u32[]{:S(2)}, u32[]{:S(2)}) collective-permute-start(f32[264,128]{1,0:T(8,128)S(1)} %get-tuple-element.67), channel_id=1, source_target_pairs={{0,4},{1,5},{2,6},{3,7},{4,0},{5,1},{6,2},{7,3},{8,12},{9,13},{10,... | collective-permute-start | bytes 405512 | tf_op jit(solution)/shard_map/ppermute | solution.py:437
  25.0 8.0 %collective-permute-start.4 = (f32[192,128]{1,0:T(8,128)S(1)}, f32[192,128]{1,0:T(8,128)S(1)}, u32[]{:S(2)}, u32[]{:S(2)}) collective-permute-start(f32[192,128]{1,0:T(8,128)S(1)} %shard_map.83.refs_4_), channel_id=1, source_target_pairs={{0,8},{1,9},{2,10},{3,11},{4,12},{5,13},{6,14},{7,15},{8,0},{9,1},... | collective-permute-start | bytes 294920 | tf_op jit(solution)/shard_map/ppermute | solution.py:437
  33.3 9.4 %collective-permute-start.8 = (f32[384,128]{1,0:T(8,128)S(1)}, f32[384,128]{1,0:T(8,128)S(1)}, u32[]{:S(2)}, u32[]{:S(2)}) collective-permute-start(f32[384,128]{1,0:T(8,128)S(1)} %get-tuple-element.69), channel_id=1, source_target_pairs={{0,6},{1,7},{2,4},{3,5},{4,2},{5,3},{6,0},{7,1},{8,14},{9,15},{10,... | collective-permute-start | bytes 589832 | tf_op jit(solution)/shard_map/ppermute | solution.py:437
  35.8 6.8 %collective-permute-start.11 = (f32[128,128]{1,0:T(8,128)S(1)}, f32[128,128]{1,0:T(8,128)S(1)}, u32[]{:S(2)}, u32[]{:S(2)}) collective-permute-start(f32[128,128]{1,0:T(8,128)S(1)} %shard_map.84.refs_5_), channel_id=1, source_target_pairs={{0,8},{1,9},{2,10},{3,11},{4,12},{5,13},{6,14},{7,15},{8,0},{9,1},... | collective-permute-start | bytes 196616 | tf_op jit(solution)/shard_map/ppermute | solution.py:437
  37.4 9.2 %collective-permute-start.9 = (f32[384,128]{1,0:T(8,128)S(1)}, f32[384,128]{1,0:T(8,128)S(1)}, u32[]{:S(2)}, u32[]{:S(2)}) collective-permute-start(f32[384,128]{1,0:T(8,128)S(1)} %get-tuple-element.70), channel_id=1, source_target_pairs={{0,2},{1,3},{2,0},{3,1},{4,6},{5,7},{6,4},{7,5},{8,10},{9,11},{10,... | collective-permute-start | bytes 589832 | tf_op jit(solution)/shard_map/ppermute | solution.py:437
  38.0 9.3 %collective-permute-start.10 = (f32[384,128]{1,0:T(8,128)S(1)}, f32[384,128]{1,0:T(8,128)S(1)}, u32[]{:S(2)}, u32[]{:S(2)}) collective-permute-start(f32[384,128]{1,0:T(8,128)S(1)} %get-tuple-element.71), channel_id=1, source_target_pairs={{0,4},{1,5},{2,6},{3,7},{4,0},{5,1},{6,2},{7,3},{8,12},{9,13},{10,... | collective-permute-start | bytes 589832 | tf_op jit(solution)/shard_map/ppermute | solution.py:437
  42.8 7.4 %collective-permute-start.13 = (f32[256,128]{1,0:T(8,128)S(1)}, f32[256,128]{1,0:T(8,128)S(1)}, u32[]{:S(2)}, u32[]{:S(2)}) collective-permute-start(f32[256,128]{1,0:T(8,128)S(1)} %get-tuple-element.74), channel_id=1, source_target_pairs={{0,6},{1,7},{2,4},{3,5},{4,2},{5,3},{6,0},{7,1},{8,14},{9,15},{10,... | collective-permute-start | bytes 393224 | tf_op jit(solution)/shard_map/ppermute | solution.py:437
  45.1 5.7 %collective-permute-start.14 = (f32[256,128]{1,0:T(8,128)S(1)}, f32[256,128]{1,0:T(8,128)S(1)}, u32[]{:S(2)}, u32[]{:S(2)}) collective-permute-start(f32[256,128]{1,0:T(8,128)S(1)} %get-tuple-element.75), channel_id=1, source_target_pairs={{0,2},{1,3},{2,0},{3,1},{4,6},{5,7},{6,4},{7,5},{8,10},{9,11},{10,... | collective-permute-start | bytes 393224 | tf_op jit(solution)/shard_map/ppermute | solution.py:437
  46.6 5.0 %collective-permute-start.15 = (f32[256,128]{1,0:T(8,128)S(1)}, f32[256,128]{1,0:T(8,128)S(1)}, u32[]{:S(2)}, u32[]{:S(2)}) collective-permute-start(f32[256,128]{1,0:T(8,128)S(1)} %get-tuple-element.76), channel_id=1, source_target_pairs={{0,4},{1,5},{2,6},{3,7},{4,0},{5,1},{6,2},{7,3},{8,12},{9,13},{10,... | collective-permute-start | bytes 393224 | tf_op jit(solution)/shard_map/ppermute | solution.py:437
  51.9 3.1 %collective-permute-start.16 = (f32[2560,128]{1,0:T(8,128)S(1)}, f32[2560,128]{1,0:T(8,128)S(1)}, u32[]{:S(2)}, u32[]{:S(2)}) collective-permute-start(f32[2560,128]{1,0:T(8,128)S(1)} %get-tuple-element.78.refs_4_), channel_id=1, source_target_pairs={{0,1},{1,0},{2,3},{3,2},{4,5},{5,4},{6,7},{7,6},{8,9},{9,8},{10,11... | collective-permute-start | bytes 3932168 | tf_op jit(solution)/shard_map/ppermute | solution.py:437
  55.6 8.8 %collective-permute-start.17 = (f32[1920,128]{1,0:T(8,128)S(1)}, f32[1920,128]{1,0:T(8,128)S(1)}, u32[]{:S(2)}, u32[]{:S(2)}) collective-permute-start(f32[1920,128]{1,0:T(8,128)S(1)} %shard_map.90.refs_5_), channel_id=1, source_target_pairs={{0,1},{1,0},{2,3},{3,2},{4,5},{5,4},{6,7},{7,6},{8,9},{9,8},{10,11... | collective-permute-start | bytes 2949128 | tf_op jit(solution)/shard_map/ppermute | solution.py:437
  55.8 7.2 %collective-permute-start.19 = (f32[192,256]{1,0:T(8,128)S(1)}, f32[192,256]{1,0:T(8,128)S(1)}, u32[]{:S(2)}, u32[]{:S(2)}) collective-permute-start(f32[192,256]{1,0:T(8,128)S(1)} %get-tuple-element.83.refs_2_.refs_1_), channel_id=1, source_target_pairs={{0,16},{16,0},{1,17},{17,1},{2,18},{18,2},{3,19},{19,3},{4,20},{20... | collective-permute-start | bytes 589832 | tf_op jit(solution)/shard_map/ppermute | solution.py:440
  57.3 7.4 %collective-permute-start.18 = (f32[192,256]{1,0:T(8,128)S(1)}, f32[192,256]{1,0:T(8,128)S(1)}, u32[]{:S(2)}, u32[]{:S(2)}) collective-permute-start(f32[192,256]{1,0:T(8,128)S(1)} %get-tuple-element.83.refs_2_.refs_1_), channel_id=1, source_target_pairs={{0,1},{1,0},{2,3},{3,2},{4,5},{5,4},{6,7},{7,6},{8,9},{9,8},{10,11... | collective-permute-start | bytes 589832 | tf_op jit(solution)/shard_map/ppermute | solution.py:437
  65.3 8.0 %collective-permute-start.21 = (f32[160,256]{1,0:T(8,128)S(1)}, f32[160,256]{1,0:T(8,128)S(1)}, u32[]{:S(2)}, u32[]{:S(2)}) collective-permute-start(f32[160,256]{1,0:T(8,128)S(1)} %get-tuple-element.87), channel_id=1, source_target_pairs={{0,6},{1,7},{2,4},{3,5},{4,2},{5,3},{6,0},{7,1},{8,14},{9,15},{10,... | collective-permute-start | bytes 491528 | tf_op jit(solution)/shard_map/ppermute | solution.py:437
  67.8 8.6 %collective-permute-start.22 = (f32[160,256]{1,0:T(8,128)S(1)}, f32[160,256]{1,0:T(8,128)S(1)}, u32[]{:S(2)}, u32[]{:S(2)}) collective-permute-start(f32[160,256]{1,0:T(8,128)S(1)} %get-tuple-element.88), channel_id=1, source_target_pairs={{0,2},{1,3},{2,0},{3,1},{4,6},{5,7},{6,4},{7,5},{8,10},{9,11},{10,... | collective-permute-start | bytes 491528 | tf_op jit(solution)/shard_map/ppermute | solution.py:437
  68.3 8.1 %collective-permute-start.23 = (f32[160,256]{1,0:T(8,128)S(1)}, f32[160,256]{1,0:T(8,128)S(1)}, u32[]{:S(2)}, u32[]{:S(2)}) collective-permute-start(f32[160,256]{1,0:T(8,128)S(1)} %get-tuple-element.89), channel_id=1, source_target_pairs={{0,4},{1,5},{2,6},{3,7},{4,0},{5,1},{6,2},{7,3},{8,12},{9,13},{10,... | collective-permute-start | bytes 491528 | tf_op jit(solution)/shard_map/ppermute | solution.py:437
  76.5 7.1 %collective-permute-start.24 = (f32[80,256]{1,0:T(8,128)S(1)}, f32[80,256]{1,0:T(8,128)S(1)}, u32[]{:S(2)}, u32[]{:S(2)}) collective-permute-start(f32[80,256]{1,0:T(8,128)S(1)} %get-tuple-element.91), channel_id=1, source_target_pairs={{0,8},{1,9},{2,10},{3,11},{4,12},{5,13},{6,14},{7,15},{8,0},{9,1},... | collective-permute-start | bytes 245768 | tf_op jit(solution)/shard_map/ppermute | solution.py:437
  (5 other events, 16.6 us)
